TPU v7x, 32 devices: a whole 2x2x4 slice. The times are simulated.
32 devices in a mesh: section: 2 (over core), row: 4 (over z), col: 4 (over y, x).
Axes of the slice: x: 2, y: 2, z: 4, core: 2. Of those that a mesh axis runs over, the one named last changes fastest.
Arguments:
- inputs: bfloat16 [2, 2048, 1536], P(None, 'row'), may hold values from -6 to 6
- positions: int32 [2, 2048], P(None, 'row'), may hold values from 0 to 7165, as said below
- w_query: bfloat16 [2, 1536, 1536], P('section', 'row', 'col'), may hold values from -0.15625 to 0.15625
- key_weight: bfloat16 [2, 1536, 768], P('section', 'row', 'col'), may hold values from -0.15625 to 0.15625
- value_weight: bfloat16 [2, 1536, 768], P('section', 'row', 'col'), may hold values from -0.15625 to 0.15625
- w_out: bfloat16 [2, 1536, 1536], P('section', 'row', 'col'), may hold values from -2.5 to 2.5
- w_gate: bfloat16 [2, 1536, 4096], P('section', 'row', 'col'), may hold values from -0.15625 to 0.15625
- w_up: bfloat16 [2, 1536, 4096], P('section', 'row', 'col'), may hold values from -0.15625 to 0.15625
- w_down: bfloat16 [2, 1536, 4096], P('section', 'row', 'col'), may hold values from -0.1875 to 0.1875
- gain_attn: bfloat16 [2, 1536], P('section', 'row'), may hold values from 0.25 to 1.75
- gain_ffn: bfloat16 [2, 1536], P('section', 'row'), may hold values from 0.25 to 1.75
- cotangent: bfloat16 [2, 2048, 1536], P(None, 'row'), may hold values from -6 to 6
Outputs:
- activations: bfloat16 [2, 2, 2048, 1536], P('section', None, 'row')
- input_grads: bfloat16 [2, 2, 2048, 1536], P('section', None, 'row')
- grad_w_query: float32 [2, 1536, 1536], P('section', 'row', 'col')
- grad_w_key: float32 [2, 1536, 768], P('section', 'row', 'col')
- grad_w_value: float32 [2, 1536, 768], P('section', 'row', 'col')
- grad_w_out: float32 [2, 1536, 1536], P('section', 'row', 'col')
- grad_w_gate: float32 [2, 1536, 4096], P('section', 'row', 'col')
- grad_w_up: float32 [2, 1536, 4096], P('section', 'row', 'col')
- grad_w_down: float32 [2, 1536, 4096], P('section', 'row', 'col')
- grad_gain_attn: float32 [2, 1536], P('section', 'row')
- grad_gain_ffn: float32 [2, 1536], P('section', 'row')
Inputs may be any that keep to these rules, and one draw needn't show every extreme that they name: A sequence's rows form four blocks of 256; in the sequence's order they stand first, third, fourth, second, and along that order the positions rise by 1 to 3 from token to token. The first sequence of micro-batch 0 starts at 0; the last one of the last micro-batch ends at 7165.
All inputs are finite; a program needn't handle non-finite values.
Results may differ from a plain program's by a relative error of at most 0.03.
Values may be sent and summed in bfloat16 or wider, within the bound.
No kernel may reach another device: no remote copies, remote signals or barrier semaphores. Data moves between devices by JAX's collectives and lax.ppermute only.
A program may use at most 192 MiB of HBM per device.

v0:
```python
import math

import jax
import jax.numpy as jnp
from jax import lax
from jax.sharding import PartitionSpec as P

HEAD_SIZE = 96
SPAN = 2


EPSILON = 1e-05
ROPE_BASE = 100000.0
MASKED = -1e30


def partner(block, axis, bit):
    count = lax.axis_size(axis)
    route = []
    for low in range(count):
        high = low | 1 << bit
        if high != low and high < count:
            route += [(low, high), (high, low)]
    return lax.ppermute(block, axis, route)


def passed_along(x, axis, by):
    devices = lax.axis_size(axis)
    pairs = [(i, i + by) for i in range(devices) if 0 <= i + by < devices]
    return lax.ppermute(x, axis, pairs)


def rotation(position_ids):
    half_dim = HEAD_SIZE // 2
    inverse = ROPE_BASE ** (-(jnp.arange(half_dim, dtype=jnp.float32) * 2.0) / HEAD_SIZE)
    angles = position_ids.astype(jnp.float32)[:, None] * inverse[None, :]
    return (jnp.cos(angles), jnp.sin(angles))


def rotate(values, cosine_table, sine_table):
    half_dim = values.shape[-1] // 2
    first_half = values[..., :half_dim]
    second_half = values[..., half_dim:]
    cos_here = cosine_table[:, None, :]
    sin_here = sine_table[:, None, :]
    return jnp.concatenate(
        [
            first_half * cos_here - second_half * sin_here,
            second_half * cos_here + first_half * sin_here,
        ],
        axis=-1,
    )


def rotate_back(grads_in, cosine_table, sine_table):
    half_dim = grads_in.shape[-1] // 2
    first_half = grads_in[..., :half_dim]
    second_half = grads_in[..., half_dim:]
    cos_here = cosine_table[:, None, :]
    sin_here = sine_table[:, None, :]
    return jnp.concatenate(
        [
            first_half * cos_here + second_half * sin_here,
            second_half * cos_here - first_half * sin_here,
        ],
        axis=-1,
    )


def contract_last(left, right):
    return lax.dot_general(
        left, right, (((1,), (1,)), ((), ())), preferred_element_type=jnp.float32
    )


def contract_first(left, right):
    return lax.dot_general(
        left, right, (((0,), (0,)), ((), ())), preferred_element_type=jnp.float32
    )


def sequence_orders(rows_here):
    half = rows_here // 2
    parity = lax.axis_index("row") % SPAN
    offsets = jnp.arange(rows_here)

    def order_of(side):
        return offsets + jnp.where(side == 0, jnp.where(offsets < half, 0, 2 * half), half)

    own_order = order_of(parity)
    partner_order = order_of(1 - parity)
    return (own_order, jnp.concatenate([partner_order, own_order], axis=0))


def allowed_mask(orders):
    query_order, key_order = orders
    return key_order[None, :] <= query_order[:, None]


def attend(query_rows, keys_all, values, orders):
    rows_here = query_rows.shape[0]
    block_rows = min(rows_here, 512)
    block_count = rows_here // block_rows
    inv_root = 1.0 / math.sqrt(HEAD_SIZE)
    blocks = query_rows.reshape((block_count, block_rows) + query_rows.shape[1:])
    block_starts = jnp.arange(block_count) * block_rows

    def one_block(block_item):
        query_block, block_start = block_item
        scores = (
            jnp.einsum("qgrd,kgd->grqk", query_block, keys_all, preferred_element_type=jnp.float32)
            * inv_root
        )
        scores = jnp.where(allowed_mask(orders), scores, MASKED)
        row_peak = jnp.max(scores, axis=-1, keepdims=True)
        weights = jnp.exp(scores - row_peak)
        row_total = jnp.sum(weights, axis=-1, keepdims=True)
        probs_low = (weights / row_total).astype(jnp.bfloat16)
        merged_heads = jnp.einsum(
            "grqk,kgd->qgrd", probs_low, values, preferred_element_type=jnp.float32
        )
        return (merged_heads.astype(jnp.bfloat16), (row_peak + jnp.log(row_total))[..., 0])

    merged_heads, log_sums = lax.map(one_block, (blocks, block_starts))
    return (merged_heads.reshape(rows_here, -1), log_sums)


def attend_back(query_rows, keys_all, values, log_sums, grad_mixed, orders):
    rows_here = query_rows.shape[0]
    block_rows = min(rows_here, 512)
    block_count = rows_here // block_rows
    inv_root = 1.0 / math.sqrt(HEAD_SIZE)
    blocks = query_rows.reshape((block_count, block_rows) + query_rows.shape[1:])
    grad_blocks = grad_mixed.reshape((block_count, block_rows) + query_rows.shape[1:])
    block_starts = jnp.arange(block_count) * block_rows

    def one_block(carried, block_item):
        grad_keys, grad_values = carried
        query_block, grad_block, lse_block, block_start = block_item
        scores = (
            jnp.einsum("qgrd,kgd->grqk", query_block, keys_all, preferred_element_type=jnp.float32)
            * inv_root
        )
        scores = jnp.where(allowed_mask(orders), scores, MASKED)
        probs_full = jnp.exp(scores - lse_block[..., None])
        grad_probs = jnp.einsum(
            "qgrd,kgd->grqk", grad_block, values, preferred_element_type=jnp.float32
        )
        inner_sum = jnp.sum(probs_full * grad_probs, axis=-1, keepdims=True)
        grad_scores = (probs_full * (grad_probs - inner_sum)).astype(jnp.bfloat16)
        grad_query = (
            jnp.einsum("grqk,kgd->qgrd", grad_scores, keys_all, preferred_element_type=jnp.float32)
            * inv_root
        )
        grad_keys = (
            grad_keys
            + jnp.einsum(
                "grqk,qgrd->kgd", grad_scores, query_block, preferred_element_type=jnp.float32
            )
            * inv_root
        )
        grad_values = grad_values + jnp.einsum(
            "grqk,qgrd->kgd",
            probs_full.astype(jnp.bfloat16),
            grad_block,
            preferred_element_type=jnp.float32,
        )
        return ((grad_keys, grad_values), grad_query)

    zero_keys = jnp.zeros(keys_all.shape, jnp.float32)
    carried, grad_query = lax.scan(
        one_block, (zero_keys, zero_keys), (blocks, grad_blocks, log_sums, block_starts)
    )
    return (grad_query.reshape(query_rows.shape), carried[0], carried[1])


def layer_forward(inputs, cosine_table, sine_table, weights, orders):
    w_query, key_weight, value_weight, w_out, w_gate, w_up, w_down, gain_attn, gain_ffn = weights
    rows_here = inputs.shape[0]
    kv_heads = key_weight.shape[1] // HEAD_SIZE
    groups = w_query.shape[1] // key_weight.shape[1]
    scale_one = lax.rsqrt(jnp.mean(inputs * inputs, axis=-1, keepdims=True) + EPSILON)
    norm_rows = (inputs * scale_one * gain_attn.astype(jnp.float32)).astype(jnp.bfloat16)
    query_raw = jnp.dot(norm_rows, w_query, preferred_element_type=jnp.float32).reshape(
        rows_here, kv_heads * groups, HEAD_SIZE
    )
    key_unrotated = jnp.dot(norm_rows, key_weight, preferred_element_type=jnp.float32).reshape(
        rows_here, kv_heads, HEAD_SIZE
    )
    value_here = (
        jnp.dot(norm_rows, value_weight, preferred_element_type=jnp.float32)
        .astype(jnp.bfloat16)
        .reshape(rows_here, kv_heads, HEAD_SIZE)
    )
    query_rotated = (
        rotate(query_raw, cosine_table, sine_table)
        .astype(jnp.bfloat16)
        .reshape(rows_here, kv_heads, groups, HEAD_SIZE)
    )
    key_rotated = rotate(key_unrotated, cosine_table, sine_table).astype(jnp.bfloat16)
    partner_key, partner_value = partner((key_rotated, value_here), "row", 0)
    keys_all = jnp.concatenate([partner_key, key_rotated], axis=0)
    values = jnp.concatenate([partner_value, value_here], axis=0)
    merged_heads, log_sums = attend(query_rotated, keys_all, values, orders)
    attn_out = lax.psum(contract_last(merged_heads, w_out), "col")
    middle = inputs + attn_out
    scale_two = lax.rsqrt(jnp.mean(middle * middle, axis=-1, keepdims=True) + EPSILON)
    normed_two = (middle * scale_two * gain_ffn.astype(jnp.float32)).astype(jnp.bfloat16)
    gate_proj = jnp.dot(normed_two, w_gate, preferred_element_type=jnp.float32)
    up_proj = jnp.dot(normed_two, w_up, preferred_element_type=jnp.float32)
    hidden = (jax.nn.silu(gate_proj) * up_proj).astype(jnp.bfloat16)
    ffn_out = lax.psum(contract_last(hidden, w_down).astype(jnp.bfloat16), "col").astype(
        jnp.float32
    )
    output = (middle + ffn_out).astype(jnp.bfloat16)
    kept_state = (
        inputs,
        scale_one,
        norm_rows,
        query_rotated,
        keys_all,
        values,
        merged_heads,
        log_sums,
        middle,
        scale_two,
        normed_two,
        gate_proj,
        up_proj,
        hidden,
    )
    return (output, kept_state)


def layer_backward(kept_state, grad_out, cosine_table, sine_table, weights, orders):
    w_query, key_weight, value_weight, w_out, w_gate, w_up, w_down, gain_attn, gain_ffn = weights
    (
        inputs,
        scale_one,
        norm_rows,
        query_rotated,
        keys_all,
        values,
        merged_heads,
        log_sums,
        middle,
        scale_two,
        normed_two,
        gate_proj,
        up_proj,
        hidden,
    ) = kept_state
    rows_here = inputs.shape[0]
    grad_ffn = grad_out.astype(jnp.bfloat16)
    grad_hidden = jnp.dot(grad_ffn, w_down, preferred_element_type=jnp.float32)
    grad_w_down = contract_first(grad_ffn, hidden)
    sigmoid_gate = jax.nn.sigmoid(gate_proj)
    grad_gate = (
        grad_hidden * up_proj * sigmoid_gate * (1.0 + gate_proj * (1.0 - sigmoid_gate))
    ).astype(jnp.bfloat16)
    grad_up = (grad_hidden * gate_proj * sigmoid_gate).astype(jnp.bfloat16)
    grad_w_gate = contract_first(normed_two, grad_gate)
    grad_w_up = contract_first(normed_two, grad_up)
    grad_norm_two = lax.psum(
        (contract_last(grad_gate, w_gate) + contract_last(grad_up, w_up)).astype(jnp.bfloat16),
        "col",
    ).astype(jnp.float32)
    unit_two = middle * scale_two
    scaled_two = grad_norm_two * gain_ffn.astype(jnp.float32)
    grad_gain_ffn = jnp.sum(grad_norm_two * unit_two, axis=0)
    grad_middle = grad_out + scale_two * (
        scaled_two - unit_two * jnp.mean(scaled_two * unit_two, axis=-1, keepdims=True)
    )
    grad_attn = grad_middle.astype(jnp.bfloat16)
    grad_mixed = jnp.dot(grad_attn, w_out, preferred_element_type=jnp.float32).astype(jnp.bfloat16)
    grad_w_out = contract_first(grad_attn, merged_heads)
    grad_query, grad_keys, grad_values = attend_back(
        query_rotated, keys_all, values, log_sums, grad_mixed.reshape(query_rotated.shape), orders
    )
    returned_key, returned_value = (
        partner(grad_keys[:rows_here].astype(jnp.bfloat16), "row", 0).astype(jnp.float32),
        partner(grad_values[:rows_here].astype(jnp.bfloat16), "row", 0).astype(jnp.float32),
    )
    grad_key = grad_keys[rows_here:] + returned_key
    grad_value = (
        (grad_values[rows_here:] + returned_value).astype(jnp.bfloat16).reshape(rows_here, -1)
    )
    grad_query = (
        rotate_back(grad_query.reshape(rows_here, -1, HEAD_SIZE), cosine_table, sine_table)
        .astype(jnp.bfloat16)
        .reshape(rows_here, -1)
    )
    grad_key = (
        rotate_back(grad_key, cosine_table, sine_table).astype(jnp.bfloat16).reshape(rows_here, -1)
    )
    grad_w_query = contract_first(norm_rows, grad_query)
    grad_w_key = contract_first(norm_rows, grad_key)
    grad_w_value = contract_first(norm_rows, grad_value)
    grad_norm_one = lax.psum(
        (
            contract_last(grad_query, w_query)
            + contract_last(grad_key, key_weight)
            + contract_last(grad_value, value_weight)
        ).astype(jnp.bfloat16),
        "col",
    ).astype(jnp.float32)
    unit_one = inputs * scale_one
    scaled_one = grad_norm_one * gain_attn.astype(jnp.float32)
    grad_gain_attn = jnp.sum(grad_norm_one * unit_one, axis=0)
    grad_inputs = grad_middle + scale_one * (
        scaled_one - unit_one * jnp.mean(scaled_one * unit_one, axis=-1, keepdims=True)
    )
    return (
        grad_inputs,
        (
            grad_w_query,
            grad_w_key,
            grad_w_value,
            grad_w_out,
            grad_w_gate,
            grad_w_up,
            grad_w_down,
            grad_gain_attn,
            grad_gain_ffn,
        ),
    )


def gather_each(local_parts):
    p_query, p_key, p_value, p_out, p_gate, p_up, p_down, p_gain_attn, p_gain_ffn = local_parts
    return (
        lax.all_gather(p_query, "row", axis=0, tiled=True),
        lax.all_gather(p_key, "row", axis=0, tiled=True),
        lax.all_gather(p_value, "row", axis=0, tiled=True),
        lax.all_gather(p_out, "row", axis=0, tiled=True),
        lax.all_gather(p_gate, "row", axis=0, tiled=True),
        lax.all_gather(p_up, "row", axis=0, tiled=True),
        lax.all_gather(p_down, "row", axis=0, tiled=True),
        lax.all_gather(p_gain_attn, "row", axis=0, tiled=True),
        lax.all_gather(p_gain_ffn, "row", axis=0, tiled=True),
    )


def scatter_end(grad_list):
    g_query, g_key, g_value, g_out, g_gate, g_up, g_down, g_gain_attn, g_gain_ffn = grad_list
    return (
        lax.psum_scatter(
            g_query.astype(jnp.bfloat16), "row", scatter_dimension=0, tiled=True
        ).astype(jnp.float32),
        lax.psum_scatter(g_key.astype(jnp.bfloat16), "row", scatter_dimension=0, tiled=True).astype(
            jnp.float32
        ),
        lax.psum_scatter(
            g_value.astype(jnp.bfloat16), "row", scatter_dimension=0, tiled=True
        ).astype(jnp.float32),
        lax.psum_scatter(g_out.astype(jnp.bfloat16), "row", scatter_dimension=0, tiled=True).astype(
            jnp.float32
        ),
        lax.psum_scatter(
            g_gate.astype(jnp.bfloat16), "row", scatter_dimension=0, tiled=True
        ).astype(jnp.float32),
        lax.psum_scatter(g_up.astype(jnp.bfloat16), "row", scatter_dimension=0, tiled=True).astype(
            jnp.float32
        ),
        lax.psum_scatter(
            g_down.astype(jnp.bfloat16), "row", scatter_dimension=0, tiled=True
        ).astype(jnp.float32),
        lax.psum_scatter(
            g_gain_attn.astype(jnp.bfloat16), "row", scatter_dimension=0, tiled=True
        ).astype(jnp.float32),
        lax.psum_scatter(
            g_gain_ffn.astype(jnp.bfloat16), "row", scatter_dimension=0, tiled=True
        ).astype(jnp.float32),
    )


def body(
    inputs,
    positions,
    w_query,
    key_weight,
    value_weight,
    w_out,
    w_gate,
    w_up,
    w_down,
    gain_attn,
    gain_ffn,
    cotangent,
):
    sections = lax.axis_size("section")
    section_id = lax.axis_index("section")
    orders = sequence_orders(inputs.shape[1])
    micro_count = inputs.shape[0]
    tick_count = micro_count + sections - 1
    local_parts = (
        w_query[0],
        key_weight[0],
        value_weight[0],
        w_out[0],
        w_gate[0],
        w_up[0],
        w_down[0],
        gain_attn[0],
        gain_ffn[0],
    )
    collected = []
    outputs_list = []
    received = jnp.zeros(inputs.shape[1:], jnp.bfloat16)
    for tick_index in range(tick_count):
        weights = gather_each(local_parts)
        micro_index = jnp.clip(tick_index - section_id, 0, micro_count - 1)
        place_ids = lax.dynamic_index_in_dim(positions, micro_index, 0, keepdims=False)
        cosine_table, sine_table = rotation(place_ids)
        section_input = jnp.where(
            section_id == 0, inputs[min(tick_index, micro_count - 1)], received
        ).astype(jnp.float32)
        output, kept_state = layer_forward(section_input, cosine_table, sine_table, weights, orders)
        if tick_index + 1 < tick_count:
            received = passed_along(output, "section", 1)
        collected.append((kept_state, cosine_table, sine_table))
        outputs_list.append(output)
    totals = None
    returned = jnp.zeros(inputs.shape[1:], jnp.bfloat16)
    grads_by_slot = [None] * tick_count
    for step_index in range(tick_count):
        slot_index = tick_count - 1 - step_index
        kept_state, cosine_table, sine_table = collected[slot_index]
        weights = gather_each(local_parts)
        last_grad = cotangent[min(max(slot_index - sections + 1, 0), micro_count - 1)]
        grad_out = jnp.where(section_id == sections - 1, last_grad, returned).astype(jnp.float32)
        grad_in, grad_list = layer_backward(
            kept_state, grad_out, cosine_table, sine_table, weights, orders
        )
        valid_tick = (slot_index - section_id >= 0) & (slot_index - section_id < micro_count)
        grad_list = tuple((jnp.where(valid_tick, tensor, 0.0) for tensor in grad_list))
        totals = (
            grad_list
            if totals is None
            else tuple((earlier + later for earlier, later in zip(totals, grad_list)))
        )
        grad_in = grad_in.astype(jnp.bfloat16)
        if step_index + 1 < tick_count:
            returned = passed_along(grad_in, "section", -1)
        grads_by_slot[slot_index] = grad_in
    totals = scatter_end(totals)
    activations = lax.dynamic_slice_in_dim(jnp.stack(outputs_list), section_id, micro_count, 0)[
        None
    ]
    input_grads = lax.dynamic_slice_in_dim(jnp.stack(grads_by_slot), section_id, micro_count, 0)[
        None
    ]
    g_query, g_key, g_value, g_out, g_gate, g_up, g_down, g_gain_attn, g_gain_ffn = totals
    return (
        activations,
        input_grads,
        g_query[None],
        g_key[None],
        g_value[None],
        g_out[None],
        g_gate[None],
        g_up[None],
        g_down[None],
        g_gain_attn[None],
        g_gain_ffn[None],
    )


def solution(mesh):
    placed = (
        P(None, "row", None),
        P(None, "row"),
        P("section", "row", "col"),
        P("section", "row", "col"),
        P("section", "row", "col"),
        P("section", "row", "col"),
        P("section", "row", "col"),
        P("section", "row", "col"),
        P("section", "row", "col"),
        P("section", "row"),
        P("section", "row"),
        P(None, "row", None),
    )
    return jax.shard_map(
        body,
        mesh=mesh,
        in_specs=placed,
        out_specs=(
            P("section", None, "row", None),
            P("section", None, "row", None),
            P("section", "row", "col"),
            P("section", "row", "col"),
            P("section", "row", "col"),
            P("section", "row", "col"),
            P("section", "row", "col"),
            P("section", "row", "col"),
            P("section", "row", "col"),
            P("section", "row"),
            P("section", "row"),
        ),
        check_vma=False,
    )
```

profile of v0, /device:TPU:0, one launch (start us, length us, event | category | flops | bytes accessed | tf_op | source)
XLA Modules:
  0.0 1604.6 jit_solution(12749915113943451399)
XLA Ops:
  8.0 13.8 all-gather
  21.8 24.5 %all-gather.2 = bf16[1,1536,192]{1,2,0:T(8,128)(2,1)S(1)} all-gather(bf16[1,384,192]{1,2,0:T(8,128)(2,1)} %param.15), channel_id=4, replica_groups=mesh['section'=2,'row'=4,'col'=4] {'row'}, dimensions={1}, use_global_device_ids=true | all-gather | bytes 737280 | tf_op jit(solution)/shard_map/all_gather | solution.py:333
  53.0 19.7 %all-gather.1 = bf16[1,1536,192]{1,2,0:T(8,128)(2,1)S(1)} all-gather(bf16[1,384,192]{1,2,0:T(8,128)(2,1)S(1)} %copy-done.146), channel_id=3, replica_groups=mesh['section'=2,'row'=4,'col'=4] {'row'}, dimensions={1}, use_global_device_ids=true | all-gather | bytes 737280 | tf_op jit(solution)/shard_map/all_gather | solution.py:334
  89.8 15.9 all-gather.17.cloned.1.call-done
  111.5 12.1 all-gather.5
  123.6 72.6 %all-reduce.16.cloned.1.call-done = f32[512,1536]{1,0:T(8,128)} async-done(((f32[512,1536]{1,0:T(8,128)}), f32[512,1536]{1,0:T(8,128)}) %all-reduce.16.cloned.1.call-update) | async-done | bytes 3145744 | tf_op jit(solution)/shard_map/psum | solution.py:205
  200.8 60.4 %all-gather.19.cloned.1.call-done = bf16[1,1536,1024]{2,1,0:T(8,128)(2,1)} async-done(((bf16[1,384,1024]{2,1,0:T(8,128)(2,1)}), bf16[1,1536,1024]{2,1,0:T(8,128)(2,1)}) %all-gather.19.cloned.1.call-update) | async-done | bytes 3145744 | tf_op jit(solution)/shard_map/all_gather | solution.py:336
  261.2 5.5 fusion.123
  266.7 58.2 %all-gather.21.cloned.1.call-done = bf16[1,1536,1024]{2,1,0:T(8,128)(2,1)} async-done(((bf16[1,384,1024]{2,1,0:T(8,128)(2,1)}), bf16[1,1536,1024]{2,1,0:T(8,128)(2,1)}) %all-gather.21.cloned.1.call-update) | async-done | bytes 3145744 | tf_op jit(solution)/shard_map/all_gather | solution.py:337
  324.9 6.6 multiply_convert_fusion.11
  331.6 57.1 %all-gather.23.cloned.1.call-done = bf16[1,1536,1024]{2,1,0:T(8,128)(2,1)} async-done(((bf16[1,384,1024]{2,1,0:T(8,128)(2,1)}), bf16[1,1536,1024]{2,1,0:T(8,128)(2,1)}) %all-gather.23.cloned.1.call-update) | async-done | bytes 3145744 | tf_op jit(solution)/shard_map/all_gather | solution.py:338
  388.6 5.2 fusion.129
  393.9 59.7 %all-reduce.18.cloned.1.call-done = bf16[512,1536]{1,0:T(8,128)(2,1)} async-done(((bf16[512,1536]{1,0:T(8,128)(2,1)}), bf16[512,1536]{1,0:T(8,128)(2,1)}) %all-reduce.18.cloned.1.call-update) | async-done | bytes 1572880 | tf_op jit(solution)/shard_map/psum | solution.py:212
  466.9 8.0 collective-permute-done.4
  485.6 86.8 %all-reduce.20.cloned.1.call-done = f32[512,1536]{1,0:T(8,128)} async-done(((f32[512,1536]{1,0:T(8,128)}), f32[512,1536]{1,0:T(8,128)}) %all-reduce.20.cloned.1.call-update) | async-done | bytes 3145744 | tf_op jit(solution)/shard_map/psum | solution.py:205
  588.1 61.0 %all-reduce.22.cloned.1.call-done = bf16[512,1536]{1,0:T(8,128)(2,1)} async-done(((bf16[512,1536]{1,0:T(8,128)(2,1)}), bf16[512,1536]{1,0:T(8,128)(2,1)}) %all-reduce.22.cloned.1.call-update) | async-done | bytes 1572880 | tf_op jit(solution)/shard_map/psum | solution.py:212
  662.4 8.1 collective-permute-done.7
  680.9 87.1 %all-reduce.24.cloned.1.call-done = f32[512,1536]{1,0:T(8,128)} async-done(((f32[512,1536]{1,0:T(8,128)}), f32[512,1536]{1,0:T(8,128)}) %all-reduce.24.cloned.1.call-update) | async-done | bytes 3145744 | tf_op jit(solution)/shard_map/psum | solution.py:205
  789.4 59.2 %all-reduce.26.cloned.1.call-done = bf16[512,1536]{1,0:T(8,128)(2,1)} async-done(((bf16[512,1536]{1,0:T(8,128)(2,1)}), bf16[512,1536]{1,0:T(8,128)(2,1)}) %all-reduce.26.cloned.1.call-update) | async-done | bytes 1572880 | tf_op jit(solution)/shard_map/psum | solution.py:264
  874.1 60.1 %all-reduce.28.cloned.1.call-done = bf16[512,1536]{1,0:T(8,128)(2,1)} async-done(((bf16[512,1536]{1,0:T(8,128)(2,1)}), bf16[512,1536]{1,0:T(8,128)(2,1)}) %all-reduce.28.cloned.1.call-update) | async-done | bytes 1572880 | tf_op jit(solution)/shard_map/psum | solution.py:299
  955.3 59.7 %all-reduce.30.cloned.1.call-done = bf16[512,1536]{1,0:T(8,128)(2,1)} async-done(((bf16[512,1536]{1,0:T(8,128)(2,1)}), bf16[512,1536]{1,0:T(8,128)(2,1)}) %all-reduce.30.cloned.1.call-update) | async-done | bytes 1572880 | tf_op jit(solution)/shard_map/psum | solution.py:264
  1040.7 60.1 %all-reduce.32.cloned.1.call-done = bf16[512,1536]{1,0:T(8,128)(2,1)} async-done(((bf16[512,1536]{1,0:T(8,128)(2,1)}), bf16[512,1536]{1,0:T(8,128)(2,1)}) %all-reduce.32.cloned.1.call-update) | async-done | bytes 1572880 | tf_op jit(solution)/shard_map/psum | solution.py:299
  1128.0 54.0 %all-reduce.34.cloned.1.call-done = bf16[512,1536]{1,0:T(8,128)(2,1)} async-done(((bf16[512,1536]{1,0:T(8,128)(2,1)}), bf16[512,1536]{1,0:T(8,128)(2,1)}) %all-reduce.34.cloned.1.call-update) | async-done | bytes 1572880 | tf_op jit(solution)/shard_map/psum | solution.py:264
  1188.2 5.5 fusion.186
  1276.6 10.0 reduce-scatter.14.cloned.1.call-done
  1288.4 29.0 %reduce-scatter.12.cloned.1.call-done = bf16[384,384]{1,0:T(8,128)(2,1)} async-done(((bf16[1536,384]{1,0:T(8,128)(2,1)}), bf16[384,384]{1,0:T(8,128)(2,1)}) %reduce-scatter.12.cloned.1.call-update) | async-done | bytes 294928 | tf_op jit(solution)/shard_map/reduce_scatter | solution.py:347
  1319.2 87.8 %all-reduce.36.cloned.1.call-done = (bf16[512,1536]{1,0:T(8,128)(2,1)}, bf16[512,1536]{1,0:T(8,128)(2,1)}) async-done(((bf16[512,1536]{1,0:T(8,128)(2,1)}, bf16[512,1536]{1,0:T(8,128)(2,1)}), (bf16[512,1536]{1,0:T(8,128)(2,1)}, bf16[512,1536]{1,0:T(8,128)(2,1)})) %all-reduce.36.cloned.1.call-update) | async-done | bytes 3145744 | tf_op jit(solution)/shard_map/psum | solution.py:212
  1410.0 12.1 all-reduce.3
  1430.1 5.1 fusion.80
  1435.2 34.7 %reduce-scatter.20.cloned.1.call-done = bf16[384,1024]{1,0:T(8,128)(2,1)} async-done(((bf16[1536,1024]{1,0:T(8,128)(2,1)}), bf16[384,1024]{1,0:T(8,128)(2,1)}) %reduce-scatter.20.cloned.1.call-update) | async-done | bytes 786448 | tf_op jit(solution)/shard_map/reduce_scatter | solution.py:365
  1472.3 60.1 %reduce-scatter.18.cloned.1.call-done = bf16[384,1024]{1,0:T(8,128)(2,1)} async-done(((bf16[1536,1024]{1,0:T(8,128)(2,1)}), bf16[384,1024]{1,0:T(8,128)(2,1)}) %reduce-scatter.18.cloned.1.call-update) | async-done | bytes 786448 | tf_op jit(solution)/shard_map/reduce_scatter | solution.py:362
  1534.9 60.3 %reduce-scatter.16.cloned.1.call-done = bf16[384,1024]{1,0:T(8,128)(2,1)} async-done(((bf16[1536,1024]{1,0:T(8,128)(2,1)}), bf16[384,1024]{1,0:T(8,128)(2,1)}) %reduce-scatter.16.cloned.1.call-update) | async-done | bytes 786448 | tf_op jit(solution)/shard_map/reduce_scatter | solution.py:359
  (696 shorter events, 326.7 us)
Async XLA Ops:
  7.2 69.0 %all-gather.15.cloned.1.call-start = ((), (), s32[]{:S(2)}) async-start(), calls=%async_computation.22 | async-start | bytes 1474560 | tf_op jit(solution)/shard_map/all_gather | solution.py:332
  7.9 97.8 %all-gather.17.cloned.1.call-start = ((), (), s32[]{:S(2)}) async-start(), calls=%async_computation.23 | async-start | bytes 1474560 | tf_op jit(solution)/shard_map/all_gather | solution.py:335
  52.8 28.2 %collective-permute-start.1 = (bf16[512,2,96]{0,2,1:T(8,128)(2,1)}, bf16[512,2,96]{0,2,1:T(8,128)(2,1)}, u32[]{:S(2)}, u32[]{:S(2)}) collective-permute-start(bf16[512,2,96]{0,2,1:T(8,128)(2,1)} %pad_maximum_fusion.11), channel_id=1, source_target_pairs={{0,4},{4,0},{8,12},{12,8},{1,5},{5,1},{9,13},{13,9},{2,6},{6,2},{1... | collective-permute-start | bytes 589832 | tf_op jit(solution)/shard_map/ppermute | solution.py:24
  74.9 10.1 collective-permute-start
  74.9 121.3 %all-reduce.16.cloned.1.call-start = ((), (), s32[]{:S(2)}) async-start(), calls=%async_computation.7 | async-start | bytes 6291456 | tf_op jit(solution)/shard_map/psum | solution.py:205
  109.7 151.5 %all-gather.19.cloned.1.call-start = ((), (), s32[]{:S(2)}) async-start(), calls=%async_computation.24 | async-start | bytes 3932160 | tf_op jit(solution)/shard_map/all_gather | solution.py:336
  110.3 214.6 %all-gather.21.cloned.1.call-start = ((), (), s32[]{:S(2)}) async-start(), calls=%async_computation.25 | async-start | bytes 3932160 | tf_op jit(solution)/shard_map/all_gather | solution.py:337
  110.9 277.7 %all-gather.23.cloned.1.call-start = ((), (), s32[]{:S(2)}) async-start(), calls=%async_computation.26 | async-start | bytes 3932160 | tf_op jit(solution)/shard_map/all_gather | solution.py:338
  111.5 342.1 %all-reduce.18.cloned.1.call-start = ((), (), s32[]{:S(2)}) async-start(), calls=%async_computation.8 | async-start | bytes 3145728 | tf_op jit(solution)/shard_map/psum | solution.py:212
  393.8 178.6 %all-reduce.20.cloned.1.call-start = ((), (), s32[]{:S(2)}) async-start(), calls=%async_computation.9 | async-start | bytes 6291456 | tf_op jit(solution)/shard_map/psum | solution.py:205
  463.4 14.5 collective-permute-start.3
  465.1 9.8 collective-permute-start.4
  485.1 164.0 %all-reduce.22.cloned.1.call-start = ((), (), s32[]{:S(2)}) async-start(), calls=%async_computation.10 | async-start | bytes 3145728 | tf_op jit(solution)/shard_map/psum | solution.py:212
  588.0 180.0 %all-reduce.24.cloned.1.call-start = ((), (), s32[]{:S(2)}) async-start(), calls=%async_computation.11 | async-start | bytes 6291456 | tf_op jit(solution)/shard_map/psum | solution.py:205
  659.0 14.5 collective-permute-start.6
  660.6 9.8 collective-permute-start.7
  680.7 167.9 %all-reduce.26.cloned.1.call-start = ((), (), s32[]{:S(2)}) async-start(), calls=%async_computation.12 | async-start | bytes 3145728 | tf_op jit(solution)/shard_map/psum | solution.py:264
  787.5 146.7 %all-reduce.28.cloned.1.call-start = ((), (), s32[]{:S(2)}) async-start(), calls=%async_computation.13 | async-start | bytes 3145728 | tf_op jit(solution)/shard_map/psum | solution.py:299
  857.2 14.6 collective-permute-start.9
  874.1 140.9 %all-reduce.30.cloned.1.call-start = ((), (), s32[]{:S(2)}) async-start(), calls=%async_computation.14 | async-start | bytes 3145728 | tf_op jit(solution)/shard_map/psum | solution.py:264
  953.9 146.8 %all-reduce.32.cloned.1.call-start = ((), (), s32[]{:S(2)}) async-start(), calls=%async_computation.15 | async-start | bytes 3145728 | tf_op jit(solution)/shard_map/psum | solution.py:299
  1023.5 14.7 collective-permute-start.12
  1040.6 141.4 %all-reduce.34.cloned.1.call-start = ((), (), s32[]{:S(2)}) async-start(), calls=%async_computation.16 | async-start | bytes 3145728 | tf_op jit(solution)/shard_map/psum | solution.py:264
  1121.0 151.8 %reduce-scatter.24.cloned.1.call-start = ((), (), s32[]{:S(2)}) async-start(), calls=%async_computation.28 | async-start | bytes 983040
  1193.8 9.5 collective-permute-start.15
  1207.3 66.5 %reduce-scatter.22.cloned.1.call-start = ((), (), s32[]{:S(2)}) async-start(), calls=%async_computation.27 | async-start | bytes 983040
  1215.4 71.2 %reduce-scatter.14.cloned.1.call-start = ((), (), s32[]{:S(2)}) async-start(), calls=%async_computation.18 | async-start | bytes 1474560 | tf_op jit(solution)/shard_map/reduce_scatter | solution.py:356
  1222.8 94.5 %reduce-scatter.12.cloned.1.call-start = ((), (), s32[]{:S(2)}) async-start(), calls=%async_computation.17 | async-start | bytes 1474560 | tf_op jit(solution)/shard_map/reduce_scatter | solution.py:347
  1230.9 176.1 %all-reduce.36.cloned.1.call-start = ((), (), s32[]{:S(2)}) async-start(), calls=%async_computation.29 | async-start | bytes 6291456 | tf_op jit(solution)/shard_map/psum | solution.py:212
  1240.0 229.9 %reduce-scatter.20.cloned.1.call-start = ((), (), s32[]{:S(2)}) async-start(), calls=%async_computation.21 | async-start | bytes 3932160 | tf_op jit(solution)/shard_map/reduce_scatter | solution.py:365
  1250.0 282.4 %reduce-scatter.18.cloned.1.call-start = ((), (), s32[]{:S(2)}) async-start(), calls=%async_computation.20 | async-start | bytes 3932160 | tf_op jit(solution)/shard_map/reduce_scatter | solution.py:362
  1260.8 334.4 %reduce-scatter.16.cloned.1.call-start = ((), (), s32[]{:S(2)}) async-start(), calls=%async_computation.19 | async-start | bytes 3932160 | tf_op jit(solution)/shard_map/reduce_scatter | solution.py:359
  (222 other events, 2930.3 us)
Sparse Core Ops, SparseCore 0:
  9.6 42.0 all-gather.14
  75.1 30.6 all-gather.16
  109.8 86.3 all-reduce.15
  197.7 63.4 all-gather.18
  262.7 62.1 all-gather.20
  326.4 62.1 all-gather.22
  393.9 59.5 all-reduce.17
  485.2 87.1 all-reduce.19
  588.1 60.8 all-reduce.21
  680.8 87.1 all-reduce.23
  787.7 60.8 all-reduce.25
  874.2 59.9 all-reduce.27
  954.1 60.8 all-reduce.29
  1040.7 59.9 all-reduce.31
  1121.1 60.8 all-reduce.33
  1207.4 23.1 reduce-scatter.23
  1232.7 22.6 reduce-scatter.21
  1258.1 28.3 reduce-scatter.13
  1289.4 27.8 reduce-scatter.11
  1320.9 86.0 all-reduce.35
  1409.4 60.4 reduce-scatter.19
  1472.3 60.1 reduce-scatter.17
  1534.9 60.2 reduce-scatter.15
where the time goes:
time: 1610 us; the launch traced here: 1600 us
  waiting for transfers between devices  1170 us (73%)
  matrix products  174 us (11%)
  other arithmetic  93.3 us (6%)
  blocking collectives  82.2 us (5%)
  local copies, waits for them, and re-layouts  40.5 us (3%)
  starting transfers between devices  21.7 us (1%)
  between operations  18.2 us (1%)
    psum x3, waiting for transfers between devices, layer_forward(): attn_out = lax.psum(contract_last(merged_heads, w_out), 'col')  246 us
    psum x3, waiting for transfers between devices, layer_forward(): lax.psum(contract_last(hidden, w_down).astype(jnp.bfloat16), 'col')  208 us
    psum x3, waiting for transfers between devices, layer_backward(): lax.psum((contract_last(grad_gate, w_gate) + contract_last(grad_up, w_up)...  173 us
    psum x2, waiting for transfers between devices, layer_backward(): lax.psum((contract_last(grad_query, w_query) + contract_last(grad_key, ke...  120 us
    all_gather x1, waiting for transfers between devices, gather_each(): lax.all_gather(p_gate, 'row', axis=0, tiled=True)  60.4 us
    reduce_scatter x1, waiting for transfers between devices, scatter_end(): lax.psum_scatter(g_gate.astype(jnp.bfloat16), 'row', scatter_dimension=0,...  60.3 us
    reduce_scatter x1, waiting for transfers between devices, scatter_end(): lax.psum_scatter(g_up.astype(jnp.bfloat16), 'row', scatter_dimension=0, t...  60.1 us
    all_gather x1, waiting for transfers between devices, gather_each(): lax.all_gather(p_up, 'row', axis=0, tiled=True)  58.2 us
  transfers between devices with their start and end apart: 39, of which 29 were waited for; matrix products, arithmetic and copies ran while one was open for 10% of the time, Pallas kernels for 0%

commit v1 on v0

v1 whole, which is shorter than its diff:
```python
import math

import jax
import jax.numpy as jnp
from jax import lax
from jax.sharding import PartitionSpec as P

HEAD_SIZE = 96
HALF = HEAD_SIZE // 2
EPSILON = 1e-05
ROPE_BASE = 100000.0
MASKED = -1e30
BF = jnp.bfloat16
F32 = jnp.float32


def mate(x, axis, k):
    n = lax.axis_size(axis)
    return lax.ppermute(x, axis, [(j, j ^ k) for j in range(n)])


def ring(x, by):
    n = lax.axis_size("row")
    return lax.ppermute(x, "row", [(j, (j + by) % n) for j in range(n)])


def rotation(position_ids):
    inverse = ROPE_BASE ** (-(jnp.arange(HALF, dtype=F32) * 2.0) / HEAD_SIZE)
    angles = position_ids.astype(F32)[:, None] * inverse[None, :]
    return (jnp.cos(angles), jnp.sin(angles))


def rotate(values, tables, sign):
    cos_here, sin_here = tables[0][:, None, :], tables[1][:, None, :] * sign
    first, second = values[..., :HALF], values[..., HALF:]
    return jnp.concatenate(
        [first * cos_here - second * sin_here, second * cos_here + first * sin_here], axis=-1
    )


def dot(left, right):
    return jnp.dot(left, right, preferred_element_type=F32)


def dot_t(left, right):
    return lax.dot_general(left, right, (((1,), (1,)), ((), ())), preferred_element_type=F32)


def t_dot(left, right):
    return lax.dot_general(left, right, (((0,), (0,)), ((), ())), preferred_element_type=F32)


def roll_features(x, blocks):
    width = x.shape[-1]
    n = lax.axis_size("row")
    return lax.dynamic_slice_in_dim(
        jnp.concatenate([x, x], -1), (blocks % n) * (width // n), width, x.ndim - 1
    )


def sum_scatter(partial):
    n = lax.axis_size("col")
    c = lax.axis_index("col")
    rows = partial.shape[0] // n

    def piece(k):
        return lax.dynamic_slice_in_dim(partial, (c ^ k) * rows, rows, 0)

    total = piece(0).astype(F32)
    for k in range(1, n):
        total = total + mate(piece(k), "col", k).astype(F32)
    return total


def gather_rows(local):
    n = lax.axis_size("col")
    c = lax.axis_index("col")
    slots = [local] + [mate(local, "col", k) for k in range(1, n)]
    out = jnp.zeros((n * local.shape[0], local.shape[1]), local.dtype)
    for k in range(n):
        out = lax.dynamic_update_slice_in_dim(out, slots[k], (c ^ k) * local.shape[0], 0)
    return out


def own_rows(x):
    rows = x.shape[0] // lax.axis_size("col")
    return lax.dynamic_slice_in_dim(x, lax.axis_index("col") * rows, rows, 0)


def allowed(rows):
    half = rows // 2
    parity = lax.axis_index("row") % 2
    offsets = jnp.arange(rows)

    def order_of(side):
        return offsets + jnp.where(side == 0, jnp.where(offsets < half, 0, 2 * half), half)

    own, other = order_of(parity), order_of(1 - parity)
    return jnp.concatenate([other, own])[None, :] <= own[:, None]


def attend(query, keys, values, mask):
    scores = jnp.einsum("qgrd,kgd->grqk", query, keys, preferred_element_type=F32)
    scores = jnp.where(mask, scores * (1.0 / math.sqrt(HEAD_SIZE)), MASKED)
    peak = jnp.max(scores, axis=-1, keepdims=True)
    weights = jnp.exp(scores - peak)
    total = jnp.sum(weights, axis=-1, keepdims=True)
    probs = (weights / total).astype(BF)
    mixed = jnp.einsum("grqk,kgd->qgrd", probs, values, preferred_element_type=F32)
    return mixed.astype(BF), peak + jnp.log(total)


def attend_back(query, keys, values, log_sums, grad_mixed, mask):
    scale = 1.0 / math.sqrt(HEAD_SIZE)
    scores = jnp.einsum("qgrd,kgd->grqk", query, keys, preferred_element_type=F32)
    scores = jnp.where(mask, scores * scale, MASKED)
    probs = jnp.exp(scores - log_sums)
    grad_probs = jnp.einsum("qgrd,kgd->grqk", grad_mixed, values, preferred_element_type=F32)
    inner = jnp.sum(probs * grad_probs, axis=-1, keepdims=True)
    grad_scores = (probs * (grad_probs - inner)).astype(BF)
    grad_query = jnp.einsum("grqk,kgd->qgrd", grad_scores, keys, preferred_element_type=F32)
    grad_keys = jnp.einsum("grqk,qgrd->kgd", grad_scores, query, preferred_element_type=F32)
    grad_values = jnp.einsum(
        "grqk,qgrd->kgd", probs.astype(BF), grad_mixed, preferred_element_type=F32
    )
    return grad_query * scale, grad_keys * scale, grad_values


def halves(w):
    width = w.shape[1] // 2
    return [w[:, :width], w[:, width:]]


def gather_weights(own_attn, own_ffn):
    s = lax.axis_index("section")
    n = lax.axis_size("row")
    layers = []
    for parts in (own_attn, own_ffn):
        keep = jnp.where(s == 0, parts[0], parts[1])
        got = mate(jnp.where(s == 0, parts[1], parts[0]), "section", 1)
        layers.append([jnp.where(s == layer, keep, got) for layer in range(2)])
    out = []
    for layer in range(2):
        groups = []
        for group in range(2):
            slots = [layers[group][layer]]
            for _ in range(1, n):
                slots.append(ring(slots[-1], -1))
            others = [mate(x, "section", 1) for x in slots]
            groups.append((jnp.concatenate(slots, 0), jnp.concatenate(others, 0)))
        out.append(groups)
    return out


def layer_weights(groups, kv, qw, ff):
    (am, ao), (fm, fo) = groups

    def both(m, o, start, width):
        return jnp.concatenate([m[:, start : start + width], o[:, start : start + width]], 1)

    return dict(
        w_query=both(am, ao, 0, qw),
        w_key=both(am, ao, qw, kv),
        w_value=both(am, ao, qw + kv, kv),
        w_out=both(am, ao, qw + 2 * kv, qw),
        gain_attn=am[:, -2].astype(F32)[None, :],
        gain_ffn=am[:, -1].astype(F32)[None, :],
        w_gate=both(fm, fo, 0, ff),
        w_up=both(fm, fo, ff, ff),
        w_down=both(fm, fo, 2 * ff, ff),
    )


def layer_forward(x, tables, w, mask):
    rows = x.shape[0]
    groups = w["w_query"].shape[1] // w["w_key"].shape[1]
    kv_heads = w["w_key"].shape[1] // HEAD_SIZE
    xf = x.astype(F32)
    r1 = lax.rsqrt(jnp.mean(xf * xf, axis=-1, keepdims=True) + EPSILON)
    n1 = (xf * r1 * w["gain_attn"]).astype(BF)
    query = dot(n1, w["w_query"]).reshape(rows, -1, HEAD_SIZE)
    key = dot(n1, w["w_key"]).reshape(rows, -1, HEAD_SIZE)
    value = dot(n1, w["w_value"]).astype(BF).reshape(rows, -1, HEAD_SIZE)
    query = rotate(query, tables, 1.0).astype(BF).reshape(rows, kv_heads, groups, HEAD_SIZE)
    key = rotate(key, tables, 1.0).astype(BF)
    both = jnp.concatenate([key, value], 1)
    there = mate(both, "row", 1)
    keys = jnp.concatenate([there[:, :kv_heads], key], 0)
    values = jnp.concatenate([there[:, kv_heads:], value], 0)
    mixed, log_sums = attend(query, keys, values, mask)
    mixed = mixed.reshape(rows, -1)
    middle = own_rows(xf) + sum_scatter(dot_t(mixed, w["w_out"]).astype(BF))
    r2 = lax.rsqrt(jnp.mean(middle * middle, axis=-1, keepdims=True) + EPSILON)
    n2 = gather_rows((middle * r2 * w["gain_ffn"]).astype(BF))
    gate = dot(n2, w["w_gate"])
    up = dot(n2, w["w_up"])
    hidden = (jax.nn.silu(gate) * up).astype(BF)
    y = (middle + sum_scatter(dot_t(hidden, w["w_down"]).astype(BF))).astype(BF)
    out = gather_rows(y)
    kept = (own_rows(xf), own_rows(r1), n1, query, keys, values, mixed, log_sums)
    return out, kept + (middle, r2, n2, gate, up, hidden)


def layer_backward(kept, grad_out, tables, w, mask):
    (x, r1, n1, query, keys, values, mixed, log_sums, middle, r2, n2, gate, up, hidden) = kept
    rows = grad_out.shape[0]
    grad_hidden = dot(grad_out, w["w_down"])
    g_down = t_dot(grad_out, hidden)
    sig = jax.nn.sigmoid(gate)
    grad_gate = (grad_hidden * up * sig * (1.0 + gate * (1.0 - sig))).astype(BF)
    grad_up = (grad_hidden * gate * sig).astype(BF)
    g_gate = t_dot(n2, grad_gate)
    g_up = t_dot(n2, grad_up)
    grad_n2 = sum_scatter(
        (dot_t(grad_gate, w["w_gate"]) + dot_t(grad_up, w["w_up"])).astype(BF)
    )
    unit = middle * r2
    scaled = grad_n2 * w["gain_ffn"]
    g_gain_ffn = jnp.sum(grad_n2 * unit, axis=0)
    grad_middle = own_rows(grad_out).astype(F32) + r2 * (
        scaled - unit * jnp.mean(scaled * unit, axis=-1, keepdims=True)
    )
    grad_attn = gather_rows(grad_middle.astype(BF))
    grad_mixed = dot(grad_attn, w["w_out"]).astype(BF).reshape(query.shape)
    g_out = t_dot(grad_attn, mixed)
    grad_query, grad_keys, grad_values = attend_back(
        query, keys, values, log_sums, grad_mixed, mask
    )
    back = mate(
        jnp.concatenate([grad_keys[:rows], grad_values[:rows]], 1).astype(BF), "row", 1
    ).astype(F32)
    kv_heads = keys.shape[1]
    grad_key = grad_keys[rows:] + back[:, :kv_heads]
    grad_value = (grad_values[rows:] + back[:, kv_heads:]).astype(BF).reshape(rows, -1)
    grad_query = rotate(grad_query.reshape(rows, -1, HEAD_SIZE), tables, -1.0)
    grad_query = grad_query.astype(BF).reshape(rows, -1)
    grad_key = rotate(grad_key, tables, -1.0).astype(BF).reshape(rows, -1)
    g_query = t_dot(n1, grad_query)
    g_key = t_dot(n1, grad_key)
    g_value = t_dot(n1, grad_value)
    grad_n1 = sum_scatter(
        (
            dot_t(grad_query, w["w_query"])
            + dot_t(grad_key, w["w_key"])
            + dot_t(grad_value, w["w_value"])
        ).astype(BF)
    )
    unit = x * r1
    scaled = grad_n1 * w["gain_attn"]
    g_gain_attn = jnp.sum(grad_n1 * unit, axis=0)
    grad_x = grad_middle + r1 * (
        scaled - unit * jnp.mean(scaled * unit, axis=-1, keepdims=True)
    )
    grad_x = gather_rows(grad_x.astype(BF))

    def split(parts):
        return [
            jnp.concatenate([halves(p)[h] for p in parts], 1).astype(BF) for h in range(2)
        ]

    attn = split([g_query, g_key, g_value, g_out])
    ffn = split([g_gate, g_up, g_down])
    return grad_x, attn, ffn, (g_gain_attn, g_gain_ffn)


def reduce_grads(mine, other):
    n = lax.axis_size("row")
    got = mate(other, "section", 1)
    total = mine.astype(F32) + got.astype(F32)
    rows = total.shape[0] // n

    def slot(k):
        return total[k * rows : (k + 1) * rows]

    moving = slot(n - 1).astype(BF)
    for t in range(1, n):
        got = ring(moving, 1).astype(F32)
        here = slot(n - 1 - t) + got
        moving = here.astype(BF)
    return here


def reduce_gains(gains):
    s = lax.axis_index("section")
    n = lax.axis_size("row")
    total = gains
    for k in range(1, lax.axis_size("col")):
        total = total + mate(gains, "col", k)
    width = gains.shape[1] // n
    here = total[:, :width]
    for k in range(1, n):
        here = here + ring(total[:, k * width : (k + 1) * width], k)
    keep = jnp.where(s == 0, here[:2], here[2:])
    send = jnp.where(s == 0, here[2:], here[:2])
    return keep + mate(send, "section", 1)


def body(
    inputs,
    positions,
    w_query,
    key_weight,
    value_weight,
    w_out,
    w_gate,
    w_up,
    w_down,
    gain_attn,
    gain_ffn,
    cotangent,
):
    s = lax.axis_index("section")
    row = lax.axis_index("row")
    half_q, half_kv, half_ff = (
        w_query.shape[2] // 2,
        key_weight.shape[2] // 2,
        w_gate.shape[2] // 2,
    )
    gains = [gain_attn[0][:, None], gain_ffn[0][:, None]]
    own_attn = [
        jnp.concatenate(
            [halves(p[0])[h] for p in (w_query, key_weight, value_weight, w_out)] + gains, 1
        )
        for h in range(2)
    ]
    own_ffn = [
        jnp.concatenate([halves(p[0])[h] for p in (w_gate, w_up, w_down)], 1) for h in range(2)
    ]
    gathered = gather_weights(own_attn, own_ffn)
    weights = [layer_weights(g, half_kv, half_q, half_ff) for g in gathered]
    x = lax.dynamic_index_in_dim(inputs, s, 0, keepdims=False)
    place = lax.dynamic_index_in_dim(positions, s, 0, keepdims=False)
    grad = lax.dynamic_index_in_dim(cotangent, s, 0, keepdims=False)
    tables = rotation(place)
    mask = allowed(x.shape[0])
    x = roll_features(x, row)
    kept, outs = [], []
    for layer in range(2):
        x, state = layer_forward(x, tables, weights[layer], mask)
        kept.append(state)
        outs.append(x)
    grad = roll_features(grad, row)
    grads, parts, gain_parts = [None, None], [None, None], [None, None]
    for layer in (1, 0):
        grad, attn, ffn, gain_grads = layer_backward(
            kept[layer], grad, tables, weights[layer], mask
        )
        grads[layer] = grad
        ffn = reduce_grads(ffn[0], ffn[1])
        attn = reduce_grads(attn[0], attn[1])
        parts[layer] = (attn, ffn)
        gain_parts[layer] = gain_grads

    def swap_out(arrays):
        n = lax.axis_size("row")
        keep = jnp.where(s == 0, arrays[0], arrays[1])
        got = mate(jnp.where(s == 0, arrays[1], arrays[0]), "section", 1)
        return jnp.where(s == 0, jnp.stack([keep, got]), jnp.stack([got, keep]))

    acts = roll_features(swap_out(outs), -row)[None]
    in_grads = roll_features(swap_out(grads), -row)[None]
    attn = swap_out([parts[0][0], parts[1][0]])
    ffn = swap_out([parts[0][1], parts[1][1]])

    def pick(array, start, width):
        return jnp.concatenate(
            [array[0, :, start : start + width], array[1, :, start : start + width]], 1
        )[None]

    gains = reduce_gains(jnp.stack(list(gain_parts[0]) + list(gain_parts[1])))
    return (
        acts,
        in_grads,
        pick(attn, 0, half_q),
        pick(attn, half_q, half_kv),
        pick(attn, half_q + half_kv, half_kv),
        pick(attn, half_q + 2 * half_kv, half_q),
        pick(ffn, 0, half_ff),
        pick(ffn, half_ff, half_ff),
        pick(ffn, 2 * half_ff, half_ff),
        gains[0:1],
        gains[1:2],
    )


def solution(mesh):
    placed = (
        P(None, "row", None),
        P(None, "row"),
        *[P("section", "row", "col")] * 7,
        *[P("section", "row")] * 2,
        P(None, "row", None),
    )
    return jax.shard_map(
        body,
        mesh=mesh,
        in_specs=placed,
        out_specs=(
            *[P("section", None, "row", None)] * 2,
            *[P("section", "row", "col")] * 7,
            *[P("section", "row")] * 2,
        ),
        check_vma=False,
    )
```

time: 1610 us -> 863 us (0.54)
  waiting for transfers between devices: 1170 us -> 500 us
  starting transfers between devices: 21.7 us -> 122 us
  matrix products: 174 us -> 81.1 us
  blocking collectives: 82.2 us -> 0 us
  local copies, waits for them, and re-layouts: 40.5 us -> 74.6 us
  other arithmetic: 93.3 us -> 74 us
    psum x11 -> x0, waiting for transfers between devices: 748 us -> none  [the longest x3 246 us: layer_forward(): attn_out = lax.psum(contract_last(merged_heads, w_out), 'col')]
    ppermute x16 -> x109, waiting for transfers between devices: 38.5 us -> 500 us  [the longest x27 320 us: ring(): return lax.ppermute(x, 'row', [(j, (j + by) % n) for j in range(n)])]
    reduce_scatter x5 -> x0, waiting for transfers between devices: 194 us -> none  [the longest x1 60.3 us: scatter_end(): lax.psum_scatter(g_gate.astype(jnp.bfloat16), 'row', scatter_dimension=0,...]
    all_gather x5 -> x0, waiting for transfers between devices: 192 us -> none  [the longest x1 60.4 us: gather_each(): lax.all_gather(p_gate, 'row', axis=0, tiled=True)]
    ppermute x16 -> x109, starting transfers between devices: 19 us -> 122 us  [the longest x82 66.6 us: mate(): return lax.ppermute(x, axis, [(j, j ^ k) for j in range(n)])]
    dot_general x81 -> x54, matrix products: 174 us -> 81.1 us  [the longest x14 25.7 us: dot(): return jnp.dot(left, right, preferred_element_type=F32)]
    all_gather x4 -> x0, blocking collectives: 70.1 us -> none  [the longest x1 24.5 us: gather_each(): lax.all_gather(p_key, 'row', axis=0, tiled=True)]
    reduce_sum x15 -> x10, other arithmetic: 34.6 us -> 6.24 us  [the longest x2 2.29 us: attend(): total = jnp.sum(weights, axis=-1, keepdims=True)]
  transfers between devices with their start and end apart: 39 -> 109, of which waited for: 29 -> 53; matrix products, arithmetic and copies ran while one was open for 10% -> 20% of each run, Pallas kernels for 0% -> 0%
where the time goes in v1:
time: 863 us; the launch traced here: 856 us
  waiting for transfers between devices  500 us (58%)
  starting transfers between devices  122 us (14%)
  matrix products  81.1 us (9%)
  local copies, waits for them, and re-layouts  74.6 us (9%)
  other arithmetic  74 us (9%)
    ppermute x27, waiting for transfers between devices, ring(): return lax.ppermute(x, 'row', [(j, (j + by) % n) for j in range(n)])  320 us
    ppermute x82, waiting for transfers between devices, mate(): return lax.ppermute(x, axis, [(j, j ^ k) for j in range(n)])  180 us
    ppermute x82, starting transfers between devices, mate(): return lax.ppermute(x, axis, [(j, j ^ k) for j in range(n)])  66.6 us
    ppermute x27, starting transfers between devices, ring(): return lax.ppermute(x, 'row', [(j, (j + by) % n) for j in range(n)])  55 us
    unnamed x304, local copies, waits for them, and re-layouts  31 us
    dot_general x14, matrix products, dot(): return jnp.dot(left, right, preferred_element_type=F32)  25.7 us
    dot_general x14, matrix products, dot_t(): lax.dot_general(left, right, (((1,), (1,)), ((), ())), preferred_element_...  20.4 us
    dot_general x14, matrix products, t_dot(): lax.dot_general(left, right, (((0,), (0,)), ((), ())), preferred_element_...  17.4 us
  transfers between devices with their start and end apart: 109, of which 53 were waited for; matrix products, arithmetic and copies ran while one was open for 20% of the time, Pallas kernels for 0%

profile of v1, /device:TPU:0, one launch (start us, length us, event | category | flops | bytes accessed | tf_op | source)
XLA Modules:
  0.0 856.1 jit_solution(15791923286043124601)
XLA Ops:
  38.8 10.4 %collective-permute-done.1 = bf16[384,578]{1,0:T(8,128)(2,1)S(1)} collective-permute-done((bf16[384,578]{1,0:T(8,128)(2,1)S(1)}, bf16[384,578]{1,0:T(8,128)(2,1)S(1)}, u32[]{:S(2)}, u32[]{:S(2)}) %collective-permute-start.1) | collective-permute-done | bytes 443936 | tf_op jit(solution)/shard_map/ppermute | solution.py:24
  92.2 34.0 %collective-permute-done.31 = bf16[384,578]{1,0:T(8,128)(2,1)S(1)} collective-permute-done((bf16[384,578]{1,0:T(8,128)(2,1)S(1)}, bf16[384,578]{1,0:T(8,128)(2,1)S(1)}, u32[]{:S(2)}, u32[]{:S(2)}) %collective-permute-start.31) | collective-permute-done | bytes 443936 | tf_op jit(solution)/shard_map/ppermute | solution.py:24
  134.9 9.3 %collective-permute-done.8 = bf16[512,4,96]{0,2,1:T(8,128)(2,1)S(1)} collective-permute-done((bf16[512,4,96]{0,2,1:T(8,128)(2,1)S(1)}, bf16[512,4,96]{0,2,1:T(8,128)(2,1)S(1)}, u32[]{:S(2)}, u32[]{:S(2)}) %collective-permute-start.8) | collective-permute-done | bytes 393248 | tf_op jit(solution)/shard_map/ppermute | solution.py:19
  161.9 9.8 %collective-permute-done.10 = bf16[128,1536]{1,0:T(8,128)(2,1)S(1)} collective-permute-done((bf16[128,1536]{1,0:T(8,128)(2,1)S(1)}, bf16[128,1536]{1,0:T(8,128)(2,1)S(1)}, u32[]{:S(2)}, u32[]{:S(2)}) %collective-permute-start.10) | collective-permute-done | bytes 393248 | tf_op jit(solution)/shard_map/ppermute | solution.py:19
  180.3 8.0 collective-permute-done.43
  195.9 17.7 %collective-permute-done.17 = bf16[384,1536]{0,1:T(8,128)(2,1)S(1)} collective-permute-done((bf16[384,1536]{0,1:T(8,128)(2,1)S(1)}, bf16[384,1536]{0,1:T(8,128)(2,1)S(1)}, u32[]{:S(2)}, u32[]{:S(2)}) %collective-permute-start.17) | collective-permute-done | bytes 1179680 | tf_op jit(solution)/shard_map/ppermute | solution.py:24
  218.0 20.9 %collective-permute-done.44 = bf16[384,1536]{0,1:T(8,128)(2,1)S(1)} collective-permute-done((bf16[384,1536]{0,1:T(8,128)(2,1)S(1)}, bf16[384,1536]{0,1:T(8,128)(2,1)S(1)}, u32[]{:S(2)}, u32[]{:S(2)}) %collective-permute-start.44) | collective-permute-done | bytes 1179680 | tf_op jit(solution)/shard_map/ppermute | solution.py:24
  243.7 20.5 %collective-permute-done.18 = bf16[384,1536]{0,1:T(8,128)(2,1)S(1)} collective-permute-done((bf16[384,1536]{0,1:T(8,128)(2,1)S(1)}, bf16[384,1536]{0,1:T(8,128)(2,1)S(1)}, u32[]{:S(2)}, u32[]{:S(2)}) %collective-permute-start.18) | collective-permute-done | bytes 1179680 | tf_op jit(solution)/shard_map/ppermute | solution.py:24
  279.6 7.3 collective-permute-done.45
  288.1 8.8 %collective-permute-done.24 = bf16[128,1536]{1,0:T(8,128)(2,1)S(1)} collective-permute-done((bf16[128,1536]{1,0:T(8,128)(2,1)S(1)}, bf16[128,1536]{1,0:T(8,128)(2,1)S(1)}, u32[]{:S(2)}, u32[]{:S(2)}) %collective-permute-start.24) | collective-permute-done | bytes 393248 | tf_op jit(solution)/shard_map/ppermute | solution.py:19
  301.3 8.1 collective-permute-done.26
  309.5 7.6 collective-permute-done.27
  321.6 7.2 collective-permute-done.36
  340.4 6.4 collective-permute-done.37
  357.7 6.1 collective-permute-done.40
  363.8 6.4 collective-permute-done.41
  405.8 6.3 collective-permute-done.50
  412.4 9.1 %collective-permute-done.51 = bf16[128,1536]{1,0:T(8,128)(2,1)S(1)} collective-permute-done((bf16[128,1536]{1,0:T(8,128)(2,1)S(1)}, bf16[128,1536]{1,0:T(8,128)(2,1)S(1)}, u32[]{:S(2)}, u32[]{:S(2)}) %collective-permute-start.51) | collective-permute-done | bytes 393248 | tf_op jit(solution)/shard_map/ppermute | solution.py:19
  429.3 8.9 %collective-permute-done.61 = bf16[128,1536]{1,0:T(8,128)(2,1)S(1)} collective-permute-done((bf16[128,1536]{1,0:T(8,128)(2,1)S(1)}, bf16[128,1536]{1,0:T(8,128)(2,1)S(1)}, u32[]{:S(2)}, u32[]{:S(2)}) %collective-permute-start.61) | collective-permute-done | bytes 393248 | tf_op jit(solution)/shard_map/ppermute | solution.py:19
  468.8 8.4 collective-permute-done.64
  477.2 8.9 %collective-permute-done.65 = bf16[128,1536]{1,0:T(8,128)(2,1)S(1)} collective-permute-done((bf16[128,1536]{1,0:T(8,128)(2,1)S(1)}, bf16[128,1536]{1,0:T(8,128)(2,1)S(1)}, u32[]{:S(2)}, u32[]{:S(2)}) %collective-permute-start.65) | collective-permute-done | bytes 393248 | tf_op jit(solution)/shard_map/ppermute | solution.py:19
  492.8 6.5 collective-permute-done.67
  499.2 8.1 collective-permute-done.68
  554.9 8.9 %collective-permute-done.75 = bf16[128,1536]{1,0:T(8,128)(2,1)S(1)} collective-permute-done((bf16[128,1536]{1,0:T(8,128)(2,1)S(1)}, bf16[128,1536]{1,0:T(8,128)(2,1)S(1)}, u32[]{:S(2)}, u32[]{:S(2)}) %collective-permute-start.75) | collective-permute-done | bytes 393248 | tf_op jit(solution)/shard_map/ppermute | solution.py:19
  592.6 7.5 collective-permute-done.77
  641.5 20.3 %collective-permute-done.98 = bf16[384,1536]{0,1:T(8,128)(2,1)S(1)} collective-permute-done((bf16[384,1536]{0,1:T(8,128)(2,1)S(1)}, bf16[384,1536]{0,1:T(8,128)(2,1)S(1)}, u32[]{:S(2)}, u32[]{:S(2)}) %collective-permute-start.98) | collective-permute-done | bytes 1179680 | tf_op jit(solution)/shard_map/ppermute | solution.py:24
  662.3 24.8 %collective-permute-done.94 = bf16[384,1536]{0,1:T(8,128)(2,1)S(1)} collective-permute-done((bf16[384,1536]{0,1:T(8,128)(2,1)S(1)}, bf16[384,1536]{0,1:T(8,128)(2,1)S(1)}, u32[]{:S(2)}, u32[]{:S(2)}) %collective-permute-start.94) | collective-permute-done | bytes 1179680 | tf_op jit(solution)/shard_map/ppermute | solution.py:24
  689.8 32.1 %collective-permute-done.99 = bf16[384,1536]{0,1:T(8,128)(2,1)S(1)} collective-permute-done((bf16[384,1536]{0,1:T(8,128)(2,1)S(1)}, bf16[384,1536]{0,1:T(8,128)(2,1)S(1)}, u32[]{:S(2)}, u32[]{:S(2)}) %collective-permute-start.99) | collective-permute-done | bytes 1179680 | tf_op jit(solution)/shard_map/ppermute | solution.py:24
  722.3 24.8 %collective-permute-done.95 = bf16[384,1536]{0,1:T(8,128)(2,1)S(1)} collective-permute-done((bf16[384,1536]{0,1:T(8,128)(2,1)S(1)}, bf16[384,1536]{0,1:T(8,128)(2,1)S(1)}, u32[]{:S(2)}, u32[]{:S(2)}) %collective-permute-start.95) | collective-permute-done | bytes 1179680 | tf_op jit(solution)/shard_map/ppermute | solution.py:24
  747.6 9.0 %collective-permute-done.85 = bf16[384,576]{0,1:T(8,128)(2,1)S(1)} collective-permute-done((bf16[384,576]{0,1:T(8,128)(2,1)S(1)}, bf16[384,576]{0,1:T(8,128)(2,1)S(1)}, u32[]{:S(2)}, u32[]{:S(2)}) %collective-permute-start.85) | collective-permute-done | bytes 442400 | tf_op jit(solution)/shard_map/ppermute | solution.py:24
  758.2 57.2 %collective-permute-done.86 = bf16[384,576]{0,1:T(8,128)(2,1)S(1)} collective-permute-done((bf16[384,576]{0,1:T(8,128)(2,1)S(1)}, bf16[384,576]{0,1:T(8,128)(2,1)S(1)}, u32[]{:S(2)}, u32[]{:S(2)}) %collective-permute-start.86) | collective-permute-done | bytes 442400 | tf_op jit(solution)/shard_map/ppermute | solution.py:24
  819.8 9.5 %collective-permute-done.87 = bf16[384,576]{0,1:T(8,128)(2,1)} collective-permute-done((bf16[384,576]{0,1:T(8,128)(2,1)}, bf16[384,576]{0,1:T(8,128)(2,1)}, u32[]{:S(2)}, u32[]{:S(2)}) %collective-permute-start.87) | collective-permute-done | bytes 442400 | tf_op jit(solution)/shard_map/ppermute | solution.py:24
  (753 shorter events, 413.0 us)
Async XLA Ops:
  27.1 47.4 %collective-permute-start.15 = (bf16[384,1536]{0,1:T(8,128)(2,1)}, bf16[384,1536]{0,1:T(8,128)(2,1)}, u32[]{:S(2)}, u32[]{:S(2)}) collective-permute-start(bf16[384,1536]{0,1:T(8,128)(2,1)} %broadcast_select_fusion.4), channel_id=1, source_target_pairs={{0,16},{16,0},{1,17},{17,1},{2,18},{18,2},{3,19},{19,3},{4,20},{20... | collective-permute-start | bytes 3538952 | tf_op jit(solution)/shard_map/ppermute | solution.py:19
  76.4 81.3 %collective-permute-start.16 = (bf16[384,1536]{0,1:T(8,128)(2,1)S(1)}, bf16[384,1536]{0,1:T(8,128)(2,1)S(1)}, u32[]{:S(2)}, u32[]{:S(2)}) collective-permute-start(bf16[384,1536]{0,1:T(8,128)(2,1)S(1)} %get-tuple-element.98), channel_id=1, source_target_pairs={{0,12},{4,0},{8,4},{12,8},{1,13},{5,1},{9,5},{13,9},{2,14},{6,2},{... | collective-permute-start | bytes 3538952 | tf_op jit(solution)/shard_map/ppermute | solution.py:24
  76.4 102.2 %collective-permute-start.19 = (bf16[384,1536]{0,1:T(8,128)(2,1)S(1)}, bf16[384,1536]{0,1:T(8,128)(2,1)S(1)}, u32[]{:S(2)}, u32[]{:S(2)}) collective-permute-start(bf16[384,1536]{0,1:T(8,128)(2,1)S(1)} %get-tuple-element.98), channel_id=1, source_target_pairs={{0,16},{16,0},{1,17},{17,1},{2,18},{18,2},{3,19},{19,3},{4,20},{20... | collective-permute-start | bytes 3538952 | tf_op jit(solution)/shard_map/ppermute | solution.py:19
  80.7 47.8 %collective-permute-start.6 = (bf16[384,578]{1,0:T(8,128)(2,1)S(1)}, bf16[384,578]{1,0:T(8,128)(2,1)S(1)}, u32[]{:S(2)}, u32[]{:S(2)}) collective-permute-start(bf16[384,578]{1,0:T(8,128)(2,1)S(1)} %collective-permute-done.2), channel_id=1, source_target_pairs={{0,16},{16,0},{1,17},{17,1},{2,18},{18,2},{3,19},{19,3},{4,20},{20... | collective-permute-start | bytes 1331720 | tf_op jit(solution)/shard_map/ppermute | solution.py:19
  80.7 45.5 %collective-permute-start.31 = (bf16[384,578]{1,0:T(8,128)(2,1)S(1)}, bf16[384,578]{1,0:T(8,128)(2,1)S(1)}, u32[]{:S(2)}, u32[]{:S(2)}) collective-permute-start(bf16[384,578]{1,0:T(8,128)(2,1)S(1)} %collective-permute-done.30), channel_id=1, source_target_pairs={{0,12},{4,0},{8,4},{12,8},{1,13},{5,1},{9,5},{13,9},{2,14},{6,2},{... | collective-permute-start | bytes 1331720 | tf_op jit(solution)/shard_map/ppermute | solution.py:24
  91.3 37.9 %collective-permute-start.34 = (bf16[384,578]{1,0:T(8,128)(2,1)S(1)}, bf16[384,578]{1,0:T(8,128)(2,1)S(1)}, u32[]{:S(2)}, u32[]{:S(2)}) collective-permute-start(bf16[384,578]{1,0:T(8,128)(2,1)S(1)} %collective-permute-done.30), channel_id=1, source_target_pairs={{0,16},{16,0},{1,17},{17,1},{2,18},{18,2},{3,19},{19,3},{4,20},{20... | collective-permute-start | bytes 1331720 | tf_op jit(solution)/shard_map/ppermute | solution.py:19
  157.6 30.7 %collective-permute-start.43 = (bf16[384,1536]{0,1:T(8,128)(2,1)S(1)}, bf16[384,1536]{0,1:T(8,128)(2,1)S(1)}, u32[]{:S(2)}, u32[]{:S(2)}) collective-permute-start(bf16[384,1536]{0,1:T(8,128)(2,1)S(1)} %get-tuple-element.97), channel_id=1, source_target_pairs={{0,12},{4,0},{8,4},{12,8},{1,13},{5,1},{9,5},{13,9},{2,14},{6,2},{... | collective-permute-start | bytes 3538952 | tf_op jit(solution)/shard_map/ppermute | solution.py:24
  171.8 41.9 %collective-permute-start.17 = (bf16[384,1536]{0,1:T(8,128)(2,1)S(1)}, bf16[384,1536]{0,1:T(8,128)(2,1)S(1)}, u32[]{:S(2)}, u32[]{:S(2)}) collective-permute-start(bf16[384,1536]{0,1:T(8,128)(2,1)S(1)} %collective-permute-done.16), channel_id=1, source_target_pairs={{0,12},{4,0},{8,4},{12,8},{1,13},{5,1},{9,5},{13,9},{2,14},{6,2},{... | collective-permute-start | bytes 3538952 | tf_op jit(solution)/shard_map/ppermute | solution.py:24
  188.3 50.6 %collective-permute-start.20 = (bf16[384,1536]{0,1:T(8,128)(2,1)S(1)}, bf16[384,1536]{0,1:T(8,128)(2,1)S(1)}, u32[]{:S(2)}, u32[]{:S(2)}) collective-permute-start(bf16[384,1536]{0,1:T(8,128)(2,1)S(1)} %collective-permute-done.16), channel_id=1, source_target_pairs={{0,16},{16,0},{1,17},{17,1},{2,18},{18,2},{3,19},{19,3},{4,20},{20... | collective-permute-start | bytes 3538952 | tf_op jit(solution)/shard_map/ppermute | solution.py:19
  188.3 50.6 %collective-permute-start.44 = (bf16[384,1536]{0,1:T(8,128)(2,1)S(1)}, bf16[384,1536]{0,1:T(8,128)(2,1)S(1)}, u32[]{:S(2)}, u32[]{:S(2)}) collective-permute-start(bf16[384,1536]{0,1:T(8,128)(2,1)S(1)} %collective-permute-done.43), channel_id=1, source_target_pairs={{0,12},{4,0},{8,4},{12,8},{1,13},{5,1},{9,5},{13,9},{2,14},{6,2},{... | collective-permute-start | bytes 3538952 | tf_op jit(solution)/shard_map/ppermute | solution.py:24
  195.2 48.2 %collective-permute-start.47 = (bf16[384,1536]{0,1:T(8,128)(2,1)S(1)}, bf16[384,1536]{0,1:T(8,128)(2,1)S(1)}, u32[]{:S(2)}, u32[]{:S(2)}) collective-permute-start(bf16[384,1536]{0,1:T(8,128)(2,1)S(1)} %collective-permute-done.43), channel_id=1, source_target_pairs={{0,16},{16,0},{1,17},{17,1},{2,18},{18,2},{3,19},{19,3},{4,20},{20... | collective-permute-start | bytes 3538952 | tf_op jit(solution)/shard_map/ppermute | solution.py:19
  213.6 50.6 %collective-permute-start.18 = (bf16[384,1536]{0,1:T(8,128)(2,1)S(1)}, bf16[384,1536]{0,1:T(8,128)(2,1)S(1)}, u32[]{:S(2)}, u32[]{:S(2)}) collective-permute-start(bf16[384,1536]{0,1:T(8,128)(2,1)S(1)} %collective-permute-done.17), channel_id=1, source_target_pairs={{0,12},{4,0},{8,4},{12,8},{1,13},{5,1},{9,5},{13,9},{2,14},{6,2},{... | collective-permute-start | bytes 3538952 | tf_op jit(solution)/shard_map/ppermute | solution.py:24
  217.9 46.3 %collective-permute-start.21 = (bf16[384,1536]{0,1:T(8,128)(2,1)S(1)}, bf16[384,1536]{0,1:T(8,128)(2,1)S(1)}, u32[]{:S(2)}, u32[]{:S(2)}) collective-permute-start(bf16[384,1536]{0,1:T(8,128)(2,1)S(1)} %collective-permute-done.17), channel_id=1, source_target_pairs={{0,16},{16,0},{1,17},{17,1},{2,18},{18,2},{3,19},{19,3},{4,20},{20... | collective-permute-start | bytes 3538952 | tf_op jit(solution)/shard_map/ppermute | solution.py:19
  238.9 99.4 %collective-permute-start.48 = (bf16[384,1536]{0,1:T(8,128)(2,1)S(1)}, bf16[384,1536]{0,1:T(8,128)(2,1)}, u32[]{:S(2)}, u32[]{:S(2)}) collective-permute-start(bf16[384,1536]{0,1:T(8,128)(2,1)S(1)} %collective-permute-done.44), channel_id=1, source_target_pairs={{0,16},{16,0},{1,17},{17,1},{2,18},{18,2},{3,19},{19,3},{4,20},{20... | collective-permute-start | bytes 3538952 | tf_op jit(solution)/shard_map/ppermute | solution.py:19
  238.9 48.0 %collective-permute-start.45 = (bf16[384,1536]{0,1:T(8,128)(2,1)S(1)}, bf16[384,1536]{0,1:T(8,128)(2,1)S(1)}, u32[]{:S(2)}, u32[]{:S(2)}) collective-permute-start(bf16[384,1536]{0,1:T(8,128)(2,1)S(1)} %collective-permute-done.44), channel_id=1, source_target_pairs={{0,12},{4,0},{8,4},{12,8},{1,13},{5,1},{9,5},{13,9},{2,14},{6,2},{... | collective-permute-start | bytes 3538952 | tf_op jit(solution)/shard_map/ppermute | solution.py:24
  299.8 40.0 %collective-permute-start.49 = (bf16[384,1536]{0,1:T(8,128)(2,1)S(1)}, bf16[384,1536]{0,1:T(8,128)(2,1)S(1)}, u32[]{:S(2)}, u32[]{:S(2)}) collective-permute-start(bf16[384,1536]{0,1:T(8,128)(2,1)S(1)} %collective-permute-done.45), channel_id=1, source_target_pairs={{0,16},{16,0},{1,17},{17,1},{2,18},{18,2},{3,19},{19,3},{4,20},{20... | collective-permute-start | bytes 3538952 | tf_op jit(solution)/shard_map/ppermute | solution.py:19
  399.9 225.8 %collective-permute-start.97 = (bf16[1536,1536]{0,1:T(8,128)(2,1)}, bf16[1536,1536]{0,1:T(8,128)(2,1)}, u32[]{:S(2)}, u32[]{:S(2)}) collective-permute-start(bf16[1536,1536]{0,1:T(8,128)(2,1)} %pad_maximum_fusion.3), channel_id=1, source_target_pairs={{0,16},{16,0},{1,17},{17,1},{2,18},{18,2},{3,19},{19,3},{4,20},{20... | collective-permute-start | bytes 14155784 | tf_op jit(solution)/shard_map/ppermute | solution.py:19
  457.6 84.5 %collective-permute-start.56 = (bf16[512,1536]{1,0:T(8,128)(2,1)S(1)}, bf16[512,1536]{1,0:T(8,128)(2,1)S(1)}, u32[]{:S(2)}, u32[]{:S(2)}) collective-permute-start(bf16[512,1536]{1,0:T(8,128)(2,1)S(1)} %get-tuple-element.114), channel_id=1, source_target_pairs={{0,16},{16,0},{1,17},{17,1},{2,18},{18,2},{3,19},{19,3},{4,20},{20... | collective-permute-start | bytes 4718600 | tf_op jit(solution)/shard_map/ppermute | solution.py:19
  534.0 45.2 %collective-permute-start.88 = (bf16[1536,576]{0,1:T(8,128)(2,1)}, bf16[1536,576]{0,1:T(8,128)(2,1)}, u32[]{:S(2)}, u32[]{:S(2)}) collective-permute-start(bf16[1536,576]{0,1:T(8,128)(2,1)} %pad_maximum_fusion.25), channel_id=1, source_target_pairs={{0,16},{16,0},{1,17},{17,1},{2,18},{18,2},{3,19},{19,3},{4,20},{20... | collective-permute-start | bytes 5308424 | tf_op jit(solution)/shard_map/ppermute | solution.py:19
  538.8 92.3 %collective-permute-start.93 = (bf16[1536,1536]{0,1:T(8,128)(2,1)}, bf16[1536,1536]{0,1:T(8,128)(2,1)}, u32[]{:S(2)}, u32[]{:S(2)}) collective-permute-start(bf16[1536,1536]{0,1:T(8,128)(2,1)} %pad_maximum_fusion.2), channel_id=1, source_target_pairs={{0,16},{16,0},{1,17},{17,1},{2,18},{18,2},{3,19},{19,3},{4,20},{20... | collective-permute-start | bytes 14155784 | tf_op jit(solution)/shard_map/ppermute | solution.py:19
  620.9 66.7 %collective-permute-start.84 = (bf16[1536,576]{0,1:T(8,128)(2,1)}, bf16[1536,576]{0,1:T(8,128)(2,1)}, u32[]{:S(2)}, u32[]{:S(2)}) collective-permute-start(bf16[1536,576]{0,1:T(8,128)(2,1)} %pad_maximum_fusion.24), channel_id=1, source_target_pairs={{0,16},{16,0},{1,17},{17,1},{2,18},{18,2},{3,19},{19,3},{4,20},{20... | collective-permute-start | bytes 5308424 | tf_op jit(solution)/shard_map/ppermute | solution.py:19
  631.0 30.7 %collective-permute-start.98 = (bf16[384,1536]{0,1:T(8,128)(2,1)S(1)}, bf16[384,1536]{0,1:T(8,128)(2,1)S(1)}, u32[]{:S(2)}, u32[]{:S(2)}) collective-permute-start(bf16[384,1536]{0,1:T(8,128)(2,1)S(1)} %slice.881), channel_id=1, source_target_pairs={{0,4},{4,8},{8,12},{12,0},{1,5},{5,9},{9,13},{13,1},{2,6},{6,10},{... | collective-permute-start | bytes 3538952 | tf_op jit(solution)/shard_map/ppermute | solution.py:24
  636.2 50.9 %collective-permute-start.94 = (bf16[384,1536]{0,1:T(8,128)(2,1)S(1)}, bf16[384,1536]{0,1:T(8,128)(2,1)S(1)}, u32[]{:S(2)}, u32[]{:S(2)}) collective-permute-start(bf16[384,1536]{0,1:T(8,128)(2,1)S(1)} %slice.882), channel_id=1, source_target_pairs={{0,4},{4,8},{8,12},{12,0},{1,5},{5,9},{9,13},{13,1},{2,6},{6,10},{... | collective-permute-start | bytes 3538952 | tf_op jit(solution)/shard_map/ppermute | solution.py:24
  639.0 108.5 %collective-permute-start.82 = (bf16[128,1536]{1,0:T(8,128)(2,1)}, bf16[128,1536]{1,0:T(8,128)(2,1)S(1)}, u32[]{:S(2)}, u32[]{:S(2)}) collective-permute-start(bf16[128,1536]{1,0:T(8,128)(2,1)} %get-tuple-element.46), channel_id=1, source_target_pairs={{0,3},{1,2},{2,1},{3,0},{4,7},{5,6},{6,5},{7,4},{8,11},{9,10},{10,... | collective-permute-start | bytes 1179656 | tf_op jit(solution)/shard_map/ppermute | solution.py:19
  640.0 179.7 %collective-permute-start.91 = (bf16[384,576]{0,1:T(8,128)(2,1)}, bf16[384,576]{0,1:T(8,128)(2,1)}, u32[]{:S(2)}, u32[]{:S(2)}) collective-permute-start(bf16[384,576]{0,1:T(8,128)(2,1)} %fusion.55), channel_id=1, source_target_pairs={{0,4},{4,8},{8,12},{12,0},{1,5},{5,9},{9,13},{13,1},{2,6},{6,10},{... | collective-permute-start | bytes 1327112 | tf_op jit(solution)/shard_map/ppermute | solution.py:24
  662.2 59.6 %collective-permute-start.99 = (bf16[384,1536]{0,1:T(8,128)(2,1)S(1)}, bf16[384,1536]{0,1:T(8,128)(2,1)S(1)}, u32[]{:S(2)}, u32[]{:S(2)}) collective-permute-start(bf16[384,1536]{0,1:T(8,128)(2,1)S(1)} %fusion.26), channel_id=1, source_target_pairs={{0,4},{4,8},{8,12},{12,0},{1,5},{5,9},{9,13},{13,1},{2,6},{6,10},{... | collective-permute-start | bytes 3538952 | tf_op jit(solution)/shard_map/ppermute | solution.py:24
  687.4 59.7 %collective-permute-start.95 = (bf16[384,1536]{0,1:T(8,128)(2,1)S(1)}, bf16[384,1536]{0,1:T(8,128)(2,1)S(1)}, u32[]{:S(2)}, u32[]{:S(2)}) collective-permute-start(bf16[384,1536]{0,1:T(8,128)(2,1)S(1)} %fusion.28), channel_id=1, source_target_pairs={{0,4},{4,8},{8,12},{12,0},{1,5},{5,9},{9,13},{13,1},{2,6},{6,10},{... | collective-permute-start | bytes 3538952 | tf_op jit(solution)/shard_map/ppermute | solution.py:24
  689.6 67.0 %collective-permute-start.85 = (bf16[384,576]{0,1:T(8,128)(2,1)S(1)}, bf16[384,576]{0,1:T(8,128)(2,1)S(1)}, u32[]{:S(2)}, u32[]{:S(2)}) collective-permute-start(bf16[384,576]{0,1:T(8,128)(2,1)S(1)} %slice.884), channel_id=1, source_target_pairs={{0,4},{4,8},{8,12},{12,0},{1,5},{5,9},{9,13},{13,1},{2,6},{6,10},{... | collective-permute-start | bytes 1327112 | tf_op jit(solution)/shard_map/ppermute | solution.py:24
  722.2 94.1 %collective-permute-start.100 = (bf16[384,1536]{0,1:T(8,128)(2,1)S(1)}, bf16[384,1536]{0,1:T(8,128)(2,1)S(1)}, u32[]{:S(2)}, u32[]{:S(2)}) collective-permute-start(bf16[384,1536]{0,1:T(8,128)(2,1)S(1)} %fusion.27), channel_id=1, source_target_pairs={{0,4},{4,8},{8,12},{12,0},{1,5},{5,9},{9,13},{13,1},{2,6},{6,10},{... | collective-permute-start | bytes 3538952 | tf_op jit(solution)/shard_map/ppermute | solution.py:24
  747.5 68.8 %collective-permute-start.96 = (bf16[384,1536]{0,1:T(8,128)(2,1)S(1)}, bf16[384,1536]{0,1:T(8,128)(2,1)}, u32[]{:S(2)}, u32[]{:S(2)}) collective-permute-start(bf16[384,1536]{0,1:T(8,128)(2,1)S(1)} %fusion.29), channel_id=1, source_target_pairs={{0,4},{4,8},{8,12},{12,0},{1,5},{5,9},{9,13},{13,1},{2,6},{6,10},{... | collective-permute-start | bytes 3538952 | tf_op jit(solution)/shard_map/ppermute | solution.py:24
  756.7 58.6 %collective-permute-start.86 = (bf16[384,576]{0,1:T(8,128)(2,1)S(1)}, bf16[384,576]{0,1:T(8,128)(2,1)S(1)}, u32[]{:S(2)}, u32[]{:S(2)}) collective-permute-start(bf16[384,576]{0,1:T(8,128)(2,1)S(1)} %fusion.56), channel_id=1, source_target_pairs={{0,4},{4,8},{8,12},{12,0},{1,5},{5,9},{9,13},{13,1},{2,6},{6,10},{... | collective-permute-start | bytes 1327112 | tf_op jit(solution)/shard_map/ppermute | solution.py:24
  758.1 73.2 %collective-permute-start.83 = (bf16[512,1536]{1,0:T(8,128)(2,1)}, bf16[512,1536]{1,0:T(8,128)(2,1)S(1)}, u32[]{:S(2)}, u32[]{:S(2)}) collective-permute-start(bf16[512,1536]{1,0:T(8,128)(2,1)} %get-tuple-element.112), channel_id=1, source_target_pairs={{0,16},{16,0},{1,17},{17,1},{2,18},{18,2},{3,19},{19,3},{4,20},{20... | collective-permute-start | bytes 4718600 | tf_op jit(solution)/shard_map/ppermute | solution.py:19
  (218 other events, 3558.9 us)

commit v2 on v1

v2 whole, which is shorter than its diff:
```python
import functools
import math

import jax
import jax.numpy as jnp
from jax import lax
from jax.experimental import pallas as pl
from jax.experimental.pallas import tpu as pltpu
from jax.sharding import PartitionSpec as P

HEAD_SIZE = 96
HALF = HEAD_SIZE // 2
EPSILON = 1e-05
ROPE_BASE = 100000.0
MASKED = -1e30
COST = 2 * 10**11
BF = jnp.bfloat16
F32 = jnp.float32
WHOLE = pl.BlockSpec(memory_space=pltpu.VMEM)
ANYWHERE = pl.BlockSpec(memory_space=pl.ANY)
FAR = pl.BlockSpec(memory_space=pltpu.HBM)
SCALAR = pl.BlockSpec(memory_space=pltpu.SMEM)


def mate(x, axis, k):
    n = lax.axis_size(axis)
    return lax.ppermute(x, axis, [(j, j ^ k) for j in range(n)])


def ring(x, by):
    n = lax.axis_size("row")
    return lax.ppermute(x, "row", [(j, (j + by) % n) for j in range(n)])


def gather_pieces(local):
    return [local] + [mate(local, "col", k) for k in range(1, lax.axis_size("col"))]


def dot(left, right):
    return jnp.dot(left, right, preferred_element_type=F32)


def dot_t(left, right):
    return lax.dot_general(left, right, (((1,), (1,)), ((), ())), preferred_element_type=F32)


def t_dot(left, right):
    return lax.dot_general(left, right, (((0,), (0,)), ((), ())), preferred_element_type=F32)


def stacked(refs):
    return jnp.concatenate([r[...] for r in refs], axis=0)


def kernel(name, body, ins, outs, grid=(), scratch=(), after=(), vmem=44, flops=0, path=False):
    arrays, specs, sizes = [], [], []
    for group in ins:
        sizes.append(len(group))
        for array, spec in group:
            arrays.append(array)
            specs.append(spec)
    count = len(arrays)
    after = list(after)
    arrays += after
    specs += [ANYWHERE] * len(after)

    def run(*refs):
        groups, at = [], 0
        for size in sizes:
            groups.append(refs[at : at + size])
            at += size
        at = count + len(after)
        body(*groups, refs[at : at + len(outs)], refs[at + len(outs) :])

    size = sum(a.size * a.dtype.itemsize for a in arrays[:count])
    size += sum(math.prod(o.shape) * jnp.dtype(o.dtype).itemsize for o, _ in outs)
    return pl.pallas_call(
        run,
        grid=grid,
        in_specs=specs,
        out_specs=[spec for _, spec in outs],
        out_shape=[shape for shape, _ in outs],
        scratch_shapes=list(scratch),
        compiler_params=pltpu.CompilerParams(vmem_limit_bytes=vmem << 20),
        cost_estimate=pl.CostEstimate(
            flops=COST if path else 0, bytes_accessed=size if path else 1, transcendentals=0
        ),
        name=name,
    )(*arrays)


def kernel_list(*args, **settings):
    return list(kernel(*args, **settings))


def shaped(shape, dtype=BF, spec=WHOLE):
    return (jax.ShapeDtypeStruct(tuple(shape), dtype), spec)


def full(arrays, spec=WHOLE):
    return [(a, spec) for a in arrays]


def enter(x, order, c, count, after=(), path=False):
    rows = x.shape[0] // count

    def body(xs, orders, cs, outs, _):
        for k in range(count):
            start = pl.multiple_of((cs[0][0] ^ k) * rows, 16)
            outs[k][...] = dot(xs[0][pl.ds(start, rows), :], orders[0][...]).astype(BF)

    return kernel_list(
        "enter",
        body,
        [full([x]), full([order]), full([c], SCALAR)],
        [shaped((rows, x.shape[1]))] * count,
        after=after,
        vmem=16,
        path=path,
    )


def leave(pieces, back, c, after=()):
    rows, width = pieces[0].shape
    count = len(pieces)

    def body(ps, orders, cs, outs, _):
        y = dot(stacked(ps), orders[0][...]).astype(BF)
        for k in range(count):
            start = pl.multiple_of((cs[0][0] ^ k) * rows, 16)
            outs[0][pl.ds(start, rows), :] = y[k * rows : (k + 1) * rows]

    return kernel(
        "leave",
        body,
        [full(pieces), full([back]), full([c], SCALAR)],
        [shaped((rows * count, width))],
        after=after,
        vmem=20,
        flops=2 * rows * count * width * width,
    )[0]


def pack(parts, s, after=()):
    h = parts[0].shape[0] // 2
    width = sum(p.shape[1] for p in parts)

    def body(ps, ss, outs, _):
        for out, side in zip(outs, (ss[0][0], 1 - ss[0][0])):
            start = pl.multiple_of(side * h, 16)
            at = 0
            for p in ps:
                out[:, at : at + p.shape[1]] = p[pl.ds(start, h), :]
                at += p.shape[1]

    return kernel("pack", body, [full(parts), full([s], SCALAR)], [shaped((h, width))] * 2, after=after, vmem=16)


def unpack(mine, theirs, s, widths, after=()):
    h, total = mine[0].shape

    def body(ms, ts, ss, outs, scratch):
        side = ss[0][0]
        for layer in range(2):

            @pl.when(side == layer)
            def _():
                copies = [
                    pltpu.make_async_copy(ref, scratch[k], scratch[2].at[k])
                    for k, ref in enumerate((ms[layer], ts[layer]))
                ]
                for copy in copies:
                    copy.start()
                for copy in copies:
                    copy.wait()

        for k, at in enumerate((side, 1 - side)):
            start = pl.multiple_of(at * h, 16)
            column = 0
            for out in outs:
                width = out.shape[1]
                out[pl.ds(start, h), :] = scratch[k][:, column : column + width].astype(F32)
                column += width

    return kernel(
        "unpack",
        body,
        [full(mine, FAR), full(theirs, FAR), full([s], SCALAR)],
        [shaped((2 * h, w), F32) for w in widths],
        scratch=[pltpu.VMEM((h, total), BF)] * 2 + [pltpu.SemaphoreType.DMA((2,))],
        after=after,
        vmem=20,
    )


def place_out(mine, theirs, s, after=()):
    shape = mine[0].shape

    def body(ms, ts, ss, outs, scratch):
        side = ss[0][0]
        for layer in range(2):

            @pl.when(side == layer)
            def _():
                copies = [
                    pltpu.make_async_copy(ref, outs[0].at[at], scratch[0].at[k])
                    for k, (ref, at) in enumerate(((ms[layer], layer), (ts[layer], 1 - layer)))
                ]
                for copy in copies:
                    copy.start()
                for copy in copies:
                    copy.wait()

    return kernel(
        "place_out",
        body,
        [full(mine, FAR), full(theirs, FAR), full([s], SCALAR)],
        [shaped((2,) + shape, mine[0].dtype)],
        scratch=[pltpu.SemaphoreType.DMA((2,))],
        after=after,
        vmem=16,
    )[0]


def meet(after):
    def body(outs, _):
        outs[0][...] = jnp.zeros(outs[0].shape, F32)

    return kernel_list("meet", body, [], [shaped((8, 128), F32)], after=after, vmem=2, path=True)


def turn(x, cosine, sine, swap, sign):
    high = x.astype(BF)
    low = (x - high.astype(F32)).astype(BF)
    return x * cosine + (dot(high, swap) + dot(low, swap)) * (sine * sign)


class Fetch:
    def __init__(self, slots, target, sems, column, base=0):
        h, width = slots[0].shape[0], target.shape[1]
        self.target = target
        self.copies = [
            pltpu.make_async_copy(
                ref.at[:, pl.ds(column, width)], target.at[pl.ds(k * h, h), :], sems.at[base + k]
            )
            for k, ref in enumerate(slots)
        ]
        for copy in self.copies:
            copy.start()

    def get(self):
        for copy in self.copies:
            copy.wait()
        return self.target[...]


def pieces_of(value, outs, count, first=0):
    rows = value.shape[0] // count
    for k in range(count):
        outs[first + k][...] = value[k * rows : (k + 1) * rows]


def project(pieces, gain, slots, tables, swaps, width_q, after=()):
    rows, width = pieces[0].shape
    tokens = rows * len(pieces)

    def body(ps, gains, ws, ts, ks, outs, scratch):
        w = Fetch(ws, scratch[0], scratch[1], 0)
        x = stacked(ps).astype(F32)
        scale = lax.rsqrt(jnp.mean(x * x, axis=-1, keepdims=True) + EPSILON)
        n1 = (x * scale * gains[0][...]).astype(BF)
        outs[0][...] = n1
        w.get()
        for part in range(2):
            cols = slice(part * width_q, (part + 1) * width_q)
            raw = dot(n1, scratch[0][:, cols])
            turned = turn(raw, ts[0][:, cols], ts[1][:, cols], ks[part][...], 1.0)
            outs[1 + part][...] = turned.astype(BF)

    return kernel(
        "project",
        body,
        [full(pieces), full([gain]), full(slots, FAR), full(tables), full(swaps)],
        [shaped((tokens, width)), shaped((tokens, width_q)), shaped((tokens, width_q))],
        scratch=[pltpu.VMEM((width, 2 * width_q), BF), pltpu.SemaphoreType.DMA((len(slots),))],
        path=True,
        after=after,
        vmem=24,
        flops=4 * tokens * width * width_q,
    )


def head(ref, at):
    return ref[:, at * HEAD_SIZE : (at + 1) * HEAD_SIZE]


def attention(query, own, there, orders, slots, count, after=()):
    tokens, width_q = query.shape
    rows = tokens // count
    width = slots[0].shape[0] * len(slots)
    heads = width_q // HEAD_SIZE
    kv = heads // 2
    scale = 1.0 / math.sqrt(HEAD_SIZE)

    def body(qs, owns, theres, os, ws, outs, scratch):
        w = Fetch(ws, scratch[0], scratch[1], 2 * width_q)
        seen = os[1][...] <= os[0][...]
        for g in range(kv):
            keys = jnp.concatenate([head(owns[0], g), head(theres[0], g)], 0)
            values = jnp.concatenate([head(owns[0], kv + g), head(theres[0], kv + g)], 0)
            for h in range(2 * g, 2 * g + 2):
                scores = jnp.where(seen, dot_t(keys, head(qs[0], h)), MASKED)
                peak = jnp.max(scores, axis=0, keepdims=True)
                weights = jnp.exp((scores - peak) * scale)
                total = jnp.sum(weights, axis=0, keepdims=True)
                outs[1][h : h + 1, :] = peak * scale + jnp.log(total)
                mixed = t_dot(values, weights.astype(BF)) / total
                outs[0][:, h * HEAD_SIZE : (h + 1) * HEAD_SIZE] = mixed.T.astype(BF)
        pieces_of(dot_t(outs[0][...], w.get()).astype(BF), outs, count, 2)

    mixed, log_sums, *pieces = kernel(
        "attention",
        body,
        [full([query]), full([own]), full([there]), full(orders), full(slots, FAR)],
        [shaped((tokens, width_q)), shaped((heads, tokens), F32)] + [shaped((rows, width))] * count,
        scratch=[pltpu.VMEM((width, width_q), BF), pltpu.SemaphoreType.DMA((len(slots),))],
        path=True,
        after=after,
        vmem=30,
        flops=2 * tokens * width * width_q + 8 * tokens * tokens * width_q,
    )
    return mixed, log_sums, pieces


def attention_back(pieces, query, own, there, log_sums, orders, slots, after=()):
    tokens, width_q = query.shape
    width = slots[0].shape[0] * len(slots)
    heads = width_q // HEAD_SIZE
    kv = heads // 2
    scale = 1.0 / math.sqrt(HEAD_SIZE)

    def body(ps, qs, owns, theres, ls, os, ws, outs, scratch):
        w = Fetch(ws, scratch[0], scratch[1], 2 * width_q)
        seen = os[1][...] <= os[0][...]
        scratch[2][...] = dot(stacked(ps), w.get()).astype(BF)
        for g in range(kv):
            keys = jnp.concatenate([head(owns[0], g), head(theres[0], g)], 0)
            values = jnp.concatenate([head(owns[0], kv + g), head(theres[0], kv + g)], 0)
            sums = [None, None]
            for h in range(2 * g, 2 * g + 2):
                q, grad = head(qs[0], h), head(scratch[2], h)
                scores = dot_t(keys, q) * scale - ls[0][h : h + 1, :]
                probs = jnp.exp(jnp.where(seen, scores, MASKED))
                grad_probs = dot_t(values, grad)
                inner = jnp.sum(probs * grad_probs, axis=0, keepdims=True)
                grad_scores = (probs * (grad_probs - inner)).astype(BF)
                cols = slice(h * HEAD_SIZE, (h + 1) * HEAD_SIZE)
                outs[0][:, cols] = (t_dot(keys, grad_scores) * scale).T
                terms = (dot(grad_scores, q) * scale, dot(probs.astype(BF), grad))
                sums = [t if u is None else t + u for t, u in zip(terms, sums)]
            for at, total in zip((g, kv + g), sums):
                cols = slice(at * HEAD_SIZE, (at + 1) * HEAD_SIZE)
                outs[1][:, cols] = total[:tokens]
                outs[2][:, cols] = total[tokens:].astype(BF)

    return kernel(
        "attention_back",
        body,
        [full(pieces), full([query]), full([own]), full([there]), full([log_sums])]
        + [full(orders), full(slots, FAR)],
        [shaped((tokens, width_q), F32)] * 2 + [shaped((tokens, width_q))],
        scratch=[
            pltpu.VMEM((width, width_q), BF),
            pltpu.SemaphoreType.DMA((len(slots),)),
            pltpu.VMEM((tokens, width_q), BF),
        ],
        path=True,
        after=after,
        vmem=32,
        flops=2 * tokens * width * width_q + 20 * tokens * tokens * width_q,
    )


def project_back(grad_query, grad_own, grad_there, slots, tables, swaps, count, after=()):
    tokens, width_q = grad_query.shape
    rows = tokens // count
    width = slots[0].shape[0] * len(slots)

    def body(qs, owns, theres, ws, ts, ks, outs, scratch):
        w = Fetch(ws, scratch[0], scratch[1], 0)
        grads = (qs[0][...], owns[0][...] + theres[0][...].astype(F32))
        for part in range(2):
            cols = slice(part * width_q, (part + 1) * width_q)
            turned = turn(grads[part], ts[0][:, cols], ts[1][:, cols], ks[part][...], -1.0)
            outs[count][:, cols] = turned.astype(BF)
        pieces_of(dot_t(outs[count][...], w.get()).astype(BF), outs, count)

    *pieces, grads = kernel(
        "project_back",
        body,
        [full([grad_query]), full([grad_own]), full([grad_there]), full(slots, FAR)]
        + [full(tables), full(swaps)],
        [shaped((rows, width))] * count + [shaped((tokens, 2 * width_q))],
        scratch=[pltpu.VMEM((width, 2 * width_q), BF), pltpu.SemaphoreType.DMA((len(slots),))],
        path=True,
        after=after,
        vmem=24,
        flops=4 * tokens * width * width_q,
    )
    return pieces, grads


def feed_forward(pieces, slots, after=()):
    rows, width = pieces[0].shape
    count = len(pieces)
    tokens = rows * count
    units = slots[0].shape[1] // 3

    def body(ps, ws, outs, scratch):
        parts = [
            Fetch(ws, scratch[k], scratch[3], k * units, k * len(slots)) for k in range(3)
        ]
        n2 = stacked(ps)
        gate = dot(n2, parts[0].get())
        up = dot(n2, parts[1].get())
        outs[0][...] = gate.astype(BF)
        outs[1][...] = up.astype(BF)
        outs[2][...] = (gate / (1.0 + jnp.exp(-gate)) * up).astype(BF)
        pieces_of(dot_t(outs[2][...], parts[2].get()).astype(BF), outs, count, 3)

    gate, up, hidden, *out = kernel(
        "feed_forward",
        body,
        [full(pieces), full(slots, FAR)],
        [shaped((tokens, units))] * 3 + [shaped((rows, width))] * count,
        scratch=[pltpu.VMEM((width, units), BF)] * 3
        + [pltpu.SemaphoreType.DMA((3 * len(slots),))],
        path=True,
        after=after,
        vmem=32,
        flops=6 * tokens * width * units,
    )
    return gate, up, hidden, out


def feed_forward_back(pieces, gate, up, slots, after=()):
    rows, width = pieces[0].shape
    count = len(pieces)
    tokens = rows * count
    units = gate.shape[1]

    def body(ps, gus, ws, outs, scratch):
        down = Fetch(ws, scratch[0], scratch[2], 2 * units)
        rest = Fetch(ws, scratch[1], scratch[2], 0, len(slots))
        grad = dot(stacked(ps), down.get())
        gate, up = gus[0][...].astype(F32), gus[1][...].astype(F32)
        sig = 1.0 / (1.0 + jnp.exp(-gate))
        part = grad * sig
        outs[0][:, :units] = (part * up * (1.0 + gate * (1.0 - sig))).astype(BF)
        outs[0][:, units:] = (part * gate).astype(BF)
        pieces_of(dot_t(outs[0][...], rest.get()).astype(BF), outs, count, 1)

    grads, *out = kernel(
        "feed_forward_back",
        body,
        [full(pieces), full([gate, up]), full(slots, FAR)],
        [shaped((tokens, 2 * units))] + [shaped((rows, width))] * count,
        scratch=[pltpu.VMEM((width, units), BF), pltpu.VMEM((width, 2 * units), BF)]
        + [pltpu.SemaphoreType.DMA((2 * len(slots),))],
        path=True,
        after=after,
        vmem=32,
        flops=6 * tokens * width * units,
    )
    return grads, out


def weight_grads(terms, half, block, got=None, after=()):
    width = terms[0][0][0].shape[1] // 2
    tokens = terms[0][1].shape[0]
    steps = [rhs.shape[1] // block for _, rhs in terms]
    total = sum(rhs.shape[1] for _, rhs in terms)
    n = 1 if got is None else lax.axis_size("row")
    rows = width // n
    ins, begins = [], []
    for k, (lhs, rhs) in enumerate(terms):
        begin = sum(steps[:k])
        begins.append(begin)
        ins.append([(a, pl.BlockSpec((a.shape[0], width), lambda j: (0, half))) for a in lhs])
        place = functools.partial(
            lambda j, lo, hi: (0, jnp.clip(j - lo, 0, hi)), lo=begin, hi=steps[k] - 1
        )
        ins.append([(rhs, pl.BlockSpec((tokens, block), place))])
    ins.append([] if got is None else [(got, pl.BlockSpec((width, block), lambda j: (0, j)))])

    def body(*refs):
        *refs, more, outs, scratch = refs
        j = pl.program_id(0)
        for k, begin in enumerate(begins):
            lhs, rhs = refs[2 * k : 2 * k + 2]

            @pl.when(j == begin)
            def _():
                scratch[0][...] = stacked(lhs).T

            @pl.when((j >= begin) & (j < begin + steps[k]))
            def _():
                value = dot(scratch[0][...], rhs[0][...])
                if got is not None:
                    value = value + more[0][...].astype(F32)
                value = value.astype(BF)
                for k in range(n):
                    outs[k][...] = value[k * rows : (k + 1) * rows]

    out = kernel(
        "weight_grads",
        body,
        ins,
        [shaped((rows, total), BF, pl.BlockSpec((rows, block), lambda j: (0, j)))] * n,
        grid=(sum(steps),),
        scratch=[pltpu.VMEM((width, tokens), BF)],
        after=after,
        vmem=20,
        flops=2 * tokens * width * total,
    )
    return out[0] if got is None else out


def total_of(refs):
    total = refs[0][...].astype(F32)
    for r in refs[1:]:
        total = total + r[...].astype(F32)
    return total


def inverse_rms(x):
    return lax.rsqrt(jnp.mean(x * x, axis=-1, keepdims=True) + EPSILON)


def add_and_norm(x, terms, gain, after=()):
    def body(xs, ts, gains, outs, _):
        middle = xs[0][...].astype(F32) + total_of(ts)
        outs[0][...] = middle
        outs[1][...] = (middle * inverse_rms(middle) * gains[0][...]).astype(BF)

    return kernel(
        "add_and_norm",
        body,
        [full([x]), full(terms), full([gain])],
        [shaped(x.shape, F32), shaped(x.shape)],
        path=True,
        after=after,
        vmem=16,
    )


def add_up(middle, terms, after=()):
    def body(xs, ts, outs, _):
        outs[0][...] = (xs[0][...] + total_of(ts)).astype(BF)

    return kernel(
        "add_up",
        body,
        [full([middle]), full(terms)],
        [shaped(middle.shape)],
        after=after,
        vmem=16,
        path=True,
    )[0]


def norm_back(x, terms, gain, straight, after=()):
    def body(xs, ts, gains, ss, outs, _):
        x = xs[0][...].astype(F32)
        grad = total_of(ts)
        scale = inverse_rms(x)
        unit = x * scale
        scaled = grad * gains[0][...]
        outs[0][...] = jnp.sum(grad * unit, axis=0, keepdims=True)
        mean = jnp.mean(scaled * unit, axis=-1, keepdims=True)
        total = ss[0][...].astype(F32) + scale * (scaled - unit * mean)
        outs[1][...] = total
        outs[2][...] = total.astype(BF)

    return kernel(
        "norm_back",
        body,
        [full([x]), full(terms), full([gain]), full([straight])],
        [shaped((1, x.shape[1]), F32), shaped(x.shape, F32), shaped(x.shape)],
        path=True,
        after=after,
        vmem=16,
    )


def behind(value, *others):
    return lax.optimization_barrier((value, *others))[0]


def strides(count):
    return [count * (k + 1) // 3 - count * k // 3 for k in range(3)]


class Gather:
    def __init__(self, mine):
        self.slots = [mine]
        self.others = [mate(mine, "section", 1)]
        self.parts = strides(lax.axis_size("row") - 1)

    def hop(self, *now):
        if now:
            self.slots[-1] = behind(self.slots[-1], *now)
        for _ in range(self.parts.pop(0)):
            self.slots.append(ring(self.slots[-1], -1))
            self.others.append(mate(self.slots[-1], "section", 1))
        return [self.slots[-1]]

    def all(self):
        return self.slots + self.others


class Scatter:
    def __init__(self, slots):
        self.slots = list(slots)
        self.moving = self.slots.pop()
        self.parts = strides(len(slots) - 1)

    def hop(self, *now):
        self.moving = behind(self.moving, *now)
        for _ in range(self.parts.pop(0)):
            got = ring(self.moving, 1).astype(F32)
            self.moving = (self.slots.pop().astype(F32) + got).astype(BF)
        return [self.moving]


def received(pieces):
    return [pieces[0]] + [mate(pieces[k], "col", k) for k in range(1, len(pieces))]


def feature_order(width, s):
    n = lax.axis_size("row")
    i = lax.axis_index("row")
    h = width // (2 * n)
    place = jnp.arange(width)
    part, block, inner = place // (n * h), (place // h) % n, place % h
    source = ((i + block) % n) * 2 * h + ((s + part) % 2) * h + inner
    return (place[:, None] == source[None, :]).astype(BF), (
        source[:, None] == place[None, :]
    ).astype(BF)


def swap_matrix(width, turned):
    source, place = jnp.arange(width)[:, None], jnp.arange(width)[None, :]
    first = (place % HEAD_SIZE) < HALF
    hit = jnp.where(first, source == place + HALF, source == place - HALF) & (place < turned)
    return jnp.where(hit, jnp.where(first, -1.0, 1.0), 0.0).astype(BF)


def token_tables(place, width_q, width_kv):
    power = -(jnp.arange(HALF, dtype=F32) * 2.0) / HEAD_SIZE
    angles = place.astype(F32)[:, None] * (ROPE_BASE**power)[None, :]
    lane = jnp.arange(2 * width_q)
    turned = lane < width_q + width_kv
    spread = (jnp.arange(HALF)[:, None] == (lane % HALF)[None, :]) & turned[None, :]
    rest = jnp.where(turned, 0.0, 1.0).astype(F32)[None, :]
    return spread_tables(jnp.cos(angles), jnp.sin(angles), spread.astype(BF), rest)


def spread_tables(cosine, sine, spread, rest):
    def body(ts, ms, rs, outs, _):
        for k in range(2):
            left, total = ts[k][...], jnp.zeros(outs[k].shape, F32)
            for _ in range(3):
                part = left.astype(BF)
                total = total + dot(part, ms[0][...])
                left = left - part.astype(F32)
            outs[k][...] = total + rs[0][...] if k == 0 else total

    shape = (cosine.shape[0], spread.shape[1])
    return kernel(
        "spread_tables",
        body,
        [full([cosine, sine]), full([spread]), full([rest])],
        [shaped(shape, F32)] * 2,
        vmem=16,
    )


def reduce_gains(gains):
    s = lax.axis_index("section")
    n = lax.axis_size("row")
    total = gains
    for k in range(1, lax.axis_size("col")):
        total = total + mate(gains, "col", k)
    h = gains.shape[1] // (2 * n)
    total = total.reshape(4, 2, n, h)
    first, second = total[:, 0], total[:, 1]
    total = jnp.concatenate(
        [jnp.where(s == 0, first, second), jnp.where(s == 0, second, first)], -1
    )
    here = total[:, 0]
    for k in range(1, n):
        here = here + ring(total[:, k], k)
    keep = jnp.where(s == 0, here[:2], here[2:])
    send = jnp.where(s == 0, here[2:], here[:2])
    return keep + mate(send, "section", 1)


def body(
    inputs,
    positions,
    w_query,
    key_weight,
    value_weight,
    w_out,
    w_gate,
    w_up,
    w_down,
    gain_attn,
    gain_ffn,
    cotangent,
):
    s = lax.axis_index("section")
    c = lax.axis_index("col")
    n = lax.axis_size("row")
    count = lax.axis_size("col")
    width_q, width_kv, units = w_query.shape[2], key_weight.shape[2], w_gate.shape[2]
    tokens, width = inputs.shape[1:]
    rows = tokens // count
    s_here, c_here = s.astype(jnp.int32)[None], c.astype(jnp.int32)[None]

    def start(parts, after):
        keep, send = pack([p[0] for p in parts], s_here, after)
        got = mate(send, "section", 1)
        return [jnp.where(s == layer, keep, got) for layer in range(2)]

    attn_start = start((w_query, key_weight, value_weight, w_out), [])
    first = attn_start[0]
    a = Gather(first)
    come = a.hop()
    ffn_start = start((w_gate, w_up, w_down), [first])
    f = Gather(ffn_start[0])

    gains = behind(jnp.concatenate([gain_attn, gain_ffn], 0), first)
    pair = mate(gains, "section", 1)
    gains = jnp.concatenate([jnp.where(s == 0, gains, pair), jnp.where(s == 0, pair, gains)], 0)
    gains = jnp.stack([gains] + [ring(gains, -k) for k in range(1, n)], 1)
    gains = gains.reshape(4, n, 2, -1)
    gains = jnp.where(s == 0, gains, gains[:, :, ::-1]).transpose(0, 2, 1, 3).reshape(4, 1, -1)
    gains = gains.astype(F32)

    inputs, positions = behind(inputs, first), behind(positions, *come)
    order, back_order = feature_order(width, behind(s, *come))
    swaps = [swap_matrix(width_q, width_q), swap_matrix(width_q, width_kv)]
    x = lax.dynamic_index_in_dim(inputs, s, 0, keepdims=False)
    place = lax.dynamic_index_in_dim(positions, s, 0, keepdims=False)
    cot = lax.dynamic_index_in_dim(cotangent, s, 0, keepdims=False)
    piece = jnp.arange(count) ^ c
    token = (piece[:, None] * rows + jnp.arange(rows)[None, :]).reshape(-1)
    place = jnp.concatenate(
        [lax.dynamic_slice_in_dim(place, (c ^ k) * rows, rows) for k in range(count)]
    )
    tables = token_tables(place, width_q, width_kv)
    parity = lax.axis_index("row") % 2

    def order_of(side):
        half = tokens // 2
        return token + jnp.where(side == 0, jnp.where(token < half, 0, 2 * half), half)

    own_order = order_of(parity)
    orders = [own_order[None, :], jnp.concatenate([own_order, order_of(1 - parity)])[:, None]]

    point = meet(come)
    come = f.hop(*come)
    x = enter(x, order, c_here, count, a.hop() + come + point, True)
    a.hop()
    grad = enter(cot, order, c_here, count)

    kept, outs, gathers = [], [], []
    for layer in range(2):
        gain1, gain2 = gains[2 * layer], gains[2 * layer + 1]
        last = layer == 1
        gathers.append((a, f))
        come = meet(x[1:] + a.slots[-1:] + grad[:1]) if last else []
        n1, query, own = project(x, gain1, a.all(), tables, swaps, width_q, come)
        there = mate(own, "row", 1)
        come = f.hop(there)
        mixed, sums, y = attention(query, own, there, orders, a.all(), count)
        sent = received(y)
        f.hop(sent[-1])
        if not last:
            a, f_old = Gather(attn_start[1]), f
            a.hop(sent[-1])
        middle, n2 = add_and_norm(x[0], sent, gain2, come)
        n2 = gather_pieces(n2)
        point = meet(n2[1:] + f.slots[-1:] + a.slots[-1:])
        if not last:
            f = Gather(ffn_start[1])
            come = f.hop(n2[-1]) + a.hop(n2[-1])
        gate, up, hidden, y = feed_forward(n2, gathers[-1][1].all(), point)
        kept.append((x[0], n1, query, own, there, mixed, sums, middle, n2, gate, up, hidden))
        if not last:
            sent = received(y)
            a.hop(sent[-1])
            x = gather_pieces(add_up(middle, sent, come))
            outs.append(x)

    def to_owner(value, layer):
        return lax.ppermute(value, "section", [(1 - layer, layer)])

    left, parts, gain_parts = [None, None], [None, None], [None, None]
    last_y, s_a, come = y, None, []
    for layer in (1, 0):
        a, f = gathers[layer]
        x, n1, query, own, there, mixed, sums, middle, n2, gate, up, hidden = kept[layer]
        gain1, gain2 = gains[2 * layer], gains[2 * layer + 1]
        grad_gu, y = feed_forward_back(grad, gate, up, f.all(), come)
        come = s_a.hop(grad[-1]) if s_a else []
        sent = received(y)
        down, rest = [(grad, behind(hidden, grad_gu))], [(n2, grad_gu)]
        got = mate(weight_grads(down, 1, units // 2), "section", 1)
        s_d = Scatter(weight_grads(down, 0, units // 2, got))
        other = weight_grads(rest, 1, units // 2)
        got = mate(other, "section", 1)
        come += [s_d.moving, other]
        g_gain2, grad_middle, grad_attn = norm_back(middle, sent, gain2, grad[0], come)
        come = s_d.hop(sent[-1]) + (s_a.hop(sent[-1]) if s_a else [])
        s_f = Scatter(weight_grads(rest, 0, units // 2, behind(got, grad_attn)))
        grad_attn = gather_pieces(grad_attn)
        grad_query, grad_own, grad_there = attention_back(
            grad_attn, query, own, there, sums, orders, a.all(), come + [s_f.moving]
        )
        come = s_f.hop(grad_attn[-1])
        if layer == 1:
            last_y = received([behind(p, grad_attn[-1]) for p in last_y])
            left[0] = leave([behind(p, grad_there) for p in outs[0]], back_order, c_here)
            come += last_y[1:] + [left[0]]
        else:
            last_y = add_up(kept[1][7], last_y)
            outs.append(gather_pieces(behind(last_y, grad_attn[-1])))
            left[1] = leave([behind(p, grad_there) for p in grad], back_order, c_here)
            come += outs[1][1:] + [left[1]]
        back = mate(grad_there, "row", 1)
        y, grad_qkv = project_back(
            grad_query, grad_own, back, a.all(), tables, swaps, count, come
        )
        come = s_f.hop(back) + (s_a.hop(back) if s_a else s_d.hop(back))
        sent = received(y)
        terms = [([n1], grad_qkv), (grad_attn, mixed)]
        other = weight_grads(terms, 1, width_q)
        got = mate(other, "section", 1)
        mine = weight_grads(terms, 0, width_q, got)
        came = come + list(mine[:1] if layer == 0 else [other])
        g_gain1, _, grad = norm_back(x, sent, gain1, grad_middle, came)
        come = s_f.hop(sent[-1]) + s_d.hop(sent[-1])
        s_a = Scatter(mine)
        grad = gather_pieces(grad)
        if layer == 1:
            come += [s_a.moving]
        parts[layer] = (s_a, s_f, s_d)
        gain_parts[layer] = (g_gain1, g_gain2)

    come += s_a.hop(sent[-1])
    acts = [left[0], leave([behind(p, g_gain1) for p in outs[1]], back_order, c_here)]
    point = meet(grad[1:] + acts[1:])
    grads = [leave([behind(p, *point) for p in grad], back_order, c_here), left[1]]
    grads_there = [to_owner(v, k) for k, v in enumerate(grads)]
    acts_there = [to_owner(behind(v, *point), k) for k, v in enumerate(acts)]
    gain_grads = jnp.concatenate(list(gain_parts[0]) + list(gain_parts[1]), 0)
    gain_grads = reduce_gains(behind(gain_grads, *point))
    come = s_d.hop(*come) + s_a.hop(*come)
    point = meet(come + grads_there + acts_there)
    s_a.hop(*come)
    acts = place_out(acts, acts_there, s_here, point)
    grads = place_out(grads, grads_there, s_here, point)

    def owned(k, widths):
        values = [behind(p[k].moving, *come) if k else p[k].moving for p in parts]
        return unpack(values, [to_owner(v, layer) for layer, v in enumerate(values)], s_here, widths)

    (g_down,) = owned(2, (units,))
    g_gate, g_up = owned(1, (units, units))
    g_query, g_key, g_value, g_out = owned(0, (width_q, width_kv, width_kv, width_q))
    return (
        acts[None],
        grads[None],
        *[g[None] for g in (g_query, g_key, g_value, g_out, g_gate, g_up, g_down)],
        gain_grads[0:1],
        gain_grads[1:2],
    )


def solution(mesh):
    placed = (
        P(None, "row", None),
        P(None, "row"),
        *[P("section", "row", "col")] * 7,
        *[P("section", "row")] * 2,
        P(None, "row", None),
    )
    return jax.shard_map(
        body,
        mesh=mesh,
        in_specs=placed,
        out_specs=(
            *[P("section", None, "row", None)] * 2,
            *[P("section", "row", "col")] * 7,
            *[P("section", "row")] * 2,
        ),
        check_vma=False,
    )
```

time: 863 us -> 702 us (0.81)
  waiting for transfers between devices: 500 us -> 288 us
  Pallas kernels: 0 us -> 173 us
  matrix products: 81.1 us -> 0 us
  other arithmetic: 74 us -> 35.2 us
  local copies, waits for them, and re-layouts: 74.6 us -> 45.4 us
  starting transfers between devices: 122 us -> 151 us
    ppermute x27 -> x36, waiting for transfers between devices: 320 us -> 127 us  [ring(): return lax.ppermute(x, 'row', [(j, (j + by) % n) for j in range(n)])]
    pallas_call x0 -> x51, Pallas kernels: none -> 173 us  [kernel(): pl.pallas_call(run, grid=grid, in_specs=specs, out_specs=[spec for _, spe...]
    dot_general x54 -> x0, matrix products: 81.1 us -> none  [the longest x14 25.7 us: dot(): return jnp.dot(left, right, preferred_element_type=F32)]
    ppermute x0 -> x10, starting transfers between devices: none -> 24.4 us  [to_owner(): return lax.ppermute(value, 'section', [(1 - layer, layer)])]
    slice x42 -> x3, local copies, waits for them, and re-layouts: 24 us -> 1.18 us  [the longest x1 0.61 us: body(): gain1, gain2 = (gains[2 * layer], gains[2 * layer + 1])]
    ppermute x82 -> x81, waiting for transfers between devices: 180 us -> 160 us  [mate(): return lax.ppermute(x, axis, [(j, j ^ k) for j in range(n)])]
    convert_element_type x19 -> x23, other arithmetic: 12.1 us -> 27.5 us  [the longest x18 22.1 us: hop(): self.moving = (self.slots.pop().astype(F32) + got).astype(BF)]
    add x9 -> x5, other arithmetic: 11.6 us -> 0.26 us  [the longest x2 0.09 us: order_of(): token + jnp.where(side == 0, jnp.where(token < half, 0, 2 * half), half)]
  transfers between devices with their start and end apart: 109 -> 127, of which waited for: 53 -> 50; matrix products, arithmetic and copies ran while one was open for 20% -> 6% of each run, Pallas kernels for 0% -> 18%
where the time goes in v2:
time: 702 us; the launch traced here: 696 us
  waiting for transfers between devices  288 us (41%)
  Pallas kernels  173 us (25%)
  starting transfers between devices  151 us (22%)
  local copies, waits for them, and re-layouts  45.4 us (6%)
  other arithmetic  35.2 us (5%)
    pallas_call x51, Pallas kernels, kernel(): pl.pallas_call(run, grid=grid, in_specs=specs, out_specs=[spec for _, spe...  173 us
    ppermute x81, waiting for transfers between devices, mate(): return lax.ppermute(x, axis, [(j, j ^ k) for j in range(n)])  160 us
    ppermute x36, waiting for transfers between devices, ring(): return lax.ppermute(x, 'row', [(j, (j + by) % n) for j in range(n)])  127 us
    ppermute x81, starting transfers between devices, mate(): return lax.ppermute(x, axis, [(j, j ^ k) for j in range(n)])  68.7 us
    ppermute x36, starting transfers between devices, ring(): return lax.ppermute(x, 'row', [(j, (j + by) % n) for j in range(n)])  57.4 us
    unnamed x332, local copies, waits for them, and re-layouts  39 us
    ppermute x10, starting transfers between devices, to_owner(): return lax.ppermute(value, 'section', [(1 - layer, layer)])  24.4 us
    convert_element_type x18, other arithmetic, hop(): self.moving = (self.slots.pop().astype(F32) + got).astype(BF)  22.1 us
  transfers between devices with their start and end apart: 127, of which 50 were waited for; matrix products, arithmetic and copies ran while one was open for 6% of the time, Pallas kernels for 18%

profile of v2, /device:TPU:0, one launch (start us, length us, event | category | flops | bytes accessed | tf_op | source)
XLA Modules:
  0.0 695.9 jit_solution(1409387131850010796)
XLA Ops:
  52.5 26.1 %collective-permute-done.9.refs_8_.refs_13_.refs_6_ = bf16[192,1152]{1,0:T(8,128)(2,1)} collective-permute-done((bf16[192,1152]{1,0:T(8,128)(2,1)}, bf16[192,1152]{1,0:T(8,128)(2,1)}, u32[]{:S(2)}, u32[]{:S(2)}) %collective-permute-start.9) | collective-permute-done | bytes 442400 | tf_op jit(solution)/shard_map/ppermute | solution.py:32
  87.5 9.9 %collective-permute-done.14.refs_2_.refs_6_ = bf16[512,384]{1,0:T(8,128)(2,1)S(1)} collective-permute-done((bf16[512,384]{1,0:T(8,128)(2,1)S(1)}, bf16[512,384]{1,0:T(8,128)(2,1)S(1)}, u32[]{:S(2)}, u32[]{:S(2)}) %collective-permute-start.14) | collective-permute-done | bytes 393248 | tf_op jit(solution)/shard_map/ppermute | solution.py:27
  102.0 7.6 %attention.2 = (bf16[512,384]{1,0:T(8,128)(2,1)S(1)}, f32[4,512]{1,0:T(4,128)S(1)}, bf16[128,1536]{1,0:T(8,128)(2,1)S(1)}, bf16[128,1536]{1,0:T(8,128)(2,1)}, bf...) custom-call(bf16[512,384]{1,0:T(8,128)(2,1)S(1)} %get-tuple-element.205.refs_0_.refs_4_, ...), custom_call_target="tpu_custom_call" | custom-call | flops 199999995904 | bytes 6699008 | tf_op jit(solution)/shard_map/attention/pallas_call | solution.py:77
  114.0 9.6 %collective-permute-done.17.refs_4_ = bf16[128,1536]{1,0:T(8,128)(2,1)S(1)} collective-permute-done((bf16[128,1536]{1,0:T(8,128)(2,1)}, bf16[128,1536]{1,0:T(8,128)(2,1)S(1)}, u32[]{:S(2)}, u32[]{:S(2)}) %collective-permute-start.17) | collective-permute-done | bytes 393248 | tf_op jit(solution)/shard_map/ppermute | solution.py:27
  143.4 9.5 %collective-permute-done.21.refs_2_.refs_3_ = bf16[128,1536]{1,0:T(8,128)(2,1)S(1)} collective-permute-done((bf16[128,1536]{1,0:T(8,128)(2,1)S(1)}, bf16[128,1536]{1,0:T(8,128)(2,1)S(1)}, u32[]{:S(2)}, u32[]{:S(2)}) %collective-permute-start.21) | collective-permute-done | bytes 393248 | tf_op jit(solution)/shard_map/ppermute | solution.py:27
  158.0 5.4 collective-permute-done.22.refs_3_.refs_7_.refs_9_
  168.8 7.8 %feed_forward.2 = (bf16[512,1024]{1,0:T(8,128)(2,1)S(1)}, bf16[512,1024]{1,0:T(8,128)(2,1)S(1)}, bf16[512,1024]{1,0:T(8,128)(2,1)S(1)}, bf16[128,1536]{1,0:T(8,1...) custom-call(bf16[128,1536]{1,0:T(8,128)(2,1)S(1)} %copy-done.34, ...), custom_call_target="tpu_custom_call" | custom-call | flops 199999995904 | bytes 15728640 | tf_op jit(solution)/shard_map/feed_forward/pallas_call | solution.py:77
  180.2 9.4 %collective-permute-done.30.refs_4_ = bf16[128,1536]{1,0:T(8,128)(2,1)S(1)} collective-permute-done((bf16[128,1536]{1,0:T(8,128)(2,1)S(1)}, bf16[128,1536]{1,0:T(8,128)(2,1)S(1)}, u32[]{:S(2)}, u32[]{:S(2)}) %collective-permute-start.30) | collective-permute-done | bytes 393248 | tf_op jit(solution)/shard_map/ppermute | solution.py:27
  212.6 6.5 collective-permute-done.34.refs_1_.refs_2_
  221.9 5.9 project.3
  227.9 11.1 %collective-permute-done.41.refs_2_.refs_6_ = bf16[512,384]{1,0:T(8,128)(2,1)S(1)} collective-permute-done((bf16[512,384]{1,0:T(8,128)(2,1)S(1)}, bf16[512,384]{1,0:T(8,128)(2,1)S(1)}, u32[]{:S(2)}, u32[]{:S(2)}) %collective-permute-start.41) | collective-permute-done | bytes 393248 | tf_op jit(solution)/shard_map/ppermute | solution.py:27
  242.1 6.7 attention.3
  255.8 8.4 %collective-permute-done.44.refs_4_ = bf16[128,1536]{1,0:T(8,128)(2,1)} collective-permute-done((bf16[128,1536]{1,0:T(8,128)(2,1)}, bf16[128,1536]{1,0:T(8,128)(2,1)}, u32[]{:S(2)}, u32[]{:S(2)}) %collective-permute-start.44) | collective-permute-done | bytes 393248 | tf_op jit(solution)/shard_map/ppermute | solution.py:27
  278.5 9.5 %collective-permute-done.48.refs_2_.refs_3_ = bf16[128,1536]{1,0:T(8,128)(2,1)S(1)} collective-permute-done((bf16[128,1536]{1,0:T(8,128)(2,1)S(1)}, bf16[128,1536]{1,0:T(8,128)(2,1)S(1)}, u32[]{:S(2)}, u32[]{:S(2)}) %collective-permute-start.48) | collective-permute-done | bytes 393248 | tf_op jit(solution)/shard_map/ppermute | solution.py:27
  288.0 6.5 collective-permute-done.47.refs_1_.refs_2_
  300.4 7.9 %feed_forward.3 = (bf16[512,1024]{1,0:T(8,128)(2,1)S(1)}, bf16[512,1024]{1,0:T(8,128)(2,1)S(1)}, bf16[512,1024]{1,0:T(8,128)(2,1)S(1)}, bf16[128,1536]{1,0:T(8,1...) custom-call(bf16[128,1536]{1,0:T(8,128)(2,1)S(1)} %copy-done.47, ...), custom_call_target="tpu_custom_call" | custom-call | flops 199999995904 | bytes 15728640 | tf_op jit(solution)/shard_map/feed_forward/pallas_call | solution.py:77
  308.3 7.9 %feed_forward_back.2 = (bf16[512,2048]{1,0:T(8,128)(2,1)S(1)}, bf16[128,1536]{1,0:T(8,128)(2,1)S(1)}, bf16[128,1536]{1,0:T(8,128)(2,1)S(1)}, bf16[128,1536]{1,0:T(8,128)(2,1)S(1)}, bf16[128,1536]{1,0:T(8,128)(2,1)S(1)}) custom-call(bf16[128,1536]{1,0:T(8,128)(2,1)S(1)} %copy-done.23, bf16[128,1536]{1,0:T(8,128)(2,1)S(1)} %copy-done.25, ...), custom_call_target="tpu_custom_call" | custom-call | flops 199999995904 | bytes 16777216 | tf_op jit(solution)/shard_map/feed_forward_back/pallas_call | solution.py:77
  331.4 7.9 %collective-permute-done.54.refs_2_ = bf16[128,1536]{1,0:T(8,128)(2,1)S(1)} collective-permute-done((bf16[128,1536]{1,0:T(8,128)(2,1)S(1)}, bf16[128,1536]{1,0:T(8,128)(2,1)S(1)}, u32[]{:S(2)}, u32[]{:S(2)}) %collective-permute-start.54) | collective-permute-done | bytes 393248 | tf_op jit(solution)/shard_map/ppermute | solution.py:27
  345.6 5.5 weight_grads.15
  353.1 7.4 %collective-permute-done.59.refs_2_.refs_4_ = bf16[128,1536]{1,0:T(8,128)(2,1)S(1)} collective-permute-done((bf16[128,1536]{1,0:T(8,128)(2,1)S(1)}, bf16[128,1536]{1,0:T(8,128)(2,1)S(1)}, u32[]{:S(2)}, u32[]{:S(2)}) %collective-permute-start.59) | collective-permute-done | bytes 393248 | tf_op jit(solution)/shard_map/ppermute | solution.py:27
  360.7 9.0 %attention_back.2 = (f32[512,384]{1,0:T(8,128)S(1)}, f32[512,384]{1,0:T(8,128)S(1)}, bf16[512,384]{1,0:T(8,128)(2,1)S(1)}) custom-call(bf16[128,1536]{1,0:T(8,128)(2,1)S(1)} %get-tuple-element.247.refs_0_.refs_2_, bf16[128,1536]{1,0:T(8,128)(2,1)S(1)} %collective-permute-done.58.refs_1_.refs_3_, ...), custom_call_target="tpu_custom_call" | custom-call | flops 199999995904 | bytes 8271872 | tf_op jit(solution)/shard_map/attention_back/pallas_call | solution.py:77
  423.4 12.7 %collective-permute-done.76 = bf16[192,2048]{1,0:T(8,128)(2,1)} collective-permute-done((bf16[192,2048]{1,0:T(8,128)(2,1)}, bf16[192,2048]{1,0:T(8,128)(2,1)}, u32[]{:S(2)}, u32[]{:S(2)}) %collective-permute-start.76) | collective-permute-done | bytes 786464 | tf_op jit(solution)/shard_map/ppermute | solution.py:32
  442.7 8.0 %feed_forward_back.3 = (bf16[512,2048]{1,0:T(8,128)(2,1)S(1)}, bf16[128,1536]{1,0:T(8,128)(2,1)S(1)}, bf16[128,1536]{1,0:T(8,128)(2,1)S(1)}, bf16[128,1536]{1,0:T(8,128)(2,1)S(1)}, bf16[128,1536]{1,0:T(8,128)(2,1)S(1)}) custom-call(bf16[128,1536]{1,0:T(8,128)(2,1)S(1)} %get-tuple-element.314.refs_0_.refs_6_, ...), custom_call_target="tpu_custom_call" | custom-call | flops 199999995904 | bytes 16777216 | tf_op jit(solution)/shard_map/feed_forward_back/pallas_call | solution.py:77
  464.7 11.2 %collective-permute-done.81.refs_4_ = bf16[128,1536]{1,0:T(8,128)(2,1)S(1)} collective-permute-done((bf16[128,1536]{1,0:T(8,128)(2,1)S(1)}, bf16[128,1536]{1,0:T(8,128)(2,1)S(1)}, u32[]{:S(2)}, u32[]{:S(2)}) %collective-permute-start.81) | collective-permute-done | bytes 393248 | tf_op jit(solution)/shard_map/ppermute | solution.py:27
  484.2 5.8 collective-permute-done.88
  491.1 9.5 %collective-permute-done.84.refs_3_.refs_5_ = bf16[128,1536]{1,0:T(8,128)(2,1)S(1)} collective-permute-done((bf16[128,1536]{1,0:T(8,128)(2,1)S(1)}, bf16[128,1536]{1,0:T(8,128)(2,1)S(1)}, u32[]{:S(2)}, u32[]{:S(2)}) %collective-permute-start.84) | collective-permute-done | bytes 393248 | tf_op jit(solution)/shard_map/ppermute | solution.py:27
  512.0 9.0 %attention_back.3 = (f32[512,384]{1,0:T(8,128)S(1)}, f32[512,384]{1,0:T(8,128)S(1)}, bf16[512,384]{1,0:T(8,128)(2,1)S(1)}) custom-call(bf16[128,1536]{1,0:T(8,128)(2,1)S(1)} %get-tuple-element.300.refs_0_.refs_2_, bf16[128,1536]{1,0:T(8,128)(2,1)S(1)} %collective-permute-done.85.refs_1_.refs_3_, ...), custom_call_target="tpu_custom_call" | custom-call | flops 199999995904 | bytes 8271872 | tf_op jit(solution)/shard_map/attention_back/pallas_call | solution.py:77
  548.4 11.6 %collective-permute-done.99 = bf16[192,1152]{1,0:T(8,128)(2,1)S(1)} collective-permute-done((bf16[192,1152]{1,0:T(8,128)(2,1)S(1)}, bf16[192,1152]{1,0:T(8,128)(2,1)S(1)}, u32[]{:S(2)}, u32[]{:S(2)}) %collective-permute-start.99) | collective-permute-done | bytes 442400 | tf_op jit(solution)/shard_map/ppermute | solution.py:32
  562.3 8.8 %collective-permute-done.97.refs_4_ = bf16[128,1536]{1,0:T(8,128)(2,1)S(1)} collective-permute-done((bf16[128,1536]{1,0:T(8,128)(2,1)S(1)}, bf16[128,1536]{1,0:T(8,128)(2,1)S(1)}, u32[]{:S(2)}, u32[]{:S(2)}) %collective-permute-start.97) | collective-permute-done | bytes 393248 | tf_op jit(solution)/shard_map/ppermute | solution.py:27
  609.6 12.8 %collective-permute-done.108 = bf16[192,1152]{1,0:T(8,128)(2,1)S(1)} collective-permute-done((bf16[192,1152]{1,0:T(8,128)(2,1)}, bf16[192,1152]{1,0:T(8,128)(2,1)S(1)}, u32[]{:S(2)}, u32[]{:S(2)}) %collective-permute-start.108) | collective-permute-done | bytes 442400 | tf_op jit(solution)/shard_map/ppermute | solution.py:32
  628.9 7.6 %collective-permute-done.109 = bf16[192,1024]{1,0:T(8,128)(2,1)S(1)} collective-permute-done((bf16[192,1024]{1,0:T(8,128)(2,1)S(1)}, bf16[192,1024]{1,0:T(8,128)(2,1)S(1)}, u32[]{:S(2)}, u32[]{:S(2)}) %collective-permute-start.109) | collective-permute-done | bytes 393248 | tf_op jit(solution)/shard_map/ppermute | solution.py:32
  636.7 6.8 collective-permute-done.110
  (672 shorter events, 403.2 us)
Async XLA Ops:
  13.3 68.0 %collective-permute-start.10 = (bf16[192,1152]{1,0:T(8,128)(2,1)}, bf16[192,1152]{1,0:T(8,128)(2,1)}, u32[]{:S(2)}, u32[]{:S(2)}) collective-permute-start(bf16[192,1152]{1,0:T(8,128)(2,1)} %get-tuple-element.405.refs_4_.refs_5_.refs_10_.refs_3_), channel_id=1, source_target_pairs={{0,16},{16,0},{1,17},{17,1},{2,18},{18,2},{3,19},{19,3},{4,20},{20... | collective-permute-start | bytes 1327112 | tf_op jit(solution)/shard_map/ppermute | solution.py:27
  37.0 41.6 %collective-permute-start.4 = (bf16[192,3072]{1,0:T(8,128)(2,1)}, bf16[192,3072]{1,0:T(8,128)(2,1)}, u32[]{:S(2)}, u32[]{:S(2)}) collective-permute-start(bf16[192,3072]{1,0:T(8,128)(2,1)} %get-tuple-element.196.refs_4_.refs_6_), channel_id=1, source_target_pairs={{0,12},{4,0},{8,4},{12,8},{1,13},{5,1},{9,5},{13,9},{2,14},{6,2},{... | collective-permute-start | bytes 3538952 | tf_op jit(solution)/shard_map/ppermute | solution.py:32
  45.0 33.6 %collective-permute-start.9 = (bf16[192,1152]{1,0:T(8,128)(2,1)}, bf16[192,1152]{1,0:T(8,128)(2,1)}, u32[]{:S(2)}, u32[]{:S(2)}) collective-permute-start(bf16[192,1152]{1,0:T(8,128)(2,1)} %collective-permute-done.2.refs_3_.refs_7_.refs_12_.refs_5_), channel_id=1, source_target_pairs={{0,12},{4,0},{8,4},{12,8},{1,13},{5,1},{9,5},{13,9},{2,14},{6,2},{... | collective-permute-start | bytes 1327112 | tf_op jit(solution)/shard_map/ppermute | solution.py:32
  51.9 29.3 %collective-permute-start.11 = (bf16[192,1152]{1,0:T(8,128)(2,1)}, bf16[192,1152]{1,0:T(8,128)(2,1)}, u32[]{:S(2)}, u32[]{:S(2)}) collective-permute-start(bf16[192,1152]{1,0:T(8,128)(2,1)} %collective-permute-done.1.refs_0_.refs_6_.refs_11_.refs_4_), channel_id=1, source_target_pairs={{0,16},{16,0},{1,17},{17,1},{2,18},{18,2},{3,19},{19,3},{4,20},{20... | collective-permute-start | bytes 1327112 | tf_op jit(solution)/shard_map/ppermute | solution.py:27
  52.0 29.3 %collective-permute-start.12 = (bf16[192,1152]{1,0:T(8,128)(2,1)}, bf16[192,1152]{1,0:T(8,128)(2,1)}, u32[]{:S(2)}, u32[]{:S(2)}) collective-permute-start(bf16[192,1152]{1,0:T(8,128)(2,1)} %collective-permute-done.2.refs_3_.refs_7_.refs_12_.refs_5_), channel_id=1, source_target_pairs={{0,16},{16,0},{1,17},{17,1},{2,18},{18,2},{3,19},{19,3},{4,20},{20... | collective-permute-start | bytes 1327112 | tf_op jit(solution)/shard_map/ppermute | solution.py:27
  97.5 31.2 %collective-permute-start.18 = (bf16[192,3072]{1,0:T(8,128)(2,1)}, bf16[192,3072]{1,0:T(8,128)(2,1)}, u32[]{:S(2)}, u32[]{:S(2)}) collective-permute-start(bf16[192,3072]{1,0:T(8,128)(2,1)} %collective-permute-done.4.refs_4_.refs_5_.refs_7_), channel_id=1, source_target_pairs={{0,12},{4,0},{8,4},{12,8},{1,13},{5,1},{9,5},{13,9},{2,14},{6,2},{... | collective-permute-start | bytes 3538952 | tf_op jit(solution)/shard_map/ppermute | solution.py:32
  124.4 28.5 %collective-permute-start.27 = (bf16[192,1152]{1,0:T(8,128)(2,1)}, bf16[192,1152]{1,0:T(8,128)(2,1)}, u32[]{:S(2)}, u32[]{:S(2)}) collective-permute-start(bf16[192,1152]{1,0:T(8,128)(2,1)} %get-tuple-element.215.refs_5_.refs_10_.refs_3_), channel_id=1, source_target_pairs={{0,12},{4,0},{8,4},{12,8},{1,13},{5,1},{9,5},{13,9},{2,14},{6,2},{... | collective-permute-start | bytes 1327112 | tf_op jit(solution)/shard_map/ppermute | solution.py:32
  128.7 34.8 %collective-permute-start.22 = (bf16[192,3072]{1,0:T(8,128)(2,1)}, bf16[192,3072]{1,0:T(8,128)(2,1)}, u32[]{:S(2)}, u32[]{:S(2)}) collective-permute-start(bf16[192,3072]{1,0:T(8,128)(2,1)} %collective-permute-done.18.refs_6_.refs_8_), channel_id=1, source_target_pairs={{0,12},{4,0},{8,4},{12,8},{1,13},{5,1},{9,5},{13,9},{2,14},{6,2},{... | collective-permute-start | bytes 3538952 | tf_op jit(solution)/shard_map/ppermute | solution.py:32
  163.4 34.7 %collective-permute-start.31 = (bf16[192,3072]{1,0:T(8,128)(2,1)}, bf16[192,3072]{1,0:T(8,128)(2,1)}, u32[]{:S(2)}, u32[]{:S(2)}) collective-permute-start(bf16[192,3072]{1,0:T(8,128)(2,1)} %get-tuple-element.220.refs_4_.refs_6_), channel_id=1, source_target_pairs={{0,12},{4,0},{8,4},{12,8},{1,13},{5,1},{9,5},{13,9},{2,14},{6,2},{... | collective-permute-start | bytes 3538952 | tf_op jit(solution)/shard_map/ppermute | solution.py:32
  189.6 29.5 %collective-permute-start.36 = (bf16[192,1152]{1,0:T(8,128)(2,1)}, bf16[192,1152]{1,0:T(8,128)(2,1)}, u32[]{:S(2)}, u32[]{:S(2)}) collective-permute-start(bf16[192,1152]{1,0:T(8,128)(2,1)} %collective-permute-done.32.refs_6_.refs_7_.refs_12_.refs_5_), channel_id=1, source_target_pairs={{0,12},{4,0},{8,4},{12,8},{1,13},{5,1},{9,5},{13,9},{2,14},{6,2},{... | collective-permute-start | bytes 1327112 | tf_op jit(solution)/shard_map/ppermute | solution.py:32
  239.1 28.0 %collective-permute-start.45 = (bf16[192,3072]{1,0:T(8,128)(2,1)}, bf16[192,3072]{1,0:T(8,128)(2,1)}, u32[]{:S(2)}, u32[]{:S(2)}) collective-permute-start(bf16[192,3072]{1,0:T(8,128)(2,1)} %collective-permute-done.31.refs_5_.refs_7_), channel_id=1, source_target_pairs={{0,12},{4,0},{8,4},{12,8},{1,13},{5,1},{9,5},{13,9},{2,14},{6,2},{... | collective-permute-start | bytes 3538952 | tf_op jit(solution)/shard_map/ppermute | solution.py:32
  267.1 28.5 %collective-permute-start.49 = (bf16[192,3072]{1,0:T(8,128)(2,1)}, bf16[192,3072]{1,0:T(8,128)(2,1)}, u32[]{:S(2)}, u32[]{:S(2)}) collective-permute-start(bf16[192,3072]{1,0:T(8,128)(2,1)} %collective-permute-done.45.refs_6_.refs_8_), channel_id=1, source_target_pairs={{0,12},{4,0},{8,4},{12,8},{1,13},{5,1},{9,5},{13,9},{2,14},{6,2},{... | collective-permute-start | bytes 3538952 | tf_op jit(solution)/shard_map/ppermute | solution.py:32
  353.1 28.7 %collective-permute-start.67 = (bf16[192,2048]{1,0:T(8,128)(2,1)}, bf16[192,2048]{1,0:T(8,128)(2,1)}, u32[]{:S(2)}, u32[]{:S(2)}) collective-permute-start(bf16[192,2048]{1,0:T(8,128)(2,1)} %get-tuple-element.269.refs_19_), channel_id=1, source_target_pairs={{0,4},{4,8},{8,12},{12,0},{1,5},{5,9},{9,13},{13,1},{2,6},{6,10},{... | collective-permute-start | bytes 2359304 | tf_op jit(solution)/shard_map/ppermute | solution.py:32
  384.1 28.2 %collective-permute-start.71 = (bf16[192,2048]{1,0:T(8,128)(2,1)}, bf16[192,2048]{1,0:T(8,128)(2,1)}, u32[]{:S(2)}, u32[]{:S(2)}) collective-permute-start(bf16[192,2048]{1,0:T(8,128)(2,1)} %add_convert_fusion.5.refs_15_), channel_id=1, source_target_pairs={{0,4},{4,8},{8,12},{12,0},{1,5},{5,9},{9,13},{13,1},{2,6},{6,10},{... | collective-permute-start | bytes 2359304 | tf_op jit(solution)/shard_map/ppermute | solution.py:32
  401.6 36.0 %collective-permute-start.78 = (bf16[768,1152]{1,0:T(8,128)(2,1)}, bf16[768,1152]{1,0:T(8,128)(2,1)}, u32[]{:S(2)}, u32[]{:S(2)}) collective-permute-start(bf16[768,1152]{1,0:T(8,128)(2,1)} %weight_grads.16.refs_9_), channel_id=1, source_target_pairs={{0,16},{16,0},{1,17},{17,1},{2,18},{18,2},{3,19},{19,3},{4,20},{20... | collective-permute-start | bytes 5308424 | tf_op jit(solution)/shard_map/ppermute | solution.py:27
  417.2 25.5 %collective-permute-start.75 = (bf16[128,1536]{1,0:T(8,128)(2,1)S(1)}, bf16[128,1536]{1,0:T(8,128)(2,1)S(1)}, u32[]{:S(2)}, u32[]{:S(2)}) collective-permute-start(bf16[128,1536]{1,0:T(8,128)(2,1)S(1)} %get-tuple-element.314.refs_0_.refs_6_), channel_id=1, source_target_pairs={{0,3},{1,2},{2,1},{3,0},{4,7},{5,6},{6,5},{7,4},{8,11},{9,10},{10,... | collective-permute-start | bytes 1179656 | tf_op jit(solution)/shard_map/ppermute | solution.py:27
  454.6 25.2 %collective-permute-start.79 = (bf16[128,1536]{1,0:T(8,128)(2,1)S(1)}, bf16[128,1536]{1,0:T(8,128)(2,1)S(1)}, u32[]{:S(2)}, u32[]{:S(2)}) collective-permute-start(bf16[128,1536]{1,0:T(8,128)(2,1)S(1)} %get-tuple-element.291), channel_id=1, source_target_pairs={{0,1},{1,0},{2,3},{3,2},{4,5},{5,4},{6,7},{7,6},{8,9},{9,8},{10,11... | collective-permute-start | bytes 1179656 | tf_op jit(solution)/shard_map/ppermute | solution.py:27
  462.9 41.0 %collective-permute-start.89 = (bf16[768,2048]{1,0:T(8,128)(2,1)}, bf16[768,2048]{1,0:T(8,128)(2,1)}, u32[]{:S(2)}, u32[]{:S(2)}) collective-permute-start(bf16[768,2048]{1,0:T(8,128)(2,1)} %weight_grads.20.refs_9_), channel_id=1, source_target_pairs={{0,16},{16,0},{1,17},{17,1},{2,18},{18,2},{3,19},{19,3},{4,20},{20... | collective-permute-start | bytes 9437192 | tf_op jit(solution)/shard_map/ppermute | solution.py:27
  480.6 29.9 %collective-permute-start.86 = (bf16[128,1536]{1,0:T(8,128)(2,1)S(1)}, bf16[128,1536]{1,0:T(8,128)(2,1)S(1)}, u32[]{:S(2)}, u32[]{:S(2)}) collective-permute-start(bf16[128,1536]{1,0:T(8,128)(2,1)S(1)} %get-tuple-element.300.refs_0_.refs_2_), channel_id=1, source_target_pairs={{0,2},{1,3},{2,0},{3,1},{4,6},{5,7},{6,4},{7,5},{8,10},{9,11},{10,... | collective-permute-start | bytes 1179656 | tf_op jit(solution)/shard_map/ppermute | solution.py:27
  481.2 30.8 %collective-permute-start.85 = (bf16[128,1536]{1,0:T(8,128)(2,1)S(1)}, bf16[128,1536]{1,0:T(8,128)(2,1)S(1)}, u32[]{:S(2)}, u32[]{:S(2)}) collective-permute-start(bf16[128,1536]{1,0:T(8,128)(2,1)S(1)} %get-tuple-element.300.refs_0_.refs_2_), channel_id=1, source_target_pairs={{0,1},{1,0},{2,3},{3,2},{4,5},{5,4},{6,7},{7,6},{8,9},{9,8},{10,11... | collective-permute-start | bytes 1179656 | tf_op jit(solution)/shard_map/ppermute | solution.py:27
  500.7 33.9 %collective-permute-start.94 = (bf16[128,1536]{1,0:T(8,128)(2,1)}, bf16[128,1536]{1,0:T(8,128)(2,1)}, u32[]{:S(2)}, u32[]{:S(2)}) collective-permute-start(bf16[128,1536]{1,0:T(8,128)(2,1)} %add_up.3.refs_0_), channel_id=1, source_target_pairs={{0,3},{1,2},{2,1},{3,0},{4,7},{5,6},{6,5},{7,4},{8,11},{9,10},{10,... | collective-permute-start | bytes 1179656 | tf_op jit(solution)/shard_map/ppermute | solution.py:27
  502.1 32.4 %collective-permute-start.93 = (bf16[128,1536]{1,0:T(8,128)(2,1)}, bf16[128,1536]{1,0:T(8,128)(2,1)}, u32[]{:S(2)}, u32[]{:S(2)}) collective-permute-start(bf16[128,1536]{1,0:T(8,128)(2,1)} %add_up.3.refs_0_), channel_id=1, source_target_pairs={{0,2},{1,3},{2,0},{3,1},{4,6},{5,7},{6,4},{7,5},{8,10},{9,11},{10,... | collective-permute-start | bytes 1179656 | tf_op jit(solution)/shard_map/ppermute | solution.py:27
  503.8 30.7 %collective-permute-start.92 = (bf16[128,1536]{1,0:T(8,128)(2,1)}, bf16[128,1536]{1,0:T(8,128)(2,1)}, u32[]{:S(2)}, u32[]{:S(2)}) collective-permute-start(bf16[128,1536]{1,0:T(8,128)(2,1)} %add_up.3.refs_0_), channel_id=1, source_target_pairs={{0,1},{1,0},{2,3},{3,2},{4,5},{5,4},{6,7},{7,6},{8,9},{9,8},{10,11... | collective-permute-start | bytes 1179656 | tf_op jit(solution)/shard_map/ppermute | solution.py:27
  545.2 32.5 %collective-permute-start.100 = (bf16[768,1152]{1,0:T(8,128)(2,1)S(1)}, bf16[768,1152]{1,0:T(8,128)(2,1)S(1)}, u32[]{:S(2)}, u32[]{:S(2)}) collective-permute-start(bf16[768,1152]{1,0:T(8,128)(2,1)S(1)} %weight_grads.22), channel_id=1, source_target_pairs={{0,16},{16,0},{1,17},{17,1},{2,18},{18,2},{3,19},{19,3},{4,20},{20... | collective-permute-start | bytes 5308424 | tf_op jit(solution)/shard_map/ppermute | solution.py:27
  545.3 31.2 %collective-permute-start.98 = (bf16[192,2048]{1,0:T(8,128)(2,1)S(1)}, bf16[192,2048]{1,0:T(8,128)(2,1)S(1)}, u32[]{:S(2)}, u32[]{:S(2)}) collective-permute-start(bf16[192,2048]{1,0:T(8,128)(2,1)S(1)} %add_convert_fusion.2.refs_15_), channel_id=1, source_target_pairs={{0,4},{4,8},{8,12},{12,0},{1,5},{5,9},{9,13},{13,1},{2,6},{6,10},{... | collective-permute-start | bytes 2359304 | tf_op jit(solution)/shard_map/ppermute | solution.py:32
  546.4 34.9 %collective-permute-start.95 = (bf16[128,1536]{1,0:T(8,128)(2,1)S(1)}, bf16[128,1536]{1,0:T(8,128)(2,1)S(1)}, u32[]{:S(2)}, u32[]{:S(2)}) collective-permute-start(bf16[128,1536]{1,0:T(8,128)(2,1)S(1)} %get-tuple-element.319), channel_id=1, source_target_pairs={{0,1},{1,0},{2,3},{3,2},{4,5},{5,4},{6,7},{7,6},{8,9},{9,8},{10,11... | collective-permute-start | bytes 1179656 | tf_op jit(solution)/shard_map/ppermute | solution.py:27
  547.2 34.1 %collective-permute-start.96 = (bf16[128,1536]{1,0:T(8,128)(2,1)S(1)}, bf16[128,1536]{1,0:T(8,128)(2,1)S(1)}, u32[]{:S(2)}, u32[]{:S(2)}) collective-permute-start(bf16[128,1536]{1,0:T(8,128)(2,1)S(1)} %get-tuple-element.320), channel_id=1, source_target_pairs={{0,2},{1,3},{2,0},{3,1},{4,6},{5,7},{6,4},{7,5},{8,10},{9,11},{10,... | collective-permute-start | bytes 1179656 | tf_op jit(solution)/shard_map/ppermute | solution.py:27
  571.2 78.3 %collective-permute-start.115 = (bf16[192,1152]{1,0:T(8,128)(2,1)}, bf16[192,1152]{1,0:T(8,128)(2,1)}, u32[]{:S(2)}, u32[]{:S(2)}) collective-permute-start(bf16[192,1152]{1,0:T(8,128)(2,1)} %add_convert_fusion.9.refs_8_.refs_1_), channel_id=1, source_target_pairs={{0,16},{1,17},{2,18},{3,19},{4,20},{5,21},{6,22},{7,23},{8,24},{9,... | collective-permute-start | bytes 1327112 | tf_op jit(solution)/shard_map/ppermute | solution.py:809
  577.6 28.9 %collective-permute-start.107 = (bf16[192,2048]{1,0:T(8,128)(2,1)}, bf16[192,2048]{1,0:T(8,128)(2,1)}, u32[]{:S(2)}, u32[]{:S(2)}) collective-permute-start(bf16[192,2048]{1,0:T(8,128)(2,1)} %add_convert_fusion.1.refs_7_), channel_id=1, source_target_pairs={{0,4},{4,8},{8,12},{12,0},{1,5},{5,9},{9,13},{13,1},{2,6},{6,10},{... | collective-permute-start | bytes 2359304 | tf_op jit(solution)/shard_map/ppermute | solution.py:32
  656.9 30.6 %collective-permute-start.112 = (bf16[512,1536]{1,0:T(8,128)(2,1)S(1)}, bf16[512,1536]{1,0:T(8,128)(2,1)}, u32[]{:S(2)}, u32[]{:S(2)}) collective-permute-start(bf16[512,1536]{1,0:T(8,128)(2,1)S(1)} %copy-done.12), channel_id=1, source_target_pairs={{0,16},{1,17},{2,18},{3,19},{4,20},{5,21},{6,22},{7,23},{8,24},{9,... | collective-permute-start | bytes 4718600 | tf_op jit(solution)/shard_map/ppermute | solution.py:809
  660.1 27.4 %collective-permute-start.104 = (bf16[512,1536]{1,0:T(8,128)(2,1)S(1)}, bf16[512,1536]{1,0:T(8,128)(2,1)}, u32[]{:S(2)}, u32[]{:S(2)}) collective-permute-start(bf16[512,1536]{1,0:T(8,128)(2,1)S(1)} %copy-done.9), channel_id=1, source_target_pairs={{16,0},{17,1},{18,2},{19,3},{20,4},{21,5},{22,6},{23,7},{24,8},{25... | collective-permute-start | bytes 4718600 | tf_op jit(solution)/shard_map/ppermute | solution.py:809
  661.4 26.1 %collective-permute-start.105 = (bf16[512,1536]{1,0:T(8,128)(2,1)}, bf16[512,1536]{1,0:T(8,128)(2,1)}, u32[]{:S(2)}, u32[]{:S(2)}) collective-permute-start(bf16[512,1536]{1,0:T(8,128)(2,1)} %leave.6.refs_1_), channel_id=1, source_target_pairs={{0,16},{1,17},{2,18},{3,19},{4,20},{5,21},{6,22},{7,23},{8,24},{9,... | collective-permute-start | bytes 4718600 | tf_op jit(solution)/shard_map/ppermute | solution.py:809
  (259 other events, 3162.8 us)

commit v3 on v2

--- a/solution.py
+++ b/solution.py
@@ -13,12 +13,14 @@
 EPSILON = 1e-05
 ROPE_BASE = 100000.0
 MASKED = -1e30
-COST = 2 * 10**11
+COST = 60000000000
+COSTS = {'add_slots': 3000000000, 'choose': 2000000000, 'sum_gains': 1000000000, 'own_gains': 1000000000}
 BF = jnp.bfloat16
 F32 = jnp.float32
 WHOLE = pl.BlockSpec(memory_space=pltpu.VMEM)
 ANYWHERE = pl.BlockSpec(memory_space=pl.ANY)
 FAR = pl.BlockSpec(memory_space=pltpu.HBM)
+FETCHED = object()
 SCALAR = pl.BlockSpec(memory_space=pltpu.SMEM)
 
 
@@ -53,18 +55,36 @@
 
 
 def kernel(name, body, ins, outs, grid=(), scratch=(), after=(), vmem=44, flops=0, path=False):
-    arrays, specs, sizes = [], [], []
+    arrays, specs, sizes, fetched = [], [], [], []
     for group in ins:
         sizes.append(len(group))
         for array, spec in group:
+            if spec is FETCHED:
+                fetched.append(len(arrays))
             arrays.append(array)
-            specs.append(spec)
+            specs.append(ANYWHERE if spec is FETCHED else spec)
     count = len(arrays)
     after = list(after)
     arrays += after
     specs += [ANYWHERE] * len(after)
+    targets = [pltpu.VMEM(arrays[k].shape, arrays[k].dtype) for k in fetched]
+    if fetched:
+        targets.append(pltpu.SemaphoreType.DMA((len(fetched),)))
 
     def run(*refs):
+        refs = list(refs)
+        extra = refs[len(refs) - len(targets) :] if targets else []
+        refs = refs[: len(refs) - len(targets)]
+        copies = [
+            pltpu.make_async_copy(refs[k], extra[j], extra[-1].at[j])
+            for j, k in enumerate(fetched)
+        ]
+        for copy in copies:
+            copy.start()
+        for copy in copies:
+            copy.wait()
+        for j, k in enumerate(fetched):
+            refs[k] = extra[j]
         groups, at = [], 0
         for size in sizes:
             groups.append(refs[at : at + size])
@@ -80,10 +100,12 @@
         in_specs=specs,
         out_specs=[spec for _, spec in outs],
         out_shape=[shape for shape, _ in outs],
-        scratch_shapes=list(scratch),
+        scratch_shapes=list(scratch) + targets,
         compiler_params=pltpu.CompilerParams(vmem_limit_bytes=vmem << 20),
         cost_estimate=pl.CostEstimate(
-            flops=COST if path else 0, bytes_accessed=size if path else 1, transcendentals=0
+            flops=COST if path else COSTS.get(name, 0),
+            bytes_accessed=size if path else 1,
+            transcendentals=0,
         ),
         name=name,
     )(*arrays)
@@ -112,7 +134,7 @@
     return kernel_list(
         "enter",
         body,
-        [full([x]), full([order]), full([c], SCALAR)],
+        [full([x], FETCHED), full([order], FETCHED), full([c], SCALAR)],
         [shaped((rows, x.shape[1]))] * count,
         after=after,
         vmem=16,
@@ -120,7 +142,7 @@
     )
 
 
-def leave(pieces, back, c, after=()):
+def leave(pieces, back, c, after=(), path=False):
     rows, width = pieces[0].shape
     count = len(pieces)
 
@@ -137,29 +159,48 @@
         [shaped((rows * count, width))],
         after=after,
         vmem=20,
+        path=path,
         flops=2 * rows * count * width * width,
     )[0]
 
 
 def pack(parts, s, after=()):
-    h = parts[0].shape[0] // 2
-    width = sum(p.shape[1] for p in parts)
-
-    def body(ps, ss, outs, _):
+    flips = [isinstance(p, tuple) for p in parts]
+    parts = [p[0] if flip else p for p, flip in zip(parts, flips)]
+    shapes = [p.shape[::-1] if flip else p.shape for p, flip in zip(parts, flips)]
+    h = shapes[0][0] // 2
+    width = sum(shape[1] for shape in shapes)
+
+    def body(ps, ss, outs, scratch):
+        scratch, sources = list(scratch), []
+        for p, flip in zip(ps, flips):
+            if flip:
+                sources.append(scratch.pop(0))
+                sources[-1][...] = p[...].T
+            else:
+                sources.append(p)
         for out, side in zip(outs, (ss[0][0], 1 - ss[0][0])):
             start = pl.multiple_of(side * h, 16)
             at = 0
-            for p in ps:
+            for p in sources:
                 out[:, at : at + p.shape[1]] = p[pl.ds(start, h), :]
                 at += p.shape[1]
 
-    return kernel("pack", body, [full(parts), full([s], SCALAR)], [shaped((h, width))] * 2, after=after, vmem=16)
-
-
-def unpack(mine, theirs, s, widths, after=()):
+    return kernel(
+        "pack",
+        body,
+        [full(parts, FETCHED), full([s], SCALAR)],
+        [shaped((h, width))] * 2,
+        scratch=[pltpu.VMEM(shape, BF) for shape, flip in zip(shapes, flips) if flip],
+        after=after,
+        vmem=16,
+    )
+
+
+def unpack(mine, got, s, widths, after=(), flips=()):
     h, total = mine[0].shape
 
-    def body(ms, ts, ss, outs, scratch):
+    def body(ms, gs, ss, outs, scratch):
         side = ss[0][0]
         for layer in range(2):
 
@@ -167,36 +208,42 @@
             def _():
                 copies = [
                     pltpu.make_async_copy(ref, scratch[k], scratch[2].at[k])
-                    for k, ref in enumerate((ms[layer], ts[layer]))
+                    for k, ref in enumerate((ms[layer], gs[0]))
                 ]
                 for copy in copies:
                     copy.start()
                 for copy in copies:
                     copy.wait()
 
+        turned = list(scratch[3:])
+        targets = [turned.pop(0) if k in flips else out for k, out in enumerate(outs)]
         for k, at in enumerate((side, 1 - side)):
             start = pl.multiple_of(at * h, 16)
             column = 0
-            for out in outs:
-                width = out.shape[1]
-                out[pl.ds(start, h), :] = scratch[k][:, column : column + width].astype(F32)
+            for target in targets:
+                width = target.shape[1]
+                target[pl.ds(start, h), :] = scratch[k][:, column : column + width].astype(F32)
                 column += width
+        for k in flips:
+            outs[k][...] = targets[k][...].T
 
     return kernel(
         "unpack",
         body,
-        [full(mine, FAR), full(theirs, FAR), full([s], SCALAR)],
-        [shaped((2 * h, w), F32) for w in widths],
-        scratch=[pltpu.VMEM((h, total), BF)] * 2 + [pltpu.SemaphoreType.DMA((2,))],
+        [full(mine, FAR), full([got], FAR), full([s], SCALAR)],
+        [shaped((w, 2 * h) if k in flips else (2 * h, w), F32) for k, w in enumerate(widths)],
+        scratch=[pltpu.VMEM((h, total), BF)] * 2
+        + [pltpu.SemaphoreType.DMA((2,))]
+        + [pltpu.VMEM((2 * h, widths[k]), F32) for k in flips],
         after=after,
         vmem=20,
     )
 
 
-def place_out(mine, theirs, s, after=()):
+def place_out(mine, got, s, after=()):
     shape = mine[0].shape
 
-    def body(ms, ts, ss, outs, scratch):
+    def body(ms, gs, ss, outs, scratch):
         side = ss[0][0]
         for layer in range(2):
 
@@ -204,7 +251,7 @@
             def _():
                 copies = [
                     pltpu.make_async_copy(ref, outs[0].at[at], scratch[0].at[k])
-                    for k, (ref, at) in enumerate(((ms[layer], layer), (ts[layer], 1 - layer)))
+                    for k, (ref, at) in enumerate(((ms[layer], layer), (gs[0], 1 - layer)))
                 ]
                 for copy in copies:
                     copy.start()
@@ -214,7 +261,7 @@
     return kernel(
         "place_out",
         body,
-        [full(mine, FAR), full(theirs, FAR), full([s], SCALAR)],
+        [full(mine, FAR), full([got], FAR), full([s], SCALAR)],
         [shaped((2,) + shape, mine[0].dtype)],
         scratch=[pltpu.SemaphoreType.DMA((2,))],
         after=after,
@@ -410,15 +457,18 @@
     return pieces, grads
 
 
-def feed_forward(pieces, slots, after=()):
+def feed_forward(pieces, wide, narrow, after=()):
     rows, width = pieces[0].shape
     count = len(pieces)
     tokens = rows * count
-    units = slots[0].shape[1] // 3
-
-    def body(ps, ws, outs, scratch):
+    units = wide[0].shape[1] // 3 if wide[0] is narrow[0] else narrow[0].shape[1]
+    last = narrow[0].shape[1] - units
+    slots = len(wide)
+
+    def body(ps, ws, vs, outs, scratch):
         parts = [
-            Fetch(ws, scratch[k], scratch[3], k * units, k * len(slots)) for k in range(3)
+            Fetch(refs, scratch[k], scratch[3], column, k * slots)
+            for k, (refs, column) in enumerate(((ws, 0), (ws, units), (vs, last)))
         ]
         n2 = stacked(ps)
         gate = dot(n2, parts[0].get())
@@ -431,10 +481,10 @@
     gate, up, hidden, *out = kernel(
         "feed_forward",
         body,
-        [full(pieces), full(slots, FAR)],
+        [full(pieces), full(wide, FAR), full(narrow, FAR)],
         [shaped((tokens, units))] * 3 + [shaped((rows, width))] * count,
         scratch=[pltpu.VMEM((width, units), BF)] * 3
-        + [pltpu.SemaphoreType.DMA((3 * len(slots),))],
+        + [pltpu.SemaphoreType.DMA((3 * slots,))],
         path=True,
         after=after,
         vmem=32,
@@ -443,15 +493,18 @@
     return gate, up, hidden, out
 
 
-def feed_forward_back(pieces, gate, up, slots, after=()):
+def feed_forward_back(pieces, gate, up, wide, narrow, after=()):
     rows, width = pieces[0].shape
     count = len(pieces)
     tokens = rows * count
     units = gate.shape[1]
 
-    def body(ps, gus, ws, outs, scratch):
-        down = Fetch(ws, scratch[0], scratch[2], 2 * units)
-        rest = Fetch(ws, scratch[1], scratch[2], 0, len(slots))
+    last = narrow[0].shape[1] - units
+    slots = len(wide)
+
+    def body(ps, gus, ws, vs, outs, scratch):
+        down = Fetch(vs, scratch[0], scratch[2], last)
+        rest = Fetch(ws, scratch[1], scratch[2], 0, slots)
         grad = dot(stacked(ps), down.get())
         gate, up = gus[0][...].astype(F32), gus[1][...].astype(F32)
         sig = 1.0 / (1.0 + jnp.exp(-gate))
@@ -463,10 +516,10 @@
     grads, *out = kernel(
         "feed_forward_back",
         body,
-        [full(pieces), full([gate, up]), full(slots, FAR)],
+        [full(pieces), full([gate, up]), full(wide, FAR), full(narrow, FAR)],
         [shaped((tokens, 2 * units))] + [shaped((rows, width))] * count,
         scratch=[pltpu.VMEM((width, units), BF), pltpu.VMEM((width, 2 * units), BF)]
-        + [pltpu.SemaphoreType.DMA((2 * len(slots),))],
+        + [pltpu.SemaphoreType.DMA((2 * slots,))],
         path=True,
         after=after,
         vmem=32,
@@ -475,12 +528,12 @@
     return grads, out
 
 
-def weight_grads(terms, half, block, got=None, after=()):
+def weight_grads(terms, half, block, after=()):
     width = terms[0][0][0].shape[1] // 2
     tokens = terms[0][1].shape[0]
     steps = [rhs.shape[1] // block for _, rhs in terms]
     total = sum(rhs.shape[1] for _, rhs in terms)
-    n = 1 if got is None else lax.axis_size("row")
+    n = 1 if half else lax.axis_size("row")
     rows = width // n
     ins, begins = [], []
     for k, (lhs, rhs) in enumerate(terms):
@@ -491,10 +544,9 @@
             lambda j, lo, hi: (0, jnp.clip(j - lo, 0, hi)), lo=begin, hi=steps[k] - 1
         )
         ins.append([(rhs, pl.BlockSpec((tokens, block), place))])
-    ins.append([] if got is None else [(got, pl.BlockSpec((width, block), lambda j: (0, j)))])
 
     def body(*refs):
-        *refs, more, outs, scratch = refs
+        *refs, outs, scratch = refs
         j = pl.program_id(0)
         for k, begin in enumerate(begins):
             lhs, rhs = refs[2 * k : 2 * k + 2]
@@ -505,25 +557,111 @@
 
             @pl.when((j >= begin) & (j < begin + steps[k]))
             def _():
-                value = dot(scratch[0][...], rhs[0][...])
-                if got is not None:
-                    value = value + more[0][...].astype(F32)
-                value = value.astype(BF)
+                value = dot(scratch[0][...], rhs[0][...]).astype(BF)
                 for k in range(n):
                     outs[k][...] = value[k * rows : (k + 1) * rows]
 
-    out = kernel(
-        "weight_grads",
-        body,
-        ins,
-        [shaped((rows, total), BF, pl.BlockSpec((rows, block), lambda j: (0, j)))] * n,
-        grid=(sum(steps),),
-        scratch=[pltpu.VMEM((width, tokens), BF)],
-        after=after,
-        vmem=20,
-        flops=2 * tokens * width * total,
-    )
-    return out[0] if got is None else out
+    return list(
+        kernel(
+            "weight_grads",
+            body,
+            ins,
+            [shaped((rows, total), BF, pl.BlockSpec((rows, block), lambda j: (0, j)))] * n,
+            grid=(sum(steps),),
+            scratch=[pltpu.VMEM((width, tokens), BF)],
+            after=after,
+            vmem=20,
+            flops=2 * tokens * width * total,
+        )
+    )
+
+
+def add_slots(slot, got, k, come=None, after=()):
+    rows, width = slot.shape
+    half = width // 2 if width % 256 == 0 else width
+    plain = pl.BlockSpec((rows, half), lambda j: (0, j))
+    ins = [(slot, plain), (got, pl.BlockSpec((rows, half), lambda j: (k, j)))]
+    if come is not None:
+        ins.append((come, plain))
+
+    def body(refs, outs, _):
+        outs[0][...] = total_of(refs).astype(BF)
+
+    return kernel(
+        "add_slots",
+        body,
+        [ins],
+        [shaped(slot.shape, BF, plain)],
+        grid=(width // half,),
+        after=after,
+        vmem=16,
+    )[0]
+
+
+def choose(values, s, after=()):
+    def body(vs, ss, outs, scratch):
+        for side in range(2):
+
+            @pl.when(ss[0][0] == side)
+            def _():
+                copy = pltpu.make_async_copy(vs[1 - side], outs[0], scratch[0].at[0])
+                copy.start()
+                copy.wait()
+
+    return kernel(
+        "choose",
+        body,
+        [full(values, ANYWHERE), full([s], SCALAR)],
+        [shaped(values[0].shape, values[0].dtype)],
+        scratch=[pltpu.SemaphoreType.DMA((1,))],
+        after=after,
+        vmem=16,
+    )[0]
+
+
+def sum_gains(terms, s, n):
+    h = terms[0].shape[1] // (2 * n)
+
+    def body(ts, ss, outs, _):
+        total = total_of(ts)
+        for k in range(n):
+            first = total[:, k * h : (k + 1) * h]
+            second = total[:, (n + k) * h : (n + k + 1) * h]
+            for side in range(2):
+
+                @pl.when(ss[0][0] == side)
+                def _():
+                    low, high = (first, second) if side == 0 else (second, first)
+                    outs[k][:, :h] = low
+                    outs[k][:, h:] = high
+
+    return kernel(
+        "sum_gains",
+        body,
+        [full(terms), full([s], SCALAR)],
+        [shaped((4, 2 * h), F32)] * n,
+        vmem=8,
+    )
+
+
+def own_gains(terms, s):
+    def body(ts, ss, outs, _):
+        total = total_of(ts)
+        for side in range(2):
+
+            @pl.when(ss[0][0] == side)
+            def _():
+                outs[0][...] = total[2 * side : 2 * side + 2]
+                outs[1][...] = total[2 - 2 * side : 4 - 2 * side]
+
+    width = terms[0].shape[1]
+    return kernel(
+        "own_gains",
+        body,
+        [full(terms), full([s], SCALAR)],
+        [shaped((2, width), F32)] * 2,
+        vmem=8,
+    )
 
 
 def total_of(refs):
@@ -546,7 +684,7 @@
     return kernel(
         "add_and_norm",
         body,
-        [full([x]), full(terms), full([gain])],
+        [full([x], FETCHED), full(terms, FETCHED), full([gain])],
         [shaped(x.shape, F32), shaped(x.shape)],
         path=True,
         after=after,
@@ -561,7 +699,7 @@
     return kernel(
         "add_up",
         body,
-        [full([middle]), full(terms)],
+        [full([middle], FETCHED), full(terms, FETCHED)],
         [shaped(middle.shape)],
         after=after,
         vmem=16,
@@ -585,7 +723,7 @@
     return kernel(
         "norm_back",
         body,
-        [full([x]), full(terms), full([gain]), full([straight])],
+        [full([x], FETCHED), full(terms, FETCHED), full([gain]), full([straight], FETCHED)],
         [shaped((1, x.shape[1]), F32), shaped(x.shape, F32), shaped(x.shape)],
         path=True,
         after=after,
@@ -620,16 +758,31 @@
 
 
 class Scatter:
-    def __init__(self, slots):
-        self.slots = list(slots)
-        self.moving = self.slots.pop()
-        self.parts = strides(len(slots) - 1)
-
-    def hop(self, *now):
-        self.moving = behind(self.moving, *now)
-        for _ in range(self.parts.pop(0)):
-            got = ring(self.moving, 1).astype(F32)
-            self.moving = (self.slots.pop().astype(F32) + got).astype(BF)
+    def __init__(self, terms, block):
+        other = weight_grads(terms, 1, block)
+        self.slots = weight_grads(terms, 0, block)
+        self.got = mate(other[0], "section", 1)
+        self.made = [self.slots[0], other[0]]
+        self.parts = strides(len(self.slots) - 1)
+        self.moving = None
+
+    def add(self, come, *now):
+        k = len(self.slots) - 1
+        self.moving = add_slots(self.slots.pop(), self.got, k, come, now)
+
+    def begin(self, *now):
+        if self.moving is None:
+            self.add(None, *now)
+        else:
+            self.moving = behind(self.moving, *now)
+        steps = self.parts.pop(0)
+        for step in range(steps):
+            self.come = ring(self.moving, 1)
+            if step < steps - 1:
+                self.add(self.come)
+
+    def finish(self, *now):
+        self.add(self.come, *now)
         return [self.moving]
 
 
@@ -686,24 +839,13 @@
     )
 
 
-def reduce_gains(gains):
-    s = lax.axis_index("section")
-    n = lax.axis_size("row")
-    total = gains
-    for k in range(1, lax.axis_size("col")):
-        total = total + mate(gains, "col", k)
-    h = gains.shape[1] // (2 * n)
-    total = total.reshape(4, 2, n, h)
-    first, second = total[:, 0], total[:, 1]
-    total = jnp.concatenate(
-        [jnp.where(s == 0, first, second), jnp.where(s == 0, second, first)], -1
-    )
-    here = total[:, 0]
-    for k in range(1, n):
-        here = here + ring(total[:, k], k)
-    keep = jnp.where(s == 0, here[:2], here[2:])
-    send = jnp.where(s == 0, here[2:], here[:2])
-    return keep + mate(send, "section", 1)
+def gather_gains(gains, s):
+    terms = [gains] + [mate(gains, "col", k) for k in range(1, lax.axis_size("col"))]
+    return list(sum_gains(terms, s, lax.axis_size("row")))
+
+
+def reduce_gains(slots, s):
+    return list(own_gains([slots[0]] + [ring(slots[k], k) for k in range(1, len(slots))], s))
 
 
 def body(
@@ -730,15 +872,16 @@
     s_here, c_here = s.astype(jnp.int32)[None], c.astype(jnp.int32)[None]
 
     def start(parts, after):
-        keep, send = pack([p[0] for p in parts], s_here, after)
+        keep, send = pack(parts, s_here, after)
         got = mate(send, "section", 1)
         return [jnp.where(s == layer, keep, got) for layer in range(2)]
 
-    attn_start = start((w_query, key_weight, value_weight, w_out), [])
+    flipped = [(jnp.swapaxes(w[0], 0, 1), True) for w in (key_weight, value_weight)]
+    attn_start = start((w_query[0], *flipped, w_out[0]), [])
     first = attn_start[0]
     a = Gather(first)
     come = a.hop()
-    ffn_start = start((w_gate, w_up, w_down), [first])
+    ffn_start = start((w_gate[0], w_up[0], w_down[0]), [first])
     f = Gather(ffn_start[0])
 
     gains = behind(jnp.concatenate([gain_attn, gain_ffn], 0), first)
@@ -771,9 +914,10 @@
     orders = [own_order[None, :], jnp.concatenate([own_order, order_of(1 - parity)])[:, None]]
 
     point = meet(come)
-    come = f.hop(*come)
-    x = enter(x, order, c_here, count, a.hop() + come + point, True)
+    come = a.hop()
+    x = enter(x, order, c_here, count, come + point + f.slots, True)
     a.hop()
+    f.hop(*come)
     grad = enter(cot, order, c_here, count)
 
     kept, outs, gathers = [], [], []
@@ -797,7 +941,9 @@
         if not last:
             f = Gather(ffn_start[1])
             come = f.hop(n2[-1]) + a.hop(n2[-1])
-        gate, up, hidden, y = feed_forward(n2, gathers[-1][1].all(), point)
+        gate, up, hidden, y = feed_forward(
+            n2, gathers[-1][1].all(), gathers[-1][1].all(), point
+        )
         kept.append((x[0], n1, query, own, there, mixed, sums, middle, n2, gate, up, hidden))
         if not last:
             sent = received(y)
@@ -805,8 +951,8 @@
             x = gather_pieces(add_up(middle, sent, come))
             outs.append(x)
 
-    def to_owner(value, layer):
-        return lax.ppermute(value, "section", [(1 - layer, layer)])
+    def exchange(values):
+        return mate(choose(values, s_here), "section", 1)
 
     left, parts, gain_parts = [None, None], [None, None], [None, None]
     last_y, s_a, come = y, None, []
@@ -814,73 +960,81 @@
         a, f = gathers[layer]
         x, n1, query, own, there, mixed, sums, middle, n2, gate, up, hidden = kept[layer]
         gain1, gain2 = gains[2 * layer], gains[2 * layer + 1]
-        grad_gu, y = feed_forward_back(grad, gate, up, f.all(), come)
-        come = s_a.hop(grad[-1]) if s_a else []
+        if s_a:
+            s_a.begin(grad[-1])
+            s_d.begin(grad[-1])
+        grad_gu, y = feed_forward_back(grad, gate, up, f.all(), f.all(), come)
         sent = received(y)
-        down, rest = [(grad, behind(hidden, grad_gu))], [(n2, grad_gu)]
-        got = mate(weight_grads(down, 1, units // 2), "section", 1)
-        s_d = Scatter(weight_grads(down, 0, units // 2, got))
-        other = weight_grads(rest, 1, units // 2)
-        got = mate(other, "section", 1)
-        come += [s_d.moving, other]
+        come = s_a.finish(sent[-1]) + s_d.finish(sent[-1]) if s_a else []
+        s_f = Scatter([(n2, grad_gu)], units // 2)
+        come += s_f.made
+        s_f.begin(sent[-1])
+        if s_a:
+            s_a.begin(sent[-1])
         g_gain2, grad_middle, grad_attn = norm_back(middle, sent, gain2, grad[0], come)
-        come = s_d.hop(sent[-1]) + (s_a.hop(sent[-1]) if s_a else [])
-        s_f = Scatter(weight_grads(rest, 0, units // 2, behind(got, grad_attn)))
+        s_d = Scatter([(grad, behind(hidden, grad_attn))], units // 2)
         grad_attn = gather_pieces(grad_attn)
+        come = s_d.made + s_f.finish(grad_attn[-1]) + (s_a.finish(grad_attn[-1]) if s_a else [])
+        s_d.begin(grad_attn[-1])
         grad_query, grad_own, grad_there = attention_back(
-            grad_attn, query, own, there, sums, orders, a.all(), come + [s_f.moving]
+            grad_attn, query, own, there, sums, orders, a.all(), come
         )
-        come = s_f.hop(grad_attn[-1])
         if layer == 1:
             last_y = received([behind(p, grad_attn[-1]) for p in last_y])
             left[0] = leave([behind(p, grad_there) for p in outs[0]], back_order, c_here)
-            come += last_y[1:] + [left[0]]
+            come = last_y[1:] + [left[0]]
         else:
-            last_y = add_up(kept[1][7], last_y)
-            outs.append(gather_pieces(behind(last_y, grad_attn[-1])))
+            outs.append(gather_pieces(add_up(kept[1][7], last_y, grad_attn[-1:])))
             left[1] = leave([behind(p, grad_there) for p in grad], back_order, c_here)
-            come += outs[1][1:] + [left[1]]
+            come = outs[1][1:] + [left[1]]
         back = mate(grad_there, "row", 1)
+        come += s_d.finish(back)
+        s_f.begin(back)
+        s_d.begin(back)
         y, grad_qkv = project_back(
             grad_query, grad_own, back, a.all(), tables, swaps, count, come
         )
-        come = s_f.hop(back) + (s_a.hop(back) if s_a else s_d.hop(back))
         sent = received(y)
-        terms = [([n1], grad_qkv), (grad_attn, mixed)]
-        other = weight_grads(terms, 1, width_q)
-        got = mate(other, "section", 1)
-        mine = weight_grads(terms, 0, width_q, got)
-        came = come + list(mine[:1] if layer == 0 else [other])
-        g_gain1, _, grad = norm_back(x, sent, gain1, grad_middle, came)
-        come = s_f.hop(sent[-1]) + s_d.hop(sent[-1])
-        s_a = Scatter(mine)
+        come = s_f.finish(sent[-1]) + s_d.finish(sent[-1])
+        s_a = Scatter([([n1], grad_qkv), (grad_attn, mixed)], width_q)
+        s_f.begin(sent[-1])
+        s_a.begin(sent[-1])
+        g_gain1, _, grad = norm_back(x, sent, gain1, grad_middle, come + s_a.made)
+        mark = meet([grad])
         grad = gather_pieces(grad)
-        if layer == 1:
-            come += [s_a.moving]
+        come = s_f.finish(grad[-1]) + s_a.finish(grad[-1])
         parts[layer] = (s_a, s_f, s_d)
         gain_parts[layer] = (g_gain1, g_gain2)
 
-    come += s_a.hop(sent[-1])
-    acts = [left[0], leave([behind(p, g_gain1) for p in outs[1]], back_order, c_here)]
-    point = meet(grad[1:] + acts[1:])
-    grads = [leave([behind(p, *point) for p in grad], back_order, c_here), left[1]]
-    grads_there = [to_owner(v, k) for k, v in enumerate(grads)]
-    acts_there = [to_owner(behind(v, *point), k) for k, v in enumerate(acts)]
+    acts = [left[0], leave([behind(p, *mark) for p in outs[1]], back_order, c_here)]
+    point = meet(grad[1:] + acts[1:] + come + mark)
+    s_a.begin(*point)
+    s_d.begin(*point)
+    mark = meet(point)
+    grads = [leave([behind(p, *mark) for p in grad], back_order, c_here, path=True), left[1]]
+    grads_got = exchange(grads)
+    acts_got = exchange([behind(v, *mark) for v in acts])
+    wide = [p[1].moving for p in parts]
+    wide_got = exchange([behind(v, *mark) for v in wide])
     gain_grads = jnp.concatenate(list(gain_parts[0]) + list(gain_parts[1]), 0)
-    gain_grads = reduce_gains(behind(gain_grads, *point))
-    come = s_d.hop(*come) + s_a.hop(*come)
-    point = meet(come + grads_there + acts_there)
-    s_a.hop(*come)
-    acts = place_out(acts, acts_there, s_here, point)
-    grads = place_out(grads, grads_there, s_here, point)
-
-    def owned(k, widths):
-        values = [behind(p[k].moving, *come) if k else p[k].moving for p in parts]
-        return unpack(values, [to_owner(v, layer) for layer, v in enumerate(values)], s_here, widths)
-
-    (g_down,) = owned(2, (units,))
-    g_gate, g_up = owned(1, (units, units))
-    g_query, g_key, g_value, g_out = owned(0, (width_q, width_kv, width_kv, width_q))
+    gain_slots = gather_gains(behind(gain_grads, grads[0]), s_here)
+    point = meet(s_a.finish(grads[0]) + s_d.finish(grads[0]) + gain_slots + mark)
+    s_a.begin(*point)
+    mark = meet(point)
+    acts = place_out([behind(v, *mark) for v in acts], acts_got, s_here)
+    grads = place_out([behind(v, *mark) for v in grads], grads_got, s_here)
+    g_gate, g_up = unpack([behind(v, *mark) for v in wide], wide_got, s_here, (units, units))
+    gain_grads = reduce_gains(gain_slots, s_here)
+    s_a.finish(grads, acts, g_up, *gain_grads)
+    gain_grads = gain_grads[0] + mate(gain_grads[1], "section", 1)
+    heads, narrow = ([p[k].moving for p in parts] for k in (0, 2))
+    heads_got, narrow_got = exchange(heads), exchange(narrow)
+    point = meet([heads_got, narrow_got, g_up, acts, grads])
+    (g_down,) = unpack(narrow, narrow_got, s_here, (units,), point)
+    g_query, g_key, g_value, g_out = unpack(
+        heads, heads_got, s_here, (width_q, width_kv, width_kv, width_q), point, (1, 2)
+    )
+    g_key, g_value = jnp.swapaxes(g_key, 0, 1), jnp.swapaxes(g_value, 0, 1)
     return (
         acts[None],
         grads[None],

time: 702 us -> 637 us (0.907)
  starting transfers between devices: 151 us -> 119 us
  other arithmetic: 35.2 us -> 11.6 us
  Pallas kernels: 173 us -> 164 us
  local copies, waits for them, and re-layouts: 45.4 us -> 37.8 us
    ppermute x81 -> x86, waiting for transfers between devices: 160 us -> 198 us  [mate(): return lax.ppermute(x, axis, [(j, j ^ k) for j in range(n)])]
    ppermute x36, waiting for transfers between devices: 127 us -> 96.8 us  [ring(): return lax.ppermute(x, 'row', [(j, (j + by) % n) for j in range(n)])]
    ppermute x10 -> x0, starting transfers between devices: 24.4 us -> none  [to_owner(): return lax.ppermute(value, 'section', [(1 - layer, layer)])]
    convert_element_type x18 -> x0, other arithmetic: 22.1 us -> none  [hop(): self.moving = (self.slots.pop().astype(F32) + got).astype(BF)]
    pallas_call x51 -> x82, Pallas kernels: 173 us -> 164 us  [kernel(): pl.pallas_call(run, grid=grid, in_specs=specs, out_specs=[spec for _, spe...]
    unnamed x332 -> x352, local copies, waits for them, and re-layouts: 39 us -> 31.4 us
    ppermute x81 -> x86, starting transfers between devices: 68.7 us -> 63.9 us  [mate(): return lax.ppermute(x, axis, [(j, j ^ k) for j in range(n)])]
  transfers between devices with their start and end apart: 127 -> 122, of which waited for: 50 -> 61; matrix products, arithmetic and copies ran while one was open for 6% -> 2% of each run, Pallas kernels for 18% -> 22%
where the time goes in v3:
time: 637 us; the launch traced here: 631 us
  waiting for transfers between devices  295 us (46%)
  Pallas kernels  164 us (26%)
  starting transfers between devices  119 us (19%)
  local copies, waits for them, and re-layouts  37.8 us (6%)
  other arithmetic  11.6 us (2%)
    ppermute x86, waiting for transfers between devices, mate(): return lax.ppermute(x, axis, [(j, j ^ k) for j in range(n)])  198 us
    pallas_call x82, Pallas kernels, kernel(): pl.pallas_call(run, grid=grid, in_specs=specs, out_specs=[spec for _, spe...  164 us
    ppermute x36, waiting for transfers between devices, ring(): return lax.ppermute(x, 'row', [(j, (j + by) % n) for j in range(n)])  96.8 us
    ppermute x86, starting transfers between devices, mate(): return lax.ppermute(x, axis, [(j, j ^ k) for j in range(n)])  63.9 us
    ppermute x36, starting transfers between devices, ring(): return lax.ppermute(x, 'row', [(j, (j + by) % n) for j in range(n)])  55.4 us
    unnamed x352, local copies, waits for them, and re-layouts  31.4 us
  transfers between devices with their start and end apart: 122, of which 61 were waited for; matrix products, arithmetic and copies ran while one was open for 2% of the time, Pallas kernels for 22%

profile of v3, /device:TPU:0, one launch (start us, length us, event | category | flops | bytes accessed | tf_op | source)
XLA Modules:
  0.0 630.8 jit_solution(15444504442549402620)
XLA Ops:
  50.2 7.6 %collective-permute-done.8.refs_8_.refs_13_.refs_6_ = bf16[192,1152]{1,0:T(8,128)(2,1)S(1)} collective-permute-done((bf16[192,1152]{1,0:T(8,128)(2,1)S(1)}, bf16[192,1152]{1,0:T(8,128)(2,1)S(1)}, u32[]{:S(2)}, u32[]{:S(2)}) %collective-permute-start.8) | collective-permute-done | bytes 442400 | tf_op jit(solution)/shard_map/ppermute | solution.py:34
  65.8 25.3 %collective-permute-done.13.refs_2_.refs_6_ = bf16[512,384]{1,0:T(8,128)(2,1)S(1)} collective-permute-done((bf16[512,384]{1,0:T(8,128)(2,1)S(1)}, bf16[512,384]{1,0:T(8,128)(2,1)S(1)}, u32[]{:S(2)}, u32[]{:S(2)}) %collective-permute-start.13) | collective-permute-done | bytes 393248 | tf_op jit(solution)/shard_map/ppermute | solution.py:29
  95.5 6.8 %attention.2 = (bf16[512,384]{1,0:T(8,128)(2,1)S(1)}, f32[4,512]{1,0:T(4,128)S(1)}, bf16[128,1536]{1,0:T(8,128)(2,1)S(1)}, bf16[128,1536]{1,0:T(8,128)(2,1)}, bf...) custom-call(bf16[512,384]{1,0:T(8,128)(2,1)S(1)} %get-tuple-element.205.refs_0_.refs_4_, ...), custom_call_target="tpu_custom_call" | custom-call | flops 60000002048 | bytes 6699008 | tf_op jit(solution)/shard_map/attention/pallas_call | solution.py:97
  107.3 9.6 %collective-permute-done.16.refs_4_ = bf16[128,1536]{1,0:T(8,128)(2,1)S(1)} collective-permute-done((bf16[128,1536]{1,0:T(8,128)(2,1)}, bf16[128,1536]{1,0:T(8,128)(2,1)S(1)}, u32[]{:S(2)}, u32[]{:S(2)}) %collective-permute-start.16) | collective-permute-done | bytes 393248 | tf_op jit(solution)/shard_map/ppermute | solution.py:29
  138.3 9.5 %collective-permute-done.21.refs_2_.refs_3_ = bf16[128,1536]{1,0:T(8,128)(2,1)S(1)} collective-permute-done((bf16[128,1536]{1,0:T(8,128)(2,1)S(1)}, bf16[128,1536]{1,0:T(8,128)(2,1)S(1)}, u32[]{:S(2)}, u32[]{:S(2)}) %collective-permute-start.21) | collective-permute-done | bytes 393248 | tf_op jit(solution)/shard_map/ppermute | solution.py:29
  161.2 7.7 %feed_forward.2 = (bf16[512,1024]{1,0:T(8,128)(2,1)S(1)}, bf16[512,1024]{1,0:T(8,128)(2,1)S(1)}, bf16[512,1024]{1,0:T(8,128)(2,1)S(1)}, bf16[128,1536]{1,0:T(8,1...) custom-call(bf16[128,1536]{1,0:T(8,128)(2,1)S(1)} %get-tuple-element.214.r, ...), custom_call_target="tpu_custom_call" | custom-call | flops 60000002048 | bytes 25165824 | tf_op jit(solution)/shard_map/feed_forward/pallas_call | solution.py:97
  173.5 9.4 %collective-permute-done.30.refs_4_ = bf16[128,1536]{1,0:T(8,128)(2,1)S(1)} collective-permute-done((bf16[128,1536]{1,0:T(8,128)(2,1)S(1)}, bf16[128,1536]{1,0:T(8,128)(2,1)S(1)}, u32[]{:S(2)}, u32[]{:S(2)}) %collective-permute-start.30) | collective-permute-done | bytes 393248 | tf_op jit(solution)/shard_map/ppermute | solution.py:29
  185.5 6.1 collective-permute-done.31.refs_5_.refs_13_.refs_7_.refs_15_
  207.0 6.5 %collective-permute-done.34.refs_1_.refs_2_ = bf16[128,1536]{1,0:T(8,128)(2,1)} collective-permute-done((bf16[128,1536]{1,0:T(8,128)(2,1)}, bf16[128,1536]{1,0:T(8,128)(2,1)}, u32[]{:S(2)}, u32[]{:S(2)}) %collective-permute-start.34) | collective-permute-done | bytes 393248 | tf_op jit(solution)/shard_map/ppermute | solution.py:29
  216.2 5.6 project.3
  221.9 11.1 %collective-permute-done.41.refs_2_.refs_6_ = bf16[512,384]{1,0:T(8,128)(2,1)S(1)} collective-permute-done((bf16[512,384]{1,0:T(8,128)(2,1)S(1)}, bf16[512,384]{1,0:T(8,128)(2,1)S(1)}, u32[]{:S(2)}, u32[]{:S(2)}) %collective-permute-start.41) | collective-permute-done | bytes 393248 | tf_op jit(solution)/shard_map/ppermute | solution.py:29
  236.4 6.8 %attention.3 = (bf16[512,384]{1,0:T(8,128)(2,1)S(1)}, f32[4,512]{1,0:T(4,128)S(1)}, bf16[128,1536]{1,0:T(8,128)(2,1)S(1)}, bf16[128,1536]{1,0:T(8,128)(2,1)}, bf...) custom-call(bf16[512,384]{1,0:T(8,128)(2,1)S(1)} %get-tuple-element.225.refs_0_.refs_4_, ...), custom_call_target="tpu_custom_call" | custom-call | flops 60000002048 | bytes 6699008 | tf_op jit(solution)/shard_map/attention/pallas_call | solution.py:97
  250.2 8.4 %collective-permute-done.44.refs_4_ = bf16[128,1536]{1,0:T(8,128)(2,1)} collective-permute-done((bf16[128,1536]{1,0:T(8,128)(2,1)}, bf16[128,1536]{1,0:T(8,128)(2,1)}, u32[]{:S(2)}, u32[]{:S(2)}) %collective-permute-start.44) | collective-permute-done | bytes 393248 | tf_op jit(solution)/shard_map/ppermute | solution.py:29
  273.2 9.5 %collective-permute-done.48.refs_2_.refs_3_ = bf16[128,1536]{1,0:T(8,128)(2,1)S(1)} collective-permute-done((bf16[128,1536]{1,0:T(8,128)(2,1)S(1)}, bf16[128,1536]{1,0:T(8,128)(2,1)S(1)}, u32[]{:S(2)}, u32[]{:S(2)}) %collective-permute-start.48) | collective-permute-done | bytes 393248 | tf_op jit(solution)/shard_map/ppermute | solution.py:29
  282.7 6.7 %collective-permute-done.47.refs_1_.refs_2_ = bf16[128,1536]{1,0:T(8,128)(2,1)S(1)} collective-permute-done((bf16[128,1536]{1,0:T(8,128)(2,1)S(1)}, bf16[128,1536]{1,0:T(8,128)(2,1)S(1)}, u32[]{:S(2)}, u32[]{:S(2)}) %collective-permute-start.47) | collective-permute-done | bytes 393248 | tf_op jit(solution)/shard_map/ppermute | solution.py:29
  293.9 7.1 %feed_forward.3 = (bf16[512,1024]{1,0:T(8,128)(2,1)S(1)}, bf16[512,1024]{1,0:T(8,128)(2,1)S(1)}, bf16[512,1024]{1,0:T(8,128)(2,1)S(1)}, bf16[128,1536]{1,0:T(8,1...) custom-call(bf16[128,1536]{1,0:T(8,128)(2,1)S(1)} %get-tuple-element.236.r, ...), custom_call_target="tpu_custom_call" | custom-call | flops 60000002048 | bytes 25165824 | tf_op jit(solution)/shard_map/feed_forward/pallas_call | solution.py:97
  301.0 7.3 %feed_forward_back.2 = (bf16[512,2048]{1,0:T(8,128)(2,1)S(1)}, bf16[128,1536]{1,0:T(8,128)(2,1)S(1)}, bf16[128,1536]{1,0:T(8,128)(2,1)S(1)}, bf16[128,1536]{1,0:T(8,128)(2,1)S(1)}, bf16[128,1536]{1,0:T(8,128)(2,1)S(1)}) custom-call(bf16[128,1536]{1,0:T(8,128)(2,1)S(1)} %copy-done.17, bf16[128,1536]{1,0:T(8,128)(2,1)S(1)} %copy-done.19, ...), custom_call_target="tpu_custom_call" | custom-call | flops 60000002048 | bytes 26214400 | tf_op jit(solution)/shard_map/feed_forward_back/pallas_call | solution.py:97
  320.4 8.8 %collective-permute-done.55.refs_3_ = bf16[128,1536]{1,0:T(8,128)(2,1)S(1)} collective-permute-done((bf16[128,1536]{1,0:T(8,128)(2,1)S(1)}, bf16[128,1536]{1,0:T(8,128)(2,1)S(1)}, u32[]{:S(2)}, u32[]{:S(2)}) %collective-permute-start.55) | collective-permute-done | bytes 393248 | tf_op jit(solution)/shard_map/ppermute | solution.py:29
  338.7 7.6 %collective-permute-done.59.refs_3_.refs_2_.refs_5_ = bf16[128,1536]{1,0:T(8,128)(2,1)S(1)} collective-permute-done((bf16[128,1536]{1,0:T(8,128)(2,1)S(1)}, bf16[128,1536]{1,0:T(8,128)(2,1)S(1)}, u32[]{:S(2)}, u32[]{:S(2)}) %collective-permute-start.59) | collective-permute-done | bytes 393248 | tf_op jit(solution)/shard_map/ppermute | solution.py:29
  346.9 8.6 %collective-permute-done.61.refs_2_ = bf16[192,2048]{1,0:T(8,128)(2,1)S(1)} collective-permute-done((bf16[192,2048]{1,0:T(8,128)(2,1)S(1)}, bf16[192,2048]{1,0:T(8,128)(2,1)S(1)}, u32[]{:S(2)}, u32[]{:S(2)}) %collective-permute-start.61) | collective-permute-done | bytes 786464 | tf_op jit(solution)/shard_map/ppermute | solution.py:34
  357.4 9.0 %attention_back.2 = (f32[512,384]{1,0:T(8,128)S(1)}, f32[512,384]{1,0:T(8,128)S(1)}, bf16[512,384]{1,0:T(8,128)(2,1)S(1)}) custom-call(bf16[128,1536]{1,0:T(8,128)(2,1)S(1)} %get-tuple-element.246.refs_0_.refs_2_, bf16[128,1536]{1,0:T(8,128)(2,1)S(1)} %collective-permute-done.57.refs_1_.refs_3_, ...), custom_call_target="tpu_custom_call" | custom-call | flops 60000002048 | bytes 8271872 | tf_op jit(solution)/shard_map/attention_back/pallas_call | solution.py:97
  378.7 6.0 collective-permute-done.64.refs_16_.refs_3_
  415.3 7.9 %collective-permute-done.75.refs_3_ = bf16[128,1536]{1,0:T(8,128)(2,1)S(1)} collective-permute-done((bf16[128,1536]{1,0:T(8,128)(2,1)S(1)}, bf16[128,1536]{1,0:T(8,128)(2,1)S(1)}, u32[]{:S(2)}, u32[]{:S(2)}) %collective-permute-start.75) | collective-permute-done | bytes 393248 | tf_op jit(solution)/shard_map/ppermute | solution.py:29
  429.1 8.5 %collective-permute-done.78.refs_2_ = bf16[192,1152]{1,0:T(8,128)(2,1)S(1)} collective-permute-done((bf16[192,1152]{1,0:T(8,128)(2,1)S(1)}, bf16[192,1152]{1,0:T(8,128)(2,1)S(1)}, u32[]{:S(2)}, u32[]{:S(2)}) %collective-permute-start.78) | collective-permute-done | bytes 442400 | tf_op jit(solution)/shard_map/ppermute | solution.py:34
  441.3 7.3 %feed_forward_back.3 = (bf16[512,2048]{1,0:T(8,128)(2,1)S(1)}, bf16[128,1536]{1,0:T(8,128)(2,1)S(1)}, bf16[128,1536]{1,0:T(8,128)(2,1)S(1)}, bf16[128,1536]{1,0:T(8,128)(2,1)S(1)}, bf16[128,1536]{1,0:T(8,128)(2,1)S(1)}) custom-call(bf16[128,1536]{1,0:T(8,128)(2,1)S(1)} %get-tuple-element.310.refs_0_.refs_6_, ...), custom_call_target="tpu_custom_call" | custom-call | flops 60000002048 | bytes 26214400 | tf_op jit(solution)/shard_map/feed_forward_back/pallas_call | solution.py:97
  470.2 8.1 %collective-permute-done.86.refs_3_.refs_5_.refs_2_ = bf16[128,1536]{1,0:T(8,128)(2,1)S(1)} collective-permute-done((bf16[128,1536]{1,0:T(8,128)(2,1)S(1)}, bf16[128,1536]{1,0:T(8,128)(2,1)S(1)}, u32[]{:S(2)}, u32[]{:S(2)}) %collective-permute-start.86) | collective-permute-done | bytes 393248 | tf_op jit(solution)/shard_map/ppermute | solution.py:29
  482.6 16.4 %collective-permute-done.88.refs_2_ = bf16[192,2048]{1,0:T(8,128)(2,1)S(1)} collective-permute-done((bf16[192,2048]{1,0:T(8,128)(2,1)S(1)}, bf16[192,2048]{1,0:T(8,128)(2,1)S(1)}, u32[]{:S(2)}, u32[]{:S(2)}) %collective-permute-start.88) | collective-permute-done | bytes 786464 | tf_op jit(solution)/shard_map/ppermute | solution.py:34
  501.2 8.7 %attention_back.3 = (f32[512,384]{1,0:T(8,128)S(1)}, f32[512,384]{1,0:T(8,128)S(1)}, bf16[512,384]{1,0:T(8,128)(2,1)S(1)}) custom-call(bf16[128,1536]{1,0:T(8,128)(2,1)S(1)} %get-tuple-element.297.refs_0_.refs_2_, bf16[128,1536]{1,0:T(8,128)(2,1)S(1)} %collective-permute-done.84.refs_1_.refs_3_, ...), custom_call_target="tpu_custom_call" | custom-call | flops 60000002048 | bytes 8271872 | tf_op jit(solution)/shard_map/attention_back/pallas_call | solution.py:97
  524.2 5.9 collective-permute-done.92.refs_16_.refs_2_
  564.6 12.6 %collective-permute-done.103.refs_3_ = bf16[128,1536]{1,0:T(8,128)(2,1)S(1)} collective-permute-done((bf16[128,1536]{1,0:T(8,128)(2,1)S(1)}, bf16[128,1536]{1,0:T(8,128)(2,1)S(1)}, u32[]{:S(2)}, u32[]{:S(2)}) %collective-permute-start.103) | collective-permute-done | bytes 393248 | tf_op jit(solution)/shard_map/ppermute | solution.py:29
  592.2 12.8 %collective-permute-done.116.refs_1_ = f32[4,384]{1,0:T(4,128)S(1)} collective-permute-done((f32[4,384]{1,0:T(4,128)S(1)}, f32[4,384]{1,0:T(4,128)S(1)}, u32[]{:S(2)}, u32[]{:S(2)}) %collective-permute-start.116) | collective-permute-done | bytes 6176 | tf_op jit(solution)/shard_map/ppermute | solution.py:34
  613.6 6.8 %collective-permute-done.114.refs_2_ = bf16[192,1152]{1,0:T(8,128)(2,1)S(1)} collective-permute-done((bf16[192,1152]{1,0:T(8,128)(2,1)S(1)}, bf16[192,1152]{1,0:T(8,128)(2,1)S(1)}, u32[]{:S(2)}, u32[]{:S(2)}) %collective-permute-start.114) | collective-permute-done | bytes 442400 | tf_op jit(solution)/shard_map/ppermute | solution.py:34
  (690 shorter events, 341.3 us)
Async XLA Ops:
  12.7 48.3 %collective-permute-start.9 = (bf16[192,1152]{1,0:T(8,128)(2,1)}, bf16[192,1152]{1,0:T(8,128)(2,1)}, u32[]{:S(2)}, u32[]{:S(2)}) collective-permute-start(bf16[192,1152]{1,0:T(8,128)(2,1)} %get-tuple-element.374.refs_4_.refs_5_.refs_10_.refs_3_), channel_id=1, source_target_pairs={{0,16},{16,0},{1,17},{17,1},{2,18},{18,2},{3,19},{19,3},{4,20},{20... | collective-permute-start | bytes 1327112 | tf_op jit(solution)/shard_map/ppermute | solution.py:29
  39.7 21.3 %collective-permute-start.10 = (bf16[192,1152]{1,0:T(8,128)(2,1)}, bf16[192,1152]{1,0:T(8,128)(2,1)S(1)}, u32[]{:S(2)}, u32[]{:S(2)}) collective-permute-start(bf16[192,1152]{1,0:T(8,128)(2,1)} %collective-permute-done.1.refs_0_.refs_6_.refs_11_.refs_4_), channel_id=1, source_target_pairs={{0,16},{16,0},{1,17},{17,1},{2,18},{18,2},{3,19},{19,3},{4,20},{20... | collective-permute-start | bytes 1327112 | tf_op jit(solution)/shard_map/ppermute | solution.py:29
  49.9 41.2 %collective-permute-start.17 = (bf16[192,3072]{1,0:T(8,128)(2,1)S(1)}, bf16[192,3072]{1,0:T(8,128)(2,1)}, u32[]{:S(2)}, u32[]{:S(2)}) collective-permute-start(bf16[192,3072]{1,0:T(8,128)(2,1)S(1)} %get-tuple-element.211.refs_5_.refs_4_.refs_12_.refs_6_.refs_14_), channel_id=1, source_target_pairs={{0,12},{4,0},{8,4},{12,8},{1,13},{5,1},{9,5},{13,9},{2,14},{6,2},{... | collective-permute-start | bytes 3538952 | tf_op jit(solution)/shard_map/ppermute | solution.py:34
  65.7 25.5 %collective-permute-start.13 = (bf16[512,384]{1,0:T(8,128)(2,1)S(1)}, bf16[512,384]{1,0:T(8,128)(2,1)S(1)}, u32[]{:S(2)}, u32[]{:S(2)}) collective-permute-start(bf16[512,384]{1,0:T(8,128)(2,1)S(1)} %get-tuple-element.206.refs_1_.refs_5_), channel_id=1, source_target_pairs={{0,4},{4,0},{8,12},{12,8},{1,5},{5,1},{9,13},{13,9},{2,6},{6,2},{1... | collective-permute-start | bytes 1179656 | tf_op jit(solution)/shard_map/ppermute | solution.py:29
  91.2 30.9 %collective-permute-start.18 = (bf16[192,3072]{1,0:T(8,128)(2,1)}, bf16[192,3072]{1,0:T(8,128)(2,1)}, u32[]{:S(2)}, u32[]{:S(2)}) collective-permute-start(bf16[192,3072]{1,0:T(8,128)(2,1)} %collective-permute-done.17.refs_5_.refs_13_.refs_7_.refs_15_), channel_id=1, source_target_pairs={{0,12},{4,0},{8,4},{12,8},{1,13},{5,1},{9,5},{13,9},{2,14},{6,2},{... | collective-permute-start | bytes 3538952 | tf_op jit(solution)/shard_map/ppermute | solution.py:34
  106.7 20.8 %collective-permute-start.15 = (bf16[128,1536]{1,0:T(8,128)(2,1)}, bf16[128,1536]{1,0:T(8,128)(2,1)S(1)}, u32[]{:S(2)}, u32[]{:S(2)}) collective-permute-start(bf16[128,1536]{1,0:T(8,128)(2,1)} %get-tuple-element.209), channel_id=1, source_target_pairs={{0,2},{1,3},{2,0},{3,1},{4,6},{5,7},{6,4},{7,5},{8,10},{9,11},{10,... | collective-permute-start | bytes 1179656 | tf_op jit(solution)/shard_map/ppermute | solution.py:29
  117.6 30.2 %collective-permute-start.27 = (bf16[192,1152]{1,0:T(8,128)(2,1)}, bf16[192,1152]{1,0:T(8,128)(2,1)S(1)}, u32[]{:S(2)}, u32[]{:S(2)}) collective-permute-start(bf16[192,1152]{1,0:T(8,128)(2,1)} %get-tuple-element.216.refs_5_.refs_10_.refs_3_), channel_id=1, source_target_pairs={{0,12},{4,0},{8,4},{12,8},{1,13},{5,1},{9,5},{13,9},{2,14},{6,2},{... | collective-permute-start | bytes 1327112 | tf_op jit(solution)/shard_map/ppermute | solution.py:34
  122.1 34.8 %collective-permute-start.22 = (bf16[192,3072]{1,0:T(8,128)(2,1)}, bf16[192,3072]{1,0:T(8,128)(2,1)S(1)}, u32[]{:S(2)}, u32[]{:S(2)}) collective-permute-start(bf16[192,3072]{1,0:T(8,128)(2,1)} %collective-permute-done.18.refs_6_.refs_14_.refs_8_.refs_16_), channel_id=1, source_target_pairs={{0,12},{4,0},{8,4},{12,8},{1,13},{5,1},{9,5},{13,9},{2,14},{6,2},{... | collective-permute-start | bytes 3538952 | tf_op jit(solution)/shard_map/ppermute | solution.py:34
  156.9 34.8 %collective-permute-start.31 = (bf16[192,3072]{1,0:T(8,128)(2,1)S(1)}, bf16[192,3072]{1,0:T(8,128)(2,1)}, u32[]{:S(2)}, u32[]{:S(2)}) collective-permute-start(bf16[192,3072]{1,0:T(8,128)(2,1)S(1)} %copy-done.36), channel_id=1, source_target_pairs={{0,12},{4,0},{8,4},{12,8},{1,13},{5,1},{9,5},{13,9},{2,14},{6,2},{... | collective-permute-start | bytes 3538952 | tf_op jit(solution)/shard_map/ppermute | solution.py:34
  182.9 30.6 %collective-permute-start.36 = (bf16[192,1152]{1,0:T(8,128)(2,1)}, bf16[192,1152]{1,0:T(8,128)(2,1)}, u32[]{:S(2)}, u32[]{:S(2)}) collective-permute-start(bf16[192,1152]{1,0:T(8,128)(2,1)} %collective-permute-done.32.refs_6_.refs_7_.refs_12_.refs_5_), channel_id=1, source_target_pairs={{0,12},{4,0},{8,4},{12,8},{1,13},{5,1},{9,5},{13,9},{2,14},{6,2},{... | collective-permute-start | bytes 1327112 | tf_op jit(solution)/shard_map/ppermute | solution.py:34
  233.0 28.3 %collective-permute-start.45 = (bf16[192,3072]{1,0:T(8,128)(2,1)}, bf16[192,3072]{1,0:T(8,128)(2,1)}, u32[]{:S(2)}, u32[]{:S(2)}) collective-permute-start(bf16[192,3072]{1,0:T(8,128)(2,1)} %collective-permute-done.31.refs_5_.refs_13_.refs_7_.refs_15_), channel_id=1, source_target_pairs={{0,12},{4,0},{8,4},{12,8},{1,13},{5,1},{9,5},{13,9},{2,14},{6,2},{... | collective-permute-start | bytes 3538952 | tf_op jit(solution)/shard_map/ppermute | solution.py:34
  261.3 28.3 %collective-permute-start.49 = (bf16[192,3072]{1,0:T(8,128)(2,1)}, bf16[192,3072]{1,0:T(8,128)(2,1)S(1)}, u32[]{:S(2)}, u32[]{:S(2)}) collective-permute-start(bf16[192,3072]{1,0:T(8,128)(2,1)} %collective-permute-done.45.refs_6_.refs_14_.refs_8_.refs_16_), channel_id=1, source_target_pairs={{0,12},{4,0},{8,4},{12,8},{1,13},{5,1},{9,5},{13,9},{2,14},{6,2},{... | collective-permute-start | bytes 3538952 | tf_op jit(solution)/shard_map/ppermute | solution.py:34
  333.3 22.2 %collective-permute-start.61 = (bf16[192,2048]{1,0:T(8,128)(2,1)S(1)}, bf16[192,2048]{1,0:T(8,128)(2,1)S(1)}, u32[]{:S(2)}, u32[]{:S(2)}) collective-permute-start(bf16[192,2048]{1,0:T(8,128)(2,1)S(1)} %add_slots.24), channel_id=1, source_target_pairs={{0,4},{4,8},{8,12},{12,0},{1,5},{5,9},{9,13},{13,1},{2,6},{6,10},{... | collective-permute-start | bytes 2359304 | tf_op jit(solution)/shard_map/ppermute | solution.py:34
  334.9 21.2 %collective-permute-start.58 = (bf16[128,1536]{1,0:T(8,128)(2,1)S(1)}, bf16[128,1536]{1,0:T(8,128)(2,1)S(1)}, u32[]{:S(2)}, u32[]{:S(2)}) collective-permute-start(bf16[128,1536]{1,0:T(8,128)(2,1)S(1)} %get-tuple-element.246.refs_0_.refs_2_), channel_id=1, source_target_pairs={{0,2},{1,3},{2,0},{3,1},{4,6},{5,7},{6,4},{7,5},{8,10},{9,11},{10,... | collective-permute-start | bytes 1179656 | tf_op jit(solution)/shard_map/ppermute | solution.py:29
  346.6 27.5 %collective-permute-start.67 = (bf16[192,1024]{1,0:T(8,128)(2,1)S(1)}, bf16[192,1024]{1,0:T(8,128)(2,1)S(1)}, u32[]{:S(2)}, u32[]{:S(2)}) collective-permute-start(bf16[192,1024]{1,0:T(8,128)(2,1)S(1)} %add_slots.26), channel_id=1, source_target_pairs={{0,4},{4,8},{8,12},{12,0},{1,5},{5,9},{9,13},{13,1},{2,6},{6,10},{... | collective-permute-start | bytes 1179656 | tf_op jit(solution)/shard_map/ppermute | solution.py:34
  377.2 20.7 %collective-permute-start.72 = (bf16[192,1024]{1,0:T(8,128)(2,1)S(1)}, bf16[192,1024]{1,0:T(8,128)(2,1)S(1)}, u32[]{:S(2)}, u32[]{:S(2)}) collective-permute-start(bf16[192,1024]{1,0:T(8,128)(2,1)S(1)} %add_slots.27.refs_19_), channel_id=1, source_target_pairs={{0,4},{4,8},{8,12},{12,0},{1,5},{5,9},{9,13},{13,1},{2,6},{6,10},{... | collective-permute-start | bytes 1179656 | tf_op jit(solution)/shard_map/ppermute | solution.py:34
  377.5 27.7 %collective-permute-start.71 = (bf16[192,2048]{1,0:T(8,128)(2,1)S(1)}, bf16[192,2048]{1,0:T(8,128)(2,1)S(1)}, u32[]{:S(2)}, u32[]{:S(2)}) collective-permute-start(bf16[192,2048]{1,0:T(8,128)(2,1)S(1)} %add_slots.25.refs_20_), channel_id=1, source_target_pairs={{0,4},{4,8},{8,12},{12,0},{1,5},{5,9},{9,13},{13,1},{2,6},{6,10},{... | collective-permute-start | bytes 2359304 | tf_op jit(solution)/shard_map/ppermute | solution.py:34
  405.8 22.3 %collective-permute-start.76 = (bf16[192,2048]{1,0:T(8,128)(2,1)S(1)}, bf16[192,2048]{1,0:T(8,128)(2,1)S(1)}, u32[]{:S(2)}, u32[]{:S(2)}) collective-permute-start(bf16[192,2048]{1,0:T(8,128)(2,1)S(1)} %add_slots.28.refs_7_), channel_id=1, source_target_pairs={{0,4},{4,8},{8,12},{12,0},{1,5},{5,9},{9,13},{13,1},{2,6},{6,10},{... | collective-permute-start | bytes 2359304 | tf_op jit(solution)/shard_map/ppermute | solution.py:34
  411.8 25.9 %collective-permute-start.78 = (bf16[192,1152]{1,0:T(8,128)(2,1)S(1)}, bf16[192,1152]{1,0:T(8,128)(2,1)S(1)}, u32[]{:S(2)}, u32[]{:S(2)}) collective-permute-start(bf16[192,1152]{1,0:T(8,128)(2,1)S(1)} %add_slots.31), channel_id=1, source_target_pairs={{0,4},{4,8},{8,12},{12,0},{1,5},{5,9},{9,13},{13,1},{2,6},{6,10},{... | collective-permute-start | bytes 1327112 | tf_op jit(solution)/shard_map/ppermute | solution.py:34
  413.2 24.7 %collective-permute-start.74 = (bf16[128,1536]{1,0:T(8,128)(2,1)S(1)}, bf16[128,1536]{1,0:T(8,128)(2,1)S(1)}, u32[]{:S(2)}, u32[]{:S(2)}) collective-permute-start(bf16[128,1536]{1,0:T(8,128)(2,1)S(1)} %get-tuple-element.310.refs_0_.refs_6_), channel_id=1, source_target_pairs={{0,2},{1,3},{2,0},{3,1},{4,6},{5,7},{6,4},{7,5},{8,10},{9,11},{10,... | collective-permute-start | bytes 1179656 | tf_op jit(solution)/shard_map/ppermute | solution.py:29
  414.6 23.3 %collective-permute-start.73 = (bf16[128,1536]{1,0:T(8,128)(2,1)S(1)}, bf16[128,1536]{1,0:T(8,128)(2,1)S(1)}, u32[]{:S(2)}, u32[]{:S(2)}) collective-permute-start(bf16[128,1536]{1,0:T(8,128)(2,1)S(1)} %get-tuple-element.310.refs_0_.refs_6_), channel_id=1, source_target_pairs={{0,1},{1,0},{2,3},{3,2},{4,5},{5,4},{6,7},{7,6},{8,9},{9,8},{10,11... | collective-permute-start | bytes 1179656 | tf_op jit(solution)/shard_map/ppermute | solution.py:29
  423.2 35.3 %collective-permute-start.83 = (bf16[192,1024]{1,0:T(8,128)(2,1)}, bf16[192,1024]{1,0:T(8,128)(2,1)S(1)}, u32[]{:S(2)}, u32[]{:S(2)}) collective-permute-start(bf16[192,1024]{1,0:T(8,128)(2,1)} %add_slots.29.refs_8_), channel_id=1, source_target_pairs={{0,4},{4,8},{8,12},{12,0},{1,5},{5,9},{9,13},{13,1},{2,6},{6,10},{... | collective-permute-start | bytes 1179656 | tf_op jit(solution)/shard_map/ppermute | solution.py:34
  467.7 31.3 %collective-permute-start.88 = (bf16[192,2048]{1,0:T(8,128)(2,1)S(1)}, bf16[192,2048]{1,0:T(8,128)(2,1)S(1)}, u32[]{:S(2)}, u32[]{:S(2)}) collective-permute-start(bf16[192,2048]{1,0:T(8,128)(2,1)S(1)} %add_slots.35), channel_id=1, source_target_pairs={{0,4},{4,8},{8,12},{12,0},{1,5},{5,9},{9,13},{13,1},{2,6},{6,10},{... | collective-permute-start | bytes 2359304 | tf_op jit(solution)/shard_map/ppermute | solution.py:34
  467.8 32.0 %collective-permute-start.85 = (bf16[128,1536]{1,0:T(8,128)(2,1)S(1)}, bf16[128,1536]{1,0:T(8,128)(2,1)S(1)}, u32[]{:S(2)}, u32[]{:S(2)}) collective-permute-start(bf16[128,1536]{1,0:T(8,128)(2,1)S(1)} %get-tuple-element.297.refs_0_.refs_2_), channel_id=1, source_target_pairs={{0,2},{1,3},{2,0},{3,1},{4,6},{5,7},{6,4},{7,5},{8,10},{9,11},{10,... | collective-permute-start | bytes 1179656 | tf_op jit(solution)/shard_map/ppermute | solution.py:29
  478.2 21.6 %collective-permute-start.84 = (bf16[128,1536]{1,0:T(8,128)(2,1)S(1)}, bf16[128,1536]{1,0:T(8,128)(2,1)S(1)}, u32[]{:S(2)}, u32[]{:S(2)}) collective-permute-start(bf16[128,1536]{1,0:T(8,128)(2,1)S(1)} %get-tuple-element.297.refs_0_.refs_2_), channel_id=1, source_target_pairs={{0,1},{1,0},{2,3},{3,2},{4,5},{5,4},{6,7},{7,6},{8,9},{9,8},{10,11... | collective-permute-start | bytes 1179656 | tf_op jit(solution)/shard_map/ppermute | solution.py:29
  482.5 34.8 %collective-permute-start.95 = (bf16[192,1024]{1,0:T(8,128)(2,1)S(1)}, bf16[192,1024]{1,0:T(8,128)(2,1)S(1)}, u32[]{:S(2)}, u32[]{:S(2)}) collective-permute-start(bf16[192,1024]{1,0:T(8,128)(2,1)S(1)} %add_slots.38), channel_id=1, source_target_pairs={{0,4},{4,8},{8,12},{12,0},{1,5},{5,9},{9,13},{13,1},{2,6},{6,10},{... | collective-permute-start | bytes 1179656 | tf_op jit(solution)/shard_map/ppermute | solution.py:34
  519.9 22.6 %collective-permute-start.102 = (bf16[192,1024]{1,0:T(8,128)(2,1)S(1)}, bf16[192,1024]{1,0:T(8,128)(2,1)S(1)}, u32[]{:S(2)}, u32[]{:S(2)}) collective-permute-start(bf16[192,1024]{1,0:T(8,128)(2,1)S(1)} %add_slots.39.refs_19_), channel_id=1, source_target_pairs={{0,4},{4,8},{8,12},{12,0},{1,5},{5,9},{9,13},{13,1},{2,6},{6,10},{... | collective-permute-start | bytes 1179656 | tf_op jit(solution)/shard_map/ppermute | solution.py:34
  520.3 27.0 %collective-permute-start.101 = (bf16[192,2048]{1,0:T(8,128)(2,1)S(1)}, bf16[192,2048]{1,0:T(8,128)(2,1)S(1)}, u32[]{:S(2)}, u32[]{:S(2)}) collective-permute-start(bf16[192,2048]{1,0:T(8,128)(2,1)S(1)} %add_slots.36.refs_20_), channel_id=1, source_target_pairs={{0,4},{4,8},{8,12},{12,0},{1,5},{5,9},{9,13},{13,1},{2,6},{6,10},{... | collective-permute-start | bytes 2359304 | tf_op jit(solution)/shard_map/ppermute | solution.py:34
  547.8 29.4 %collective-permute-start.106 = (bf16[192,2048]{1,0:T(8,128)(2,1)S(1)}, bf16[192,2048]{1,0:T(8,128)(2,1)S(1)}, u32[]{:S(2)}, u32[]{:S(2)}) collective-permute-start(bf16[192,2048]{1,0:T(8,128)(2,1)S(1)} %add_slots.41.refs_7_), channel_id=1, source_target_pairs={{0,4},{4,8},{8,12},{12,0},{1,5},{5,9},{9,13},{13,1},{2,6},{6,10},{... | collective-permute-start | bytes 2359304 | tf_op jit(solution)/shard_map/ppermute | solution.py:34
  556.5 21.5 %collective-permute-start.105 = (bf16[128,1536]{1,0:T(8,128)(2,1)S(1)}, bf16[128,1536]{1,0:T(8,128)(2,1)S(1)}, u32[]{:S(2)}, u32[]{:S(2)}) collective-permute-start(bf16[128,1536]{1,0:T(8,128)(2,1)S(1)} %get-tuple-element.338.refs_0_), channel_id=1, source_target_pairs={{0,2},{1,3},{2,0},{3,1},{4,6},{5,7},{6,4},{7,5},{8,10},{9,11},{10,... | collective-permute-start | bytes 1179656 | tf_op jit(solution)/shard_map/ppermute | solution.py:29
  557.2 20.8 %collective-permute-start.104 = (bf16[128,1536]{1,0:T(8,128)(2,1)S(1)}, bf16[128,1536]{1,0:T(8,128)(2,1)S(1)}, u32[]{:S(2)}, u32[]{:S(2)}) collective-permute-start(bf16[128,1536]{1,0:T(8,128)(2,1)S(1)} %get-tuple-element.338.refs_0_), channel_id=1, source_target_pairs={{0,1},{1,0},{2,3},{3,2},{4,5},{5,4},{6,7},{7,6},{8,9},{9,8},{10,11... | collective-permute-start | bytes 1179656 | tf_op jit(solution)/shard_map/ppermute | solution.py:29
  584.2 21.4 %collective-permute-start.108 = (bf16[192,1024]{1,0:T(8,128)(2,1)S(1)}, bf16[192,1024]{1,0:T(8,128)(2,1)S(1)}, u32[]{:S(2)}, u32[]{:S(2)}) collective-permute-start(bf16[192,1024]{1,0:T(8,128)(2,1)S(1)} %add_slots.42.refs_8_), channel_id=1, source_target_pairs={{0,4},{4,8},{8,12},{12,0},{1,5},{5,9},{9,13},{13,1},{2,6},{6,10},{... | collective-permute-start | bytes 1179656 | tf_op jit(solution)/shard_map/ppermute | solution.py:34
  (266 other events, 2822.7 us)

commit v4 on v3

--- a/solution.py
+++ b/solution.py
@@ -21,6 +21,7 @@
 ANYWHERE = pl.BlockSpec(memory_space=pl.ANY)
 FAR = pl.BlockSpec(memory_space=pltpu.HBM)
 FETCHED = object()
+NEAR = object()
 SCALAR = pl.BlockSpec(memory_space=pltpu.SMEM)
 
 
@@ -59,10 +60,10 @@
     for group in ins:
         sizes.append(len(group))
         for array, spec in group:
-            if spec is FETCHED:
+            if spec is FETCHED or spec is NEAR:
                 fetched.append(len(arrays))
             arrays.append(array)
-            specs.append(ANYWHERE if spec is FETCHED else spec)
+            specs.append(FAR if spec is FETCHED else ANYWHERE if spec is NEAR else spec)
     count = len(arrays)
     after = list(after)
     arrays += after
@@ -969,13 +970,13 @@
         s_f = Scatter([(n2, grad_gu)], units // 2)
         come += s_f.made
         s_f.begin(sent[-1])
-        if s_a:
-            s_a.begin(sent[-1])
         g_gain2, grad_middle, grad_attn = norm_back(middle, sent, gain2, grad[0], come)
         s_d = Scatter([(grad, behind(hidden, grad_attn))], units // 2)
         grad_attn = gather_pieces(grad_attn)
-        come = s_d.made + s_f.finish(grad_attn[-1]) + (s_a.finish(grad_attn[-1]) if s_a else [])
+        come = s_d.made + s_f.finish(grad_attn[-1])
         s_d.begin(grad_attn[-1])
+        if s_a:
+            s_a.begin(grad_attn[-1])
         grad_query, grad_own, grad_there = attention_back(
             grad_attn, query, own, there, sums, orders, a.all(), come
         )
@@ -984,11 +985,12 @@
             left[0] = leave([behind(p, grad_there) for p in outs[0]], back_order, c_here)
             come = last_y[1:] + [left[0]]
         else:
-            outs.append(gather_pieces(add_up(kept[1][7], last_y, grad_attn[-1:])))
+            last_y = add_up(kept[1][7], last_y, [grad_attn[0]])
+            outs.append(gather_pieces(behind(last_y, grad_attn[-1])))
             left[1] = leave([behind(p, grad_there) for p in grad], back_order, c_here)
             come = outs[1][1:] + [left[1]]
         back = mate(grad_there, "row", 1)
-        come += s_d.finish(back)
+        come += s_d.finish(back) + (s_a.finish(back) if s_a else [])
         s_f.begin(back)
         s_d.begin(back)
         y, grad_qkv = project_back(
@@ -1007,7 +1009,9 @@
         gain_parts[layer] = (g_gain1, g_gain2)
 
     acts = [left[0], leave([behind(p, *mark) for p in outs[1]], back_order, c_here)]
-    point = meet(grad[1:] + acts[1:] + come + mark)
+    gain_grads = jnp.concatenate(list(gain_parts[0]) + list(gain_parts[1]), 0)
+    gain_slots = gather_gains(gain_grads, s_here)
+    point = meet(grad[1:] + acts[1:] + come + mark + gain_slots)
     s_a.begin(*point)
     s_d.begin(*point)
     mark = meet(point)
@@ -1016,16 +1020,14 @@
     acts_got = exchange([behind(v, *mark) for v in acts])
     wide = [p[1].moving for p in parts]
     wide_got = exchange([behind(v, *mark) for v in wide])
-    gain_grads = jnp.concatenate(list(gain_parts[0]) + list(gain_parts[1]), 0)
-    gain_slots = gather_gains(behind(gain_grads, grads[0]), s_here)
-    point = meet(s_a.finish(grads[0]) + s_d.finish(grads[0]) + gain_slots + mark)
+    gain_grads = reduce_gains([behind(v, *mark) for v in gain_slots], s_here)
+    point = meet(s_a.finish(grads[0]) + s_d.finish(grads[0]) + gain_grads + mark)
     s_a.begin(*point)
     mark = meet(point)
     acts = place_out([behind(v, *mark) for v in acts], acts_got, s_here)
     grads = place_out([behind(v, *mark) for v in grads], grads_got, s_here)
     g_gate, g_up = unpack([behind(v, *mark) for v in wide], wide_got, s_here, (units, units))
-    gain_grads = reduce_gains(gain_slots, s_here)
-    s_a.finish(grads, acts, g_up, *gain_grads)
+    s_a.finish(grads, acts, g_up)
     gain_grads = gain_grads[0] + mate(gain_grads[1], "section", 1)
     heads, narrow = ([p[k].moving for p in parts] for k in (0, 2))
     heads_got, narrow_got = exchange(heads), exchange(narrow)

time: 637 us -> 631 us (level)
  waiting for transfers between devices: 295 us -> 286 us
    ppermute x86, waiting for transfers between devices: 198 us -> 184 us  [mate(): return lax.ppermute(x, axis, [(j, j ^ k) for j in range(n)])]
  transfers between devices with their start and end apart: 122 -> 122, of which waited for: 61 -> 56; matrix products, arithmetic and copies ran while one was open for 2% -> 3% of each run, Pallas kernels for 22% -> 22%
where the time goes in v4:
time: 631 us; the launch traced here: 625 us
  waiting for transfers between devices  286 us (45%)
  Pallas kernels  163 us (26%)
  starting transfers between devices  120 us (19%)
  local copies, waits for them, and re-layouts  40.7 us (6%)
  other arithmetic  11.6 us (2%)
    ppermute x86, waiting for transfers between devices, mate(): return lax.ppermute(x, axis, [(j, j ^ k) for j in range(n)])  184 us
    pallas_call x82, Pallas kernels, kernel(): pl.pallas_call(run, grid=grid, in_specs=specs, out_specs=[spec for _, spe...  163 us
    ppermute x36, waiting for transfers between devices, ring(): return lax.ppermute(x, 'row', [(j, (j + by) % n) for j in range(n)])  101 us
    ppermute x86, starting transfers between devices, mate(): return lax.ppermute(x, axis, [(j, j ^ k) for j in range(n)])  64 us
    ppermute x36, starting transfers between devices, ring(): return lax.ppermute(x, 'row', [(j, (j + by) % n) for j in range(n)])  56.1 us
    unnamed x352, local copies, waits for them, and re-layouts  34.4 us
  transfers between devices with their start and end apart: 122, of which 56 were waited for; matrix products, arithmetic and copies ran while one was open for 3% of the time, Pallas kernels for 22%

profile of v4, /device:TPU:0, one launch (start us, length us, event | category | flops | bytes accessed | tf_op | source)
XLA Modules:
  0.0 625.1 jit_solution(5531265943796209814)
XLA Ops:
  50.2 7.6 %collective-permute-done.8.refs_8_.refs_13_.refs_6_ = bf16[192,1152]{1,0:T(8,128)(2,1)S(1)} collective-permute-done((bf16[192,1152]{1,0:T(8,128)(2,1)S(1)}, bf16[192,1152]{1,0:T(8,128)(2,1)S(1)}, u32[]{:S(2)}, u32[]{:S(2)}) %collective-permute-start.8) | collective-permute-done | bytes 442400 | tf_op jit(solution)/shard_map/ppermute | solution.py:35
  65.8 25.3 %collective-permute-done.13.refs_2_.refs_6_ = bf16[512,384]{1,0:T(8,128)(2,1)S(1)} collective-permute-done((bf16[512,384]{1,0:T(8,128)(2,1)S(1)}, bf16[512,384]{1,0:T(8,128)(2,1)S(1)}, u32[]{:S(2)}, u32[]{:S(2)}) %collective-permute-start.13) | collective-permute-done | bytes 393248 | tf_op jit(solution)/shard_map/ppermute | solution.py:30
  95.5 6.8 %attention.2 = (bf16[512,384]{1,0:T(8,128)(2,1)S(1)}, f32[4,512]{1,0:T(4,128)S(1)}, bf16[128,1536]{1,0:T(8,128)(2,1)S(1)}, bf16[128,1536]{1,0:T(8,128)(2,1)}, bf...) custom-call(bf16[512,384]{1,0:T(8,128)(2,1)S(1)} %get-tuple-element.209.refs_0_.refs_4_, ...), custom_call_target="tpu_custom_call" | custom-call | flops 60000002048 | bytes 6699008 | tf_op jit(solution)/shard_map/attention/pallas_call | solution.py:98
  107.3 9.6 %collective-permute-done.16.refs_4_ = bf16[128,1536]{1,0:T(8,128)(2,1)S(1)} collective-permute-done((bf16[128,1536]{1,0:T(8,128)(2,1)}, bf16[128,1536]{1,0:T(8,128)(2,1)S(1)}, u32[]{:S(2)}, u32[]{:S(2)}) %collective-permute-start.16) | collective-permute-done | bytes 393248 | tf_op jit(solution)/shard_map/ppermute | solution.py:30
  138.3 9.5 %collective-permute-done.21.refs_2_.refs_3_ = bf16[128,1536]{1,0:T(8,128)(2,1)S(1)} collective-permute-done((bf16[128,1536]{1,0:T(8,128)(2,1)S(1)}, bf16[128,1536]{1,0:T(8,128)(2,1)S(1)}, u32[]{:S(2)}, u32[]{:S(2)}) %collective-permute-start.21) | collective-permute-done | bytes 393248 | tf_op jit(solution)/shard_map/ppermute | solution.py:30
  161.2 7.7 %feed_forward.2 = (bf16[512,1024]{1,0:T(8,128)(2,1)S(1)}, bf16[512,1024]{1,0:T(8,128)(2,1)S(1)}, bf16[512,1024]{1,0:T(8,128)(2,1)S(1)}, bf16[128,1536]{1,0:T(8,1...) custom-call(bf16[128,1536]{1,0:T(8,128)(2,1)S(1)} %get-tuple-element.218.r, ...), custom_call_target="tpu_custom_call" | custom-call | flops 60000002048 | bytes 25165824 | tf_op jit(solution)/shard_map/feed_forward/pallas_call | solution.py:98
  173.5 9.4 %collective-permute-done.30.refs_4_ = bf16[128,1536]{1,0:T(8,128)(2,1)S(1)} collective-permute-done((bf16[128,1536]{1,0:T(8,128)(2,1)S(1)}, bf16[128,1536]{1,0:T(8,128)(2,1)S(1)}, u32[]{:S(2)}, u32[]{:S(2)}) %collective-permute-start.30) | collective-permute-done | bytes 393248 | tf_op jit(solution)/shard_map/ppermute | solution.py:30
  185.5 6.1 collective-permute-done.31.refs_5_.refs_13_.refs_7_.refs_15_
  207.0 6.5 %collective-permute-done.34.refs_1_.refs_2_ = bf16[128,1536]{1,0:T(8,128)(2,1)} collective-permute-done((bf16[128,1536]{1,0:T(8,128)(2,1)}, bf16[128,1536]{1,0:T(8,128)(2,1)}, u32[]{:S(2)}, u32[]{:S(2)}) %collective-permute-start.34) | collective-permute-done | bytes 393248 | tf_op jit(solution)/shard_map/ppermute | solution.py:30
  216.2 5.6 project.3
  221.9 11.1 %collective-permute-done.41.refs_2_.refs_6_ = bf16[512,384]{1,0:T(8,128)(2,1)S(1)} collective-permute-done((bf16[512,384]{1,0:T(8,128)(2,1)S(1)}, bf16[512,384]{1,0:T(8,128)(2,1)S(1)}, u32[]{:S(2)}, u32[]{:S(2)}) %collective-permute-start.41) | collective-permute-done | bytes 393248 | tf_op jit(solution)/shard_map/ppermute | solution.py:30
  236.4 6.8 %attention.3 = (bf16[512,384]{1,0:T(8,128)(2,1)S(1)}, f32[4,512]{1,0:T(4,128)S(1)}, bf16[128,1536]{1,0:T(8,128)(2,1)S(1)}, bf16[128,1536]{1,0:T(8,128)(2,1)}, bf...) custom-call(bf16[512,384]{1,0:T(8,128)(2,1)S(1)} %get-tuple-element.229.refs_0_.refs_4_, ...), custom_call_target="tpu_custom_call" | custom-call | flops 60000002048 | bytes 6699008 | tf_op jit(solution)/shard_map/attention/pallas_call | solution.py:98
  250.2 8.4 %collective-permute-done.44.refs_4_ = bf16[128,1536]{1,0:T(8,128)(2,1)} collective-permute-done((bf16[128,1536]{1,0:T(8,128)(2,1)}, bf16[128,1536]{1,0:T(8,128)(2,1)}, u32[]{:S(2)}, u32[]{:S(2)}) %collective-permute-start.44) | collective-permute-done | bytes 393248 | tf_op jit(solution)/shard_map/ppermute | solution.py:30
  273.2 9.5 %collective-permute-done.48.refs_2_.refs_3_ = bf16[128,1536]{1,0:T(8,128)(2,1)S(1)} collective-permute-done((bf16[128,1536]{1,0:T(8,128)(2,1)S(1)}, bf16[128,1536]{1,0:T(8,128)(2,1)S(1)}, u32[]{:S(2)}, u32[]{:S(2)}) %collective-permute-start.48) | collective-permute-done | bytes 393248 | tf_op jit(solution)/shard_map/ppermute | solution.py:30
  282.7 6.7 %collective-permute-done.47.refs_1_.refs_2_ = bf16[128,1536]{1,0:T(8,128)(2,1)S(1)} collective-permute-done((bf16[128,1536]{1,0:T(8,128)(2,1)S(1)}, bf16[128,1536]{1,0:T(8,128)(2,1)S(1)}, u32[]{:S(2)}, u32[]{:S(2)}) %collective-permute-start.47) | collective-permute-done | bytes 393248 | tf_op jit(solution)/shard_map/ppermute | solution.py:30
  293.9 7.1 %feed_forward.3 = (bf16[512,1024]{1,0:T(8,128)(2,1)S(1)}, bf16[512,1024]{1,0:T(8,128)(2,1)S(1)}, bf16[512,1024]{1,0:T(8,128)(2,1)S(1)}, bf16[128,1536]{1,0:T(8,1...) custom-call(bf16[128,1536]{1,0:T(8,128)(2,1)S(1)} %get-tuple-element.240.r, ...), custom_call_target="tpu_custom_call" | custom-call | flops 60000002048 | bytes 25165824 | tf_op jit(solution)/shard_map/feed_forward/pallas_call | solution.py:98
  301.0 7.3 %feed_forward_back.2 = (bf16[512,2048]{1,0:T(8,128)(2,1)S(1)}, bf16[128,1536]{1,0:T(8,128)(2,1)S(1)}, bf16[128,1536]{1,0:T(8,128)(2,1)S(1)}, bf16[128,1536]{1,0:T(8,128)(2,1)S(1)}, bf16[128,1536]{1,0:T(8,128)(2,1)S(1)}) custom-call(bf16[128,1536]{1,0:T(8,128)(2,1)S(1)} %copy-done.17, bf16[128,1536]{1,0:T(8,128)(2,1)S(1)} %copy-done.19, ...), custom_call_target="tpu_custom_call" | custom-call | flops 60000002048 | bytes 26214400 | tf_op jit(solution)/shard_map/feed_forward_back/pallas_call | solution.py:98
  320.4 8.8 %collective-permute-done.55.refs_3_ = bf16[128,1536]{1,0:T(8,128)(2,1)S(1)} collective-permute-done((bf16[128,1536]{1,0:T(8,128)(2,1)S(1)}, bf16[128,1536]{1,0:T(8,128)(2,1)S(1)}, u32[]{:S(2)}, u32[]{:S(2)}) %collective-permute-start.55) | collective-permute-done | bytes 393248 | tf_op jit(solution)/shard_map/ppermute | solution.py:30
  338.7 7.6 %collective-permute-done.59.refs_3_.refs_2_.refs_5_ = bf16[128,1536]{1,0:T(8,128)(2,1)S(1)} collective-permute-done((bf16[128,1536]{1,0:T(8,128)(2,1)S(1)}, bf16[128,1536]{1,0:T(8,128)(2,1)S(1)}, u32[]{:S(2)}, u32[]{:S(2)}) %collective-permute-start.59) | collective-permute-done | bytes 393248 | tf_op jit(solution)/shard_map/ppermute | solution.py:30
  346.9 8.6 %collective-permute-done.61.refs_2_ = bf16[192,2048]{1,0:T(8,128)(2,1)S(1)} collective-permute-done((bf16[192,2048]{1,0:T(8,128)(2,1)S(1)}, bf16[192,2048]{1,0:T(8,128)(2,1)S(1)}, u32[]{:S(2)}, u32[]{:S(2)}) %collective-permute-start.61) | collective-permute-done | bytes 786464 | tf_op jit(solution)/shard_map/ppermute | solution.py:35
  357.4 9.0 %attention_back.2 = (f32[512,384]{1,0:T(8,128)S(1)}, f32[512,384]{1,0:T(8,128)S(1)}, bf16[512,384]{1,0:T(8,128)(2,1)S(1)}) custom-call(bf16[128,1536]{1,0:T(8,128)(2,1)S(1)} %get-tuple-element.250.refs_0_.refs_2_, bf16[128,1536]{1,0:T(8,128)(2,1)S(1)} %collective-permute-done.57.refs_1_.refs_3_, ...), custom_call_target="tpu_custom_call" | custom-call | flops 60000002048 | bytes 8271872 | tf_op jit(solution)/shard_map/attention_back/pallas_call | solution.py:98
  378.7 6.0 collective-permute-done.64.refs_16_.refs_3_
  415.3 7.9 %collective-permute-done.75.refs_3_ = bf16[128,1536]{1,0:T(8,128)(2,1)S(1)} collective-permute-done((bf16[128,1536]{1,0:T(8,128)(2,1)S(1)}, bf16[128,1536]{1,0:T(8,128)(2,1)S(1)}, u32[]{:S(2)}, u32[]{:S(2)}) %collective-permute-start.75) | collective-permute-done | bytes 393248 | tf_op jit(solution)/shard_map/ppermute | solution.py:30
  429.1 8.5 %collective-permute-done.78.refs_2_ = bf16[192,1152]{1,0:T(8,128)(2,1)S(1)} collective-permute-done((bf16[192,1152]{1,0:T(8,128)(2,1)S(1)}, bf16[192,1152]{1,0:T(8,128)(2,1)S(1)}, u32[]{:S(2)}, u32[]{:S(2)}) %collective-permute-start.78) | collective-permute-done | bytes 442400 | tf_op jit(solution)/shard_map/ppermute | solution.py:35
  441.3 7.3 %feed_forward_back.3 = (bf16[512,2048]{1,0:T(8,128)(2,1)S(1)}, bf16[128,1536]{1,0:T(8,128)(2,1)S(1)}, bf16[128,1536]{1,0:T(8,128)(2,1)S(1)}, bf16[128,1536]{1,0:T(8,128)(2,1)S(1)}, bf16[128,1536]{1,0:T(8,128)(2,1)S(1)}) custom-call(bf16[128,1536]{1,0:T(8,128)(2,1)S(1)} %get-tuple-element.314.refs_0_.refs_6_, ...), custom_call_target="tpu_custom_call" | custom-call | flops 60000002048 | bytes 26214400 | tf_op jit(solution)/shard_map/feed_forward_back/pallas_call | solution.py:98
  472.3 7.6 %collective-permute-done.86.refs_3_.refs_2_.refs_5_ = bf16[128,1536]{1,0:T(8,128)(2,1)S(1)} collective-permute-done((bf16[128,1536]{1,0:T(8,128)(2,1)S(1)}, bf16[128,1536]{1,0:T(8,128)(2,1)S(1)}, u32[]{:S(2)}, u32[]{:S(2)}) %collective-permute-start.86) | collective-permute-done | bytes 393248 | tf_op jit(solution)/shard_map/ppermute | solution.py:30
  491.4 8.7 %attention_back.3 = (f32[512,384]{1,0:T(8,128)S(1)}, f32[512,384]{1,0:T(8,128)S(1)}, bf16[512,384]{1,0:T(8,128)(2,1)S(1)}) custom-call(bf16[128,1536]{1,0:T(8,128)(2,1)S(1)} %get-tuple-element.301.refs_0_.refs_5_.refs_2_, bf16[128,1536]{1,0:T(8,128)(2,1)S(1)} %collective-permute-done.84.refs_1_.refs_3_, ...), custom_call_target="tpu_custom_call" | custom-call | flops 60000002048 | bytes 8271872 | tf_op jit(solution)/shard_map/attention_back/pallas_call | solution.py:98
  507.7 7.3 %collective-permute-done.89.refs_3_.refs_2_ = bf16[512,384]{1,0:T(8,128)(2,1)S(1)} collective-permute-done((bf16[512,384]{1,0:T(8,128)(2,1)S(1)}, bf16[512,384]{1,0:T(8,128)(2,1)S(1)}, u32[]{:S(2)}, u32[]{:S(2)}) %collective-permute-start.89) | collective-permute-done | bytes 393248 | tf_op jit(solution)/shard_map/ppermute | solution.py:30
  537.6 7.5 %collective-permute-done.101.refs_2_ = bf16[192,2048]{1,0:T(8,128)(2,1)S(1)} collective-permute-done((bf16[192,2048]{1,0:T(8,128)(2,1)S(1)}, bf16[192,2048]{1,0:T(8,128)(2,1)S(1)}, u32[]{:S(2)}, u32[]{:S(2)}) %collective-permute-start.101) | collective-permute-done | bytes 786464 | tf_op jit(solution)/shard_map/ppermute | solution.py:35
  559.4 6.3 %collective-permute-done.103.refs_3_ = bf16[128,1536]{1,0:T(8,128)(2,1)S(1)} collective-permute-done((bf16[128,1536]{1,0:T(8,128)(2,1)S(1)}, bf16[128,1536]{1,0:T(8,128)(2,1)S(1)}, u32[]{:S(2)}, u32[]{:S(2)}) %collective-permute-start.103) | collective-permute-done | bytes 393248 | tf_op jit(solution)/shard_map/ppermute | solution.py:30
  565.7 9.2 %collective-permute-done.106.refs_2_ = bf16[192,2048]{1,0:T(8,128)(2,1)S(1)} collective-permute-done((bf16[192,2048]{1,0:T(8,128)(2,1)S(1)}, bf16[192,2048]{1,0:T(8,128)(2,1)S(1)}, u32[]{:S(2)}, u32[]{:S(2)}) %collective-permute-start.106) | collective-permute-done | bytes 786464 | tf_op jit(solution)/shard_map/ppermute | solution.py:35
  575.5 6.2 collective-permute-done.98.refs_2_
  (690 shorter events, 353.8 us)
Async XLA Ops:
  12.7 48.3 %collective-permute-start.9 = (bf16[192,1152]{1,0:T(8,128)(2,1)}, bf16[192,1152]{1,0:T(8,128)(2,1)}, u32[]{:S(2)}, u32[]{:S(2)}) collective-permute-start(bf16[192,1152]{1,0:T(8,128)(2,1)} %get-tuple-element.382.refs_4_.refs_5_.refs_10_.refs_3_), channel_id=1, source_target_pairs={{0,16},{16,0},{1,17},{17,1},{2,18},{18,2},{3,19},{19,3},{4,20},{20... | collective-permute-start | bytes 1327112 | tf_op jit(solution)/shard_map/ppermute | solution.py:30
  39.7 21.3 %collective-permute-start.10 = (bf16[192,1152]{1,0:T(8,128)(2,1)}, bf16[192,1152]{1,0:T(8,128)(2,1)S(1)}, u32[]{:S(2)}, u32[]{:S(2)}) collective-permute-start(bf16[192,1152]{1,0:T(8,128)(2,1)} %collective-permute-done.1.refs_0_.refs_6_.refs_11_.refs_4_), channel_id=1, source_target_pairs={{0,16},{16,0},{1,17},{17,1},{2,18},{18,2},{3,19},{19,3},{4,20},{20... | collective-permute-start | bytes 1327112 | tf_op jit(solution)/shard_map/ppermute | solution.py:30
  49.9 41.2 %collective-permute-start.17 = (bf16[192,3072]{1,0:T(8,128)(2,1)S(1)}, bf16[192,3072]{1,0:T(8,128)(2,1)}, u32[]{:S(2)}, u32[]{:S(2)}) collective-permute-start(bf16[192,3072]{1,0:T(8,128)(2,1)S(1)} %get-tuple-element.215.refs_5_.refs_4_.refs_12_.refs_6_.refs_14_), channel_id=1, source_target_pairs={{0,12},{4,0},{8,4},{12,8},{1,13},{5,1},{9,5},{13,9},{2,14},{6,2},{... | collective-permute-start | bytes 3538952 | tf_op jit(solution)/shard_map/ppermute | solution.py:35
  65.7 25.5 %collective-permute-start.13 = (bf16[512,384]{1,0:T(8,128)(2,1)S(1)}, bf16[512,384]{1,0:T(8,128)(2,1)S(1)}, u32[]{:S(2)}, u32[]{:S(2)}) collective-permute-start(bf16[512,384]{1,0:T(8,128)(2,1)S(1)} %get-tuple-element.210.refs_1_.refs_5_), channel_id=1, source_target_pairs={{0,4},{4,0},{8,12},{12,8},{1,5},{5,1},{9,13},{13,9},{2,6},{6,2},{1... | collective-permute-start | bytes 1179656 | tf_op jit(solution)/shard_map/ppermute | solution.py:30
  91.2 30.9 %collective-permute-start.18 = (bf16[192,3072]{1,0:T(8,128)(2,1)}, bf16[192,3072]{1,0:T(8,128)(2,1)}, u32[]{:S(2)}, u32[]{:S(2)}) collective-permute-start(bf16[192,3072]{1,0:T(8,128)(2,1)} %collective-permute-done.17.refs_5_.refs_13_.refs_7_.refs_15_), channel_id=1, source_target_pairs={{0,12},{4,0},{8,4},{12,8},{1,13},{5,1},{9,5},{13,9},{2,14},{6,2},{... | collective-permute-start | bytes 3538952 | tf_op jit(solution)/shard_map/ppermute | solution.py:35
  106.7 20.8 %collective-permute-start.15 = (bf16[128,1536]{1,0:T(8,128)(2,1)}, bf16[128,1536]{1,0:T(8,128)(2,1)S(1)}, u32[]{:S(2)}, u32[]{:S(2)}) collective-permute-start(bf16[128,1536]{1,0:T(8,128)(2,1)} %get-tuple-element.213), channel_id=1, source_target_pairs={{0,2},{1,3},{2,0},{3,1},{4,6},{5,7},{6,4},{7,5},{8,10},{9,11},{10,... | collective-permute-start | bytes 1179656 | tf_op jit(solution)/shard_map/ppermute | solution.py:30
  117.6 30.2 %collective-permute-start.27 = (bf16[192,1152]{1,0:T(8,128)(2,1)}, bf16[192,1152]{1,0:T(8,128)(2,1)S(1)}, u32[]{:S(2)}, u32[]{:S(2)}) collective-permute-start(bf16[192,1152]{1,0:T(8,128)(2,1)} %get-tuple-element.220.refs_5_.refs_10_.refs_3_), channel_id=1, source_target_pairs={{0,12},{4,0},{8,4},{12,8},{1,13},{5,1},{9,5},{13,9},{2,14},{6,2},{... | collective-permute-start | bytes 1327112 | tf_op jit(solution)/shard_map/ppermute | solution.py:35
  122.1 34.8 %collective-permute-start.22 = (bf16[192,3072]{1,0:T(8,128)(2,1)}, bf16[192,3072]{1,0:T(8,128)(2,1)S(1)}, u32[]{:S(2)}, u32[]{:S(2)}) collective-permute-start(bf16[192,3072]{1,0:T(8,128)(2,1)} %collective-permute-done.18.refs_6_.refs_14_.refs_8_.refs_16_), channel_id=1, source_target_pairs={{0,12},{4,0},{8,4},{12,8},{1,13},{5,1},{9,5},{13,9},{2,14},{6,2},{... | collective-permute-start | bytes 3538952 | tf_op jit(solution)/shard_map/ppermute | solution.py:35
  156.9 34.8 %collective-permute-start.31 = (bf16[192,3072]{1,0:T(8,128)(2,1)S(1)}, bf16[192,3072]{1,0:T(8,128)(2,1)}, u32[]{:S(2)}, u32[]{:S(2)}) collective-permute-start(bf16[192,3072]{1,0:T(8,128)(2,1)S(1)} %copy-done.36), channel_id=1, source_target_pairs={{0,12},{4,0},{8,4},{12,8},{1,13},{5,1},{9,5},{13,9},{2,14},{6,2},{... | collective-permute-start | bytes 3538952 | tf_op jit(solution)/shard_map/ppermute | solution.py:35
  182.9 30.6 %collective-permute-start.36 = (bf16[192,1152]{1,0:T(8,128)(2,1)}, bf16[192,1152]{1,0:T(8,128)(2,1)}, u32[]{:S(2)}, u32[]{:S(2)}) collective-permute-start(bf16[192,1152]{1,0:T(8,128)(2,1)} %collective-permute-done.32.refs_6_.refs_7_.refs_12_.refs_5_), channel_id=1, source_target_pairs={{0,12},{4,0},{8,4},{12,8},{1,13},{5,1},{9,5},{13,9},{2,14},{6,2},{... | collective-permute-start | bytes 1327112 | tf_op jit(solution)/shard_map/ppermute | solution.py:35
  233.0 28.3 %collective-permute-start.45 = (bf16[192,3072]{1,0:T(8,128)(2,1)}, bf16[192,3072]{1,0:T(8,128)(2,1)}, u32[]{:S(2)}, u32[]{:S(2)}) collective-permute-start(bf16[192,3072]{1,0:T(8,128)(2,1)} %collective-permute-done.31.refs_5_.refs_13_.refs_7_.refs_15_), channel_id=1, source_target_pairs={{0,12},{4,0},{8,4},{12,8},{1,13},{5,1},{9,5},{13,9},{2,14},{6,2},{... | collective-permute-start | bytes 3538952 | tf_op jit(solution)/shard_map/ppermute | solution.py:35
  261.3 28.3 %collective-permute-start.49 = (bf16[192,3072]{1,0:T(8,128)(2,1)}, bf16[192,3072]{1,0:T(8,128)(2,1)S(1)}, u32[]{:S(2)}, u32[]{:S(2)}) collective-permute-start(bf16[192,3072]{1,0:T(8,128)(2,1)} %collective-permute-done.45.refs_6_.refs_14_.refs_8_.refs_16_), channel_id=1, source_target_pairs={{0,12},{4,0},{8,4},{12,8},{1,13},{5,1},{9,5},{13,9},{2,14},{6,2},{... | collective-permute-start | bytes 3538952 | tf_op jit(solution)/shard_map/ppermute | solution.py:35
  333.3 22.2 %collective-permute-start.61 = (bf16[192,2048]{1,0:T(8,128)(2,1)S(1)}, bf16[192,2048]{1,0:T(8,128)(2,1)S(1)}, u32[]{:S(2)}, u32[]{:S(2)}) collective-permute-start(bf16[192,2048]{1,0:T(8,128)(2,1)S(1)} %add_slots.24), channel_id=1, source_target_pairs={{0,4},{4,8},{8,12},{12,0},{1,5},{5,9},{9,13},{13,1},{2,6},{6,10},{... | collective-permute-start | bytes 2359304 | tf_op jit(solution)/shard_map/ppermute | solution.py:35
  334.9 21.2 %collective-permute-start.58 = (bf16[128,1536]{1,0:T(8,128)(2,1)S(1)}, bf16[128,1536]{1,0:T(8,128)(2,1)S(1)}, u32[]{:S(2)}, u32[]{:S(2)}) collective-permute-start(bf16[128,1536]{1,0:T(8,128)(2,1)S(1)} %get-tuple-element.250.refs_0_.refs_2_), channel_id=1, source_target_pairs={{0,2},{1,3},{2,0},{3,1},{4,6},{5,7},{6,4},{7,5},{8,10},{9,11},{10,... | collective-permute-start | bytes 1179656 | tf_op jit(solution)/shard_map/ppermute | solution.py:30
  346.6 27.5 %collective-permute-start.67 = (bf16[192,1024]{1,0:T(8,128)(2,1)S(1)}, bf16[192,1024]{1,0:T(8,128)(2,1)S(1)}, u32[]{:S(2)}, u32[]{:S(2)}) collective-permute-start(bf16[192,1024]{1,0:T(8,128)(2,1)S(1)} %add_slots.26), channel_id=1, source_target_pairs={{0,4},{4,8},{8,12},{12,0},{1,5},{5,9},{9,13},{13,1},{2,6},{6,10},{... | collective-permute-start | bytes 1179656 | tf_op jit(solution)/shard_map/ppermute | solution.py:35
  377.2 20.7 %collective-permute-start.72 = (bf16[192,1024]{1,0:T(8,128)(2,1)S(1)}, bf16[192,1024]{1,0:T(8,128)(2,1)S(1)}, u32[]{:S(2)}, u32[]{:S(2)}) collective-permute-start(bf16[192,1024]{1,0:T(8,128)(2,1)S(1)} %add_slots.27.refs_19_), channel_id=1, source_target_pairs={{0,4},{4,8},{8,12},{12,0},{1,5},{5,9},{9,13},{13,1},{2,6},{6,10},{... | collective-permute-start | bytes 1179656 | tf_op jit(solution)/shard_map/ppermute | solution.py:35
  377.5 27.7 %collective-permute-start.71 = (bf16[192,2048]{1,0:T(8,128)(2,1)S(1)}, bf16[192,2048]{1,0:T(8,128)(2,1)S(1)}, u32[]{:S(2)}, u32[]{:S(2)}) collective-permute-start(bf16[192,2048]{1,0:T(8,128)(2,1)S(1)} %add_slots.25.refs_20_), channel_id=1, source_target_pairs={{0,4},{4,8},{8,12},{12,0},{1,5},{5,9},{9,13},{13,1},{2,6},{6,10},{... | collective-permute-start | bytes 2359304 | tf_op jit(solution)/shard_map/ppermute | solution.py:35
  405.8 22.3 %collective-permute-start.76 = (bf16[192,2048]{1,0:T(8,128)(2,1)S(1)}, bf16[192,2048]{1,0:T(8,128)(2,1)S(1)}, u32[]{:S(2)}, u32[]{:S(2)}) collective-permute-start(bf16[192,2048]{1,0:T(8,128)(2,1)S(1)} %add_slots.28.refs_7_), channel_id=1, source_target_pairs={{0,4},{4,8},{8,12},{12,0},{1,5},{5,9},{9,13},{13,1},{2,6},{6,10},{... | collective-permute-start | bytes 2359304 | tf_op jit(solution)/shard_map/ppermute | solution.py:35
  411.8 25.9 %collective-permute-start.78 = (bf16[192,1152]{1,0:T(8,128)(2,1)S(1)}, bf16[192,1152]{1,0:T(8,128)(2,1)S(1)}, u32[]{:S(2)}, u32[]{:S(2)}) collective-permute-start(bf16[192,1152]{1,0:T(8,128)(2,1)S(1)} %add_slots.31), channel_id=1, source_target_pairs={{0,4},{4,8},{8,12},{12,0},{1,5},{5,9},{9,13},{13,1},{2,6},{6,10},{... | collective-permute-start | bytes 1327112 | tf_op jit(solution)/shard_map/ppermute | solution.py:35
  413.2 24.7 %collective-permute-start.74 = (bf16[128,1536]{1,0:T(8,128)(2,1)S(1)}, bf16[128,1536]{1,0:T(8,128)(2,1)S(1)}, u32[]{:S(2)}, u32[]{:S(2)}) collective-permute-start(bf16[128,1536]{1,0:T(8,128)(2,1)S(1)} %get-tuple-element.314.refs_0_.refs_6_), channel_id=1, source_target_pairs={{0,2},{1,3},{2,0},{3,1},{4,6},{5,7},{6,4},{7,5},{8,10},{9,11},{10,... | collective-permute-start | bytes 1179656 | tf_op jit(solution)/shard_map/ppermute | solution.py:30
  414.6 23.3 %collective-permute-start.73 = (bf16[128,1536]{1,0:T(8,128)(2,1)S(1)}, bf16[128,1536]{1,0:T(8,128)(2,1)S(1)}, u32[]{:S(2)}, u32[]{:S(2)}) collective-permute-start(bf16[128,1536]{1,0:T(8,128)(2,1)S(1)} %get-tuple-element.314.refs_0_.refs_6_), channel_id=1, source_target_pairs={{0,1},{1,0},{2,3},{3,2},{4,5},{5,4},{6,7},{7,6},{8,9},{9,8},{10,11... | collective-permute-start | bytes 1179656 | tf_op jit(solution)/shard_map/ppermute | solution.py:30
  423.2 35.3 %collective-permute-start.83 = (bf16[192,1024]{1,0:T(8,128)(2,1)S(1)}, bf16[192,1024]{1,0:T(8,128)(2,1)S(1)}, u32[]{:S(2)}, u32[]{:S(2)}) collective-permute-start(bf16[192,1024]{1,0:T(8,128)(2,1)S(1)} %add_slots.29.refs_8_), channel_id=1, source_target_pairs={{0,4},{4,8},{8,12},{12,0},{1,5},{5,9},{9,13},{13,1},{2,6},{6,10},{... | collective-permute-start | bytes 1179656 | tf_op jit(solution)/shard_map/ppermute | solution.py:35
  467.0 22.2 %collective-permute-start.88 = (bf16[192,2048]{1,0:T(8,128)(2,1)S(1)}, bf16[192,2048]{1,0:T(8,128)(2,1)S(1)}, u32[]{:S(2)}, u32[]{:S(2)}) collective-permute-start(bf16[192,2048]{1,0:T(8,128)(2,1)S(1)} %add_slots.35), channel_id=1, source_target_pairs={{0,4},{4,8},{8,12},{12,0},{1,5},{5,9},{9,13},{13,1},{2,6},{6,10},{... | collective-permute-start | bytes 2359304 | tf_op jit(solution)/shard_map/ppermute | solution.py:35
  468.6 21.4 %collective-permute-start.85 = (bf16[128,1536]{1,0:T(8,128)(2,1)S(1)}, bf16[128,1536]{1,0:T(8,128)(2,1)S(1)}, u32[]{:S(2)}, u32[]{:S(2)}) collective-permute-start(bf16[128,1536]{1,0:T(8,128)(2,1)S(1)} %get-tuple-element.301.refs_0_.refs_5_.refs_2_), channel_id=1, source_target_pairs={{0,2},{1,3},{2,0},{3,1},{4,6},{5,7},{6,4},{7,5},{8,10},{9,11},{10,... | collective-permute-start | bytes 1179656 | tf_op jit(solution)/shard_map/ppermute | solution.py:30
  469.2 20.8 %collective-permute-start.84 = (bf16[128,1536]{1,0:T(8,128)(2,1)S(1)}, bf16[128,1536]{1,0:T(8,128)(2,1)S(1)}, u32[]{:S(2)}, u32[]{:S(2)}) collective-permute-start(bf16[128,1536]{1,0:T(8,128)(2,1)S(1)} %get-tuple-element.301.refs_0_.refs_5_.refs_2_), channel_id=1, source_target_pairs={{0,1},{1,0},{2,3},{3,2},{4,5},{5,4},{6,7},{7,6},{8,9},{9,8},{10,11... | collective-permute-start | bytes 1179656 | tf_op jit(solution)/shard_map/ppermute | solution.py:30
  479.9 35.5 %collective-permute-start.95 = (bf16[192,1152]{1,0:T(8,128)(2,1)S(1)}, bf16[192,1152]{1,0:T(8,128)(2,1)S(1)}, u32[]{:S(2)}, u32[]{:S(2)}) collective-permute-start(bf16[192,1152]{1,0:T(8,128)(2,1)S(1)} %add_slots.33.refs_7_), channel_id=1, source_target_pairs={{0,4},{4,8},{8,12},{12,0},{1,5},{5,9},{9,13},{13,1},{2,6},{6,10},{... | collective-permute-start | bytes 1327112 | tf_op jit(solution)/shard_map/ppermute | solution.py:35
  480.2 26.9 %collective-permute-start.94 = (bf16[192,1024]{1,0:T(8,128)(2,1)S(1)}, bf16[192,1024]{1,0:T(8,128)(2,1)S(1)}, u32[]{:S(2)}, u32[]{:S(2)}) collective-permute-start(bf16[192,1024]{1,0:T(8,128)(2,1)S(1)} %add_slots.37), channel_id=1, source_target_pairs={{0,4},{4,8},{8,12},{12,0},{1,5},{5,9},{9,13},{13,1},{2,6},{6,10},{... | collective-permute-start | bytes 1179656 | tf_op jit(solution)/shard_map/ppermute | solution.py:35
  515.5 29.7 %collective-permute-start.101 = (bf16[192,2048]{1,0:T(8,128)(2,1)S(1)}, bf16[192,2048]{1,0:T(8,128)(2,1)S(1)}, u32[]{:S(2)}, u32[]{:S(2)}) collective-permute-start(bf16[192,2048]{1,0:T(8,128)(2,1)S(1)} %add_slots.36.refs_20_), channel_id=1, source_target_pairs={{0,4},{4,8},{8,12},{12,0},{1,5},{5,9},{9,13},{13,1},{2,6},{6,10},{... | collective-permute-start | bytes 2359304 | tf_op jit(solution)/shard_map/ppermute | solution.py:35
  552.7 22.3 %collective-permute-start.106 = (bf16[192,2048]{1,0:T(8,128)(2,1)S(1)}, bf16[192,2048]{1,0:T(8,128)(2,1)S(1)}, u32[]{:S(2)}, u32[]{:S(2)}) collective-permute-start(bf16[192,2048]{1,0:T(8,128)(2,1)S(1)} %add_slots.41.refs_7_), channel_id=1, source_target_pairs={{0,4},{4,8},{8,12},{12,0},{1,5},{5,9},{9,13},{13,1},{2,6},{6,10},{... | collective-permute-start | bytes 2359304 | tf_op jit(solution)/shard_map/ppermute | solution.py:35
  554.4 27.3 %collective-permute-start.98 = (bf16[192,1152]{1,0:T(8,128)(2,1)S(1)}, bf16[192,1152]{1,0:T(8,128)(2,1)S(1)}, u32[]{:S(2)}, u32[]{:S(2)}) collective-permute-start(bf16[192,1152]{1,0:T(8,128)(2,1)S(1)} %add_slots.40), channel_id=1, source_target_pairs={{0,4},{4,8},{8,12},{12,0},{1,5},{5,9},{9,13},{13,1},{2,6},{6,10},{... | collective-permute-start | bytes 1327112 | tf_op jit(solution)/shard_map/ppermute | solution.py:35
  557.1 24.8 %collective-permute-start.105 = (bf16[128,1536]{1,0:T(8,128)(2,1)S(1)}, bf16[128,1536]{1,0:T(8,128)(2,1)S(1)}, u32[]{:S(2)}, u32[]{:S(2)}) collective-permute-start(bf16[128,1536]{1,0:T(8,128)(2,1)S(1)} %get-tuple-element.351.refs_0_), channel_id=1, source_target_pairs={{0,2},{1,3},{2,0},{3,1},{4,6},{5,7},{6,4},{7,5},{8,10},{9,11},{10,... | collective-permute-start | bytes 1179656 | tf_op jit(solution)/shard_map/ppermute | solution.py:30
  557.8 24.1 %collective-permute-start.104 = (bf16[128,1536]{1,0:T(8,128)(2,1)S(1)}, bf16[128,1536]{1,0:T(8,128)(2,1)S(1)}, u32[]{:S(2)}, u32[]{:S(2)}) collective-permute-start(bf16[128,1536]{1,0:T(8,128)(2,1)S(1)} %get-tuple-element.351.refs_0_), channel_id=1, source_target_pairs={{0,1},{1,0},{2,3},{3,2},{4,5},{5,4},{6,7},{7,6},{8,9},{9,8},{10,11... | collective-permute-start | bytes 1179656 | tf_op jit(solution)/shard_map/ppermute | solution.py:30
  (266 other events, 2787.2 us)
